TPU v7x, 32 devices: a whole 2x2x4 slice. The times are simulated.
32 devices in a mesh: dp: 4 (over z), tr: 2 (over x), tc: 4 (over y, core).
Axes of the slice: x: 2, y: 2, z: 4, core: 2. Of those that a mesh axis runs over, the one named last changes fastest.
Arguments:
- tokens: bfloat16 [4096, 2048], P('dp', 'tc'), may hold values from -6 to 6
- cotangent: bfloat16 [4096, 2048], P('dp', 'tc'), may hold values from -6 to 6
- segment_ids: int32 [4096], P('dp'), may hold values from 0 to 4, as said below
- attn_gain: float32 [2048], P('tc'), may hold values from 0.1 to 1.9
- q_gain: float32 [128], replicated, may hold values from 0.1 to 1.9
- k_gain: float32 [128], replicated, may hold values from 0.1 to 1.9
- mlp_gain: float32 [2048], P('tc'), may hold values from 0.1 to 1.9
- w_query: bfloat16 [2048, 2048], P('tc', 'tr'), may hold values from -0.125 to 0.125
- w_key: bfloat16 [2048, 1024], P('tc', 'tr'), may hold values from -0.125 to 0.125
- w_value: bfloat16 [2048, 1024], P('tc', 'tr'), may hold values from -0.125 to 0.125
- w_out: bfloat16 [2048, 2048], P('tr', 'tc'), may hold values from -1.5 to 1.5
- w_gate: bfloat16 [2048, 6144], P('tc', 'tr'), may hold values from -0.125 to 0.125
- w_up: bfloat16 [2048, 6144], P('tc', 'tr'), may hold values from -0.125 to 0.125
- w_down: bfloat16 [6144, 2048], P('tr', 'tc'), may hold values from -0.078125 to 0.078125
Outputs:
- mixed: bfloat16 [4096, 2048], P('dp', 'tc')
- token_grad: bfloat16 [4096, 2048], P('dp', 'tc')
- attn_gain_grad: float32 [2048], P('tc')
- q_gain_grad: float32 [128], replicated
- k_gain_grad: float32 [128], replicated
- mlp_gain_grad: float32 [2048], P('tc')
- w_query_grad: float32 [2048, 2048], P('tc', 'tr')
- w_key_grad: float32 [2048, 1024], P('tc', 'tr')
- w_value_grad: float32 [2048, 1024], P('tc', 'tr')
- w_out_grad: float32 [2048, 2048], P('tr', 'tc')
- w_gate_grad: float32 [2048, 6144], P('tc', 'tr')
- w_up_grad: float32 [2048, 6144], P('tc', 'tr')
- w_down_grad: float32 [6144, 2048], P('tr', 'tc')
Inputs may be any that keep to these rules, and one draw needn't show every extreme that they name: `segment_ids`: within each aligned block of 1024 rows the ids start at 0, never fall and rise by one at each new sequence; some block holds a single sequence of 1024 tokens and some block holds five sequences.
All inputs are finite; a program needn't handle non-finite values.
Results may differ from a plain program's by a relative error of at most 0.017.
Values may be sent and summed in bfloat16 or wider, within the bound.
No kernel may reach another device: no remote copies, remote signals or barrier semaphores. Data moves between devices by JAX's collectives and lax.ppermute only.
A program may use at most 192 MiB of HBM per device.

v0:
```python
import jax
import jax.numpy as jnp
from jax import lax
from jax.experimental import pallas as pl
from jax.experimental.pallas import tpu as pltpu
from jax.sharding import PartitionSpec as P

norm_eps = 1e-06
rope_base = 1000000.0
neg_big = -1e30
f32 = jnp.float32
bf16 = jnp.bfloat16


def dot(left_side, right_side):
    return jnp.dot(left_side, right_side, preferred_element_type=f32)


def contract_rows(left_side, right_side):
    return lax.dot_general(
        left_side, right_side, (((0,), (0,)), ((), ())), preferred_element_type=f32
    )


def contract_cols(left_side, right_side):
    return lax.dot_general(
        left_side, right_side, (((1,), (1,)), ((), ())), preferred_element_type=f32
    )


def swap_core(block):
    return lax.ppermute(block, "tc", [(i, i ^ 1) for i in range(4)])


def swap_y(block):
    return lax.ppermute(block, "tc", [(i, i ^ 2) for i in range(4)])


def swap_diag(block):
    return lax.ppermute(block, "tc", [(i, i ^ 3) for i in range(4)])


def swap_x(block):
    return lax.ppermute(block, "tr", [(0, 1), (1, 0)])


def width_total(rows):
    rows = rows + swap_core(rows)
    return rows + swap_y(rows)


class LineSums:
    def __init__(self, lag=4):
        self.lag = lag
        self.last = ()
        self.short = lax.axis_size("dp") == 4
        place = lax.axis_index("dp")
        self.middle = (place == 1) | (place == 2)
        self.queue, self.names, self.pieces = [], [], []
        self.outer, self.total = [], []

    def add(self, name, grad, axis):
        size = min(grad.shape)
        for k in range(0, grad.shape[axis], size):
            self.queue.append((name, lax.slice_in_dim(grad, k, k + size, axis=axis)))

    def waiting(self):
        return [piece for _, piece in self.queue]

    def _consume(self, which, marker):
        got, piece = after((self.outer[which], self.pieces[which]), marker)
        inward = low(piece.astype(f32) + got.astype(f32))
        across = lax.ppermute(inward, "dp", [(1, 2), (2, 1)])
        self.total.append(low(inward.astype(f32) + across.astype(f32)))
        return inward

    def _swap_outer(self, piece):
        self.outer.append(lax.ppermute(piece, "dp", [(0, 1), (1, 0), (2, 3), (3, 2)]))

    def send(self, marker=(), strict=True):
        which = len(self.pieces)
        name, piece = self.queue.pop(0)
        self.names.append(name)
        self.pieces.append(piece)
        if not self.short:
            return piece
        if which >= 2:
            marker = self._consume(which - 2, marker)
        out = after(piece, marker)
        if which >= self.lag:
            out = jnp.where(self.middle, self.total[which - self.lag], out)
        self._swap_outer(out)
        return (marker, out) if strict else marker

    def finish(self):
        count = len(self.pieces)
        if self.short:
            self.last = self._consume(count - 2, ())
            self._consume(count - 1, ())
            for which in range(count - self.lag, count):
                self._swap_outer(self.total[which])
            sums = [(self.total[k], self.outer[k + self.lag]) for k in range(count)]
        else:
            sums = [(lax.psum(piece, "dp"),) for piece in self.pieces]
        return lambda name: [s for n, s in zip(self.names, sums) if n == name]


def after(value, *others):
    return lax.optimization_barrier((value, others))[0]


def low(array):
    return array.astype(bf16)


def scatter_width(product, near=lambda ready: ready):
    from_far = swap_core(low(product(3)))
    from_core = swap_core(low(product(1)))
    from_far = after(from_far, near(from_far))
    for_y = low(product(2) + from_far.astype(f32))
    from_y = swap_y(for_y)
    return (product(0) + from_core.astype(f32), from_y, for_y)


def scatter_all(product, started, turned):
    far_y, far_own = swap_core(low(product(3))), swap_core(low(product(1)))
    for_y = low(product(2) + far_y.astype(f32))
    own = low(product(0) + far_own.astype(f32))
    half = own.shape[0] // 2
    quarter = half // 2
    width = own.shape[1]
    y_first = swap_y(jnp.concatenate([for_y[quarter:half], for_y[half + quarter :]], axis=0))
    x_first = swap_x(
        jnp.concatenate([own[half : half + quarter], for_y[half : half + quarter]], axis=1)
    )
    x_first, y_first = after((x_first, y_first), started((own, for_y)))
    top_in = low(for_y[:quarter].astype(f32) + x_first[:, width:].astype(f32))
    low_in = low(own[half + quarter :].astype(f32) + y_first[quarter:].astype(f32))
    top_y, low_x = after((swap_y(top_in), swap_x(low_in)), turned((top_in, low_in)))
    top = own[:quarter].astype(f32) + x_first[:, :width].astype(f32) + top_y.astype(f32)
    bottom = own[quarter:half].astype(f32) + y_first[:quarter].astype(f32) + low_x.astype(f32)
    return jnp.concatenate([top, bottom], axis=0)


def positions_of(segment):
    slot_ids = jnp.arange(5, dtype=jnp.int32)
    before = jnp.sum((segment[None, :] < slot_ids[:, None]).astype(jnp.int32), axis=1)
    starts = jnp.sum(jnp.where(segment[:, None] == slot_ids[None, :], before[None, :], 0), axis=1)
    return jnp.arange(segment.shape[0], dtype=jnp.int32) - starts


def rope_tables(positions, head_size):
    half_size = head_size // 2
    frequency = rope_base ** (-jnp.arange(half_size, dtype=f32) * 2.0 / head_size)
    angles = positions.astype(f32)[:, None] * frequency[None, :]
    cosine, sine = jnp.cos(angles), jnp.sin(angles)
    return (
        jnp.concatenate([cosine, cosine], axis=1),
        jnp.concatenate([-sine, sine], axis=1),
    )


def turn(vectors):
    return pltpu.roll(vectors, vectors.shape[-1] // 2, axis=1)


def inverse_norm(vectors):
    return lax.rsqrt(jnp.mean(vectors * vectors, axis=-1, keepdims=True) + norm_eps)


def allowed_keys(seg_col, seg_row, start, size, extent):
    row = lax.broadcasted_iota(jnp.int32, (size, extent), 0) + start
    col = lax.broadcasted_iota(jnp.int32, (size, extent), 1)
    return (seg_col[start : start + size, :] == seg_row[:, :extent]) & (col <= row)


def attend_kernel(
    side, own, from_y, rstd, cos, sin, seg_col, seg_row, q_gain, k_gain,
    proj, q_out, k_out, v_out, lse, att,
):
    rows = own.shape[0]
    size = cos.shape[1]
    heads = q_out.shape[1] // size
    block = rows // 4
    scale = size**-0.5
    k_at = heads * size
    v_at = k_at + size

    def ready(i, carry):
        at = pl.ds(pl.multiple_of(i * block, block), block)
        raw = (own[at, :] + from_y[at, :].astype(f32)) * rstd[at, :]
        proj[at, :] = raw

        def rope(part, gain):
            n = part * inverse_norm(part) * gain[...]
            return (n * cos[at, :] + turn(n) * sin[at, :]).astype(bf16)

        for h in range(heads):
            q_out[at, h * size : (h + 1) * size] = rope(raw[:, h * size : (h + 1) * size], q_gain)
        k_out[at, :] = rope(raw[:, k_at:v_at], k_gain)
        v_out[at, :] = raw[:, v_at:].astype(bf16)
        return carry

    lax.fori_loop(0, 4, ready, 0)
    for i in range(4):
        start = i * block
        extent = start + block
        allowed = allowed_keys(seg_col, seg_row, start, block, extent)
        to = pl.ds(pl.multiple_of(lax.rem(start + side[0] * (rows // 2), rows), block), block)
        for h in range(heads):
            of_head = slice(h * size, (h + 1) * size)
            scores = contract_cols(q_out[start:extent, of_head], k_out[:extent, :]) * scale
            scores = jnp.where(allowed, scores, neg_big)
            top = jnp.max(scores, axis=-1, keepdims=True)
            expd = jnp.exp(scores - top)
            total = jnp.sum(expd, axis=-1, keepdims=True)
            weights = (expd * (1.0 / total)).astype(bf16)
            att[to, of_head] = dot(weights, v_out[:extent, :]).astype(bf16)
            lse[start:extent, h : h + 1] = top + jnp.log(total)


def attend_back_kernel(
    side, own, from_y, proj, q_in, k_in, v_in, lse, cos, sin, seg_col, seg_row, q_gain, k_gain,
    grads, q_gain_part, k_gain_part, inner, k_acc, v_acc,
):
    rows = own.shape[0]
    size = cos.shape[1]
    heads = q_in.shape[1] // size
    block = rows // 4
    scale = size**-0.5
    k_at = heads * size
    v_at = k_at + size

    def unrope(grad, part, gain, start):
        rows_at = slice(start, start + block)
        m = grad * cos[rows_at, :] - turn(grad) * sin[rows_at, :]
        r = inverse_norm(part)
        hat = part * r
        mg = m * gain[...]
        back = (r * (mg - hat * jnp.mean(mg * hat, axis=-1, keepdims=True))).astype(bf16)
        gain_part = jnp.sum(m * hat, axis=0, keepdims=True)
        return (back, gain_part, jnp.sum(back.astype(f32) * part, axis=-1, keepdims=True))

    k_acc[...] = jnp.zeros_like(k_acc)
    v_acc[...] = jnp.zeros_like(v_acc)
    q_total = jnp.zeros(q_gain_part.shape, f32)
    for i in range(4):
        start = i * block
        extent = start + block
        allowed = allowed_keys(seg_col, seg_row, start, block, extent)
        at = pl.ds(pl.multiple_of(lax.rem(start + side[0] * (rows // 2), rows), block), block)
        inner_sum = jnp.zeros((block, 1), f32)
        for h in range(heads):
            of_head = slice(h * size, (h + 1) * size)
            query = q_in[start:extent, of_head]
            grad = (own[at, of_head] + from_y[at, of_head].astype(f32)).astype(bf16)
            scores = contract_cols(query, k_in[:extent, :]) * scale
            scores = jnp.where(allowed, scores, neg_big)
            probs = jnp.exp(scores - lse[start:extent, h : h + 1])
            prob_grad = contract_cols(grad, v_in[:extent, :])
            delta = jnp.sum(probs * prob_grad, axis=-1, keepdims=True)
            score_grad = (probs * (prob_grad - delta)).astype(bf16)
            query_grad = dot(score_grad, k_in[:extent, :]) * scale
            k_acc[:extent, :] += contract_rows(score_grad, query) * scale
            v_acc[:extent, :] += contract_rows(probs.astype(bf16), grad)
            back, gain_part, part_inner = unrope(
                query_grad, proj[start:extent, of_head], q_gain, start
            )
            grads[start:extent, of_head] = back
            q_total = q_total + gain_part
            inner_sum = inner_sum + part_inner
        inner[start:extent, :] = inner_sum
    q_gain_part[...] = q_total
    k_total = jnp.zeros(k_gain_part.shape, f32)
    for i in range(4):
        start = i * block
        extent = start + block
        back, gain_part, part_inner = unrope(
            k_acc[start:extent, :], proj[start:extent, k_at:v_at], k_gain, start
        )
        grads[start:extent, k_at:v_at] = back
        k_total = k_total + gain_part
        v_back = v_acc[start:extent, :].astype(bf16)
        grads[start:extent, v_at:] = v_back
        inner[start:extent, :] += part_inner + jnp.sum(
            v_back.astype(f32) * proj[start:extent, v_at:], axis=-1, keepdims=True
        )
    k_gain_part[...] = k_total


vmem = pl.BlockSpec(memory_space=pltpu.VMEM)
smem = pl.BlockSpec(memory_space=pltpu.SMEM)
def whole_kernel(body, outs, scratch=(), grant=50):
    def call(*operands):
        return pl.pallas_call(
            body,
            out_shape=outs,
            in_specs=[smem if o.ndim == 1 else vmem for o in operands],
            out_specs=[vmem] * len(outs),
            scratch_shapes=scratch,
            compiler_params=pltpu.CompilerParams(vmem_limit_bytes=grant * 2**20),
            cost_estimate=pl.CostEstimate(flops=0, bytes_accessed=2**10, transcendentals=0),
        )(*operands)

    return call


def units_kernel(*refs):
    ins, weights, cots, downs = refs[:4], refs[4:8], refs[8:12], refs[12:16]
    rstd_ref = refs[16]
    hidden, pair, scaled, inner = refs[-4:]
    units = hidden.shape[1]
    chunk = min(256, units)
    rstd = rstd_ref[...]

    def product(at):
        total = dot(ins[0][...], weights[0][:, at])
        for k in range(1, 4):
            total = total + dot(ins[k][...], weights[k][:, at])
        return total * rstd

    inner_sum = jnp.zeros(inner.shape, f32)
    for start in range(0, units, chunk):
        of_gate = slice(start, start + chunk)
        of_up = slice(units + start, units + start + chunk)
        gate, up = product(of_gate), product(of_up)
        grad = contract_cols(cots[0][...], downs[0][of_gate, :])
        for k in range(1, 4):
            grad = grad + contract_cols(cots[k][...], downs[k][of_gate, :])
        sig = jax.nn.sigmoid(gate)
        silu = gate * sig
        hidden[:, of_gate] = low(silu * up)
        gate_grad = low(grad * up * sig * (1.0 + gate * (1.0 - sig)))
        up_grad = low(grad * silu)
        pair[:, of_gate] = gate_grad
        pair[:, of_up] = up_grad
        gate_grad, up_grad = gate_grad.astype(f32), up_grad.astype(f32)
        scaled[:, of_gate] = low(gate_grad * rstd)
        scaled[:, of_up] = low(up_grad * rstd)
        inner_sum = inner_sum + jnp.sum(gate_grad * gate + up_grad * up, axis=-1, keepdims=True)
    inner[...] = inner_sum


def units_of_half(ins, weights, cots, downs, rstd, which, earlier):
    half, depth = ins[0].shape
    units = downs[0].shape[0]
    block = half // 2
    first = which * (half // block)
    outs = [
        jax.ShapeDtypeStruct((2 * half, units), bf16),
        jax.ShapeDtypeStruct((2 * half, 2 * units), bf16),
        jax.ShapeDtypeStruct((2 * half, 2 * units), bf16),
        jax.ShapeDtypeStruct((2 * half, 1), f32),
    ]

    def whole(array):
        return pl.BlockSpec(array.shape, lambda i: (0, 0))

    def of_two(array, k):
        return pl.BlockSpec((None, *array.shape[1:]), lambda i: (k, 0, 0))

    near_by, core, both = downs
    downs = [near_by, core, both, both]
    down_specs = [whole(near_by), whole(core), of_two(both, 0), of_two(both, 1)]
    here = pl.BlockSpec((block, depth), lambda i: (i, 0))
    at = lambda i: (first + i, 0)
    of_all = pl.BlockSpec((block, depth), at)
    earlier = list(earlier or [])
    return pl.pallas_call(
        units_kernel,
        grid=(half // block,),
        out_shape=outs,
        in_specs=[here] * 4
        + [whole(w) for w in weights]
        + [of_all, of_all, here, here]
        + down_specs
        + [pl.BlockSpec((block, 1), at)]
        + [pl.BlockSpec(memory_space=pl.ANY)] * len(earlier),
        out_specs=[pl.BlockSpec((block, o.shape[1]), at) for o in outs],
        input_output_aliases={17 + k: k for k in range(len(earlier))},
        compiler_params=pltpu.CompilerParams(vmem_limit_bytes=50 * 2**20),
        cost_estimate=pl.CostEstimate(flops=0, bytes_accessed=2**10, transcendentals=0),
    )(*ins, *weights, *cots, *downs, rstd, *earlier)


def place_sums(scalars, pieces, outs, plan):
    flat = [a for piece in pieces for a in piece]

    def kernel(words, *refs):
        ins, results = list(refs[: len(flat)]), refs[len(flat) :]
        groups = [[ins.pop(0) for _ in piece] for piece in pieces]
        for k in range(4):

            @pl.when(pl.program_id(0) == k)
            def _(k=k):
                for piece, at, out, to in plan[k]:
                    value = groups[piece][0][at]
                    if len(groups[piece]) == 2:
                        value = jnp.where(words[4] == 1, value, groups[piece][1][at])
                    results[out][to] = value.astype(f32)

    def quarter(shape, axis):
        block = tuple(n // 4 if i == axis else n for i, n in enumerate(shape))
        if axis == 0:
            return pl.BlockSpec(block, lambda k, words: (words[k], 0))
        return pl.BlockSpec(block, lambda k, words: (0, words[k]))

    return pl.pallas_call(
        kernel,
        grid_spec=pltpu.PrefetchScalarGridSpec(
            num_scalar_prefetch=1,
            grid=(4,),
            in_specs=[pl.BlockSpec(a.shape, lambda k, words: (0, 0)) for a in flat],
            out_specs=[quarter(*out) for out in outs],
        ),
        out_shape=[jax.ShapeDtypeStruct(shape, f32) for shape, _ in outs],
        compiler_params=pltpu.CompilerParams(vmem_limit_bytes=50 * 2**20),
        cost_estimate=pl.CostEstimate(flops=0, bytes_accessed=2**10, transcendentals=0),
    )(scalars, *flat)


def on_device(
    tokens,
    cotangent,
    segment_ids,
    attn_gain,
    q_gain,
    k_gain,
    mlp_gain,
    w_query,
    w_key,
    w_value,
    w_out,
    w_gate,
    w_up,
    w_down,
):
    assert lax.axis_size("tc") == 4 and lax.axis_size("tr") == 2
    col = lax.axis_index("tc")
    side = lax.axis_index("tr")
    rows, width = tokens.shape
    half = rows // 2
    full_width = width * 4
    head_size = q_gain.shape[0]
    q_width = w_query.shape[1] // 4
    k_width = w_key.shape[1] // 4
    units = w_gate.shape[1] // 4
    around = [col, col ^ 1, col ^ 2, col ^ 3]

    def cols_of(array, which, size):
        return lax.dynamic_slice_in_dim(array, around[which] * size, size, 1)

    def rows_of(array, which, size):
        return lax.dynamic_slice_in_dim(array, around[which] * size, size, 0)

    def flip(array):
        return jnp.concatenate(
            [
                lax.dynamic_slice_in_dim(array, side * half, half, 0),
                lax.dynamic_slice_in_dim(array, (1 - side) * half, half, 0),
            ],
            axis=0,
        )

    shares = lax.axis_size("dp")
    place = lax.axis_index("dp")

    def share_of(block):
        size = block.shape[0] // shares
        return lax.dynamic_slice_in_dim(block, place * size, size, 0)

    def gather_shares(from_y, from_diag):
        return lax.all_gather(jnp.stack([from_y, from_diag]), "dp", axis=1, tiled=True)

    def ffn_columns(which, rows_at):
        return jnp.concatenate(
            [rows_at(cols_of(w, which, units)) for w in (w_gate, w_up)], axis=1
        )

    down_y, down_diag = (share_of(rows_of(w_down, k, units)) for k in (2, 3))
    share_y, share_diag = ffn_columns(2, share_of), ffn_columns(3, share_of)

    qkv_weights = [
        jnp.concatenate(
            [cols_of(w_query, k, q_width), cols_of(w_key, k, k_width), cols_of(w_value, k, k_width)],
            axis=1,
        )
        for k in range(4)
    ]
    inputs = tokens.astype(f32)
    down_y, down_diag = swap_y(down_y), swap_diag(down_diag)
    share_y, share_diag, inputs = after((share_y, share_diag, inputs), down_y, down_diag)
    scaled_in = low(inputs * attn_gain[None, :])
    raw_own, raw_y, for_y = scatter_width(lambda k: dot(scaled_in, qkv_weights[k]))
    down_gathered = gather_shares(down_y, down_diag)
    w_gate, w_up, w_down, w_out, segment_ids, cotangent, inputs = after(
        (w_gate, w_up, w_down, w_out, segment_ids, cotangent, inputs), for_y
    )
    square_sum = width_total(jnp.sum(inputs * inputs, axis=1))
    cos_table, sin_table = rope_tables(positions_of(segment_ids), head_size)
    side_word = side.astype(jnp.int32).reshape(1)
    tables = (
        cos_table,
        sin_table,
        segment_ids.reshape(rows, 1),
        segment_ids.reshape(1, rows),
        q_gain.reshape(1, head_size),
        k_gain.reshape(1, head_size),
    )
    whole = lambda block: block
    blocks_core = (ffn_columns(1, whole), rows_of(w_down, 1, units))
    raw_y, share_y, share_diag, square_sum = after(
        (raw_y, swap_y(share_y), swap_diag(share_diag), square_sum), raw_own, tables, blocks_core
    )
    ffn_y, ffn_diag = (lax.all_gather(w, "dp", axis=0, tiled=True) for w in (share_y, share_diag))
    attn_rstd = lax.rsqrt(square_sum / full_width + norm_eps)
    attn_hat = inputs * attn_rstd[:, None]
    normed = low(attn_hat * attn_gain[None, :])

    heads = q_width // head_size
    projected, q_low, k_low, v_low, log_totals, att_rel = whole_kernel(
        attend_kernel,
        [
            jax.ShapeDtypeStruct((rows, q_width + 2 * k_width), f32),
            jax.ShapeDtypeStruct((rows, q_width), bf16),
            jax.ShapeDtypeStruct((rows, k_width), bf16),
            jax.ShapeDtypeStruct((rows, k_width), bf16),
            jax.ShapeDtypeStruct((rows, heads), f32),
            jax.ShapeDtypeStruct((rows, q_width), bf16),
        ],
    )(side_word, raw_own, raw_y, attn_rstd.reshape(rows, 1), *tables)
    cot_rel = flip(cotangent)
    cot_y = swap_y(after(cot_rel[:half], raw_y))
    att_y, cot_x, down_gathered = after((swap_y(att_rel), swap_x(cot_y), down_gathered), att_rel)
    atts = [att_rel, swap_core(att_rel), att_y, swap_core(att_y)]
    outs = [rows_of(w_out, k, q_width) for k in range(4)]

    def out_rows(at):
        return (dot(atts[0][at], outs[0]) + dot(atts[1][at], outs[1])) + (
            dot(atts[2][at], outs[2]) + dot(atts[3][at], outs[3])
        )

    from_x = swap_x(low(out_rows(slice(half, rows))))
    home = out_rows(slice(0, half))

    prefetched = (
        swap_core(cot_rel),
        *map(swap_core, blocks_core),
    )
    from_x, (cot_core, ffn_core, down_core), ffn_y = after((from_x, prefetched, ffn_y), home)
    cot_y_core, cot_x_core = swap_core(cot_y), swap_core(cot_x)
    downs = (rows_of(w_down, 0, units), down_core, down_gathered)
    tokens_half = lax.dynamic_slice_in_dim(tokens, side * half, half, 0).astype(f32)
    residual = tokens_half + home + from_x.astype(f32)

    mlp_square = jnp.sum(residual * residual, axis=1)
    mlp_square = width_total(jnp.concatenate([mlp_square, swap_x(mlp_square)]))
    mlp_own = low(residual * mlp_gain[None, :])
    mlp_rstd = lax.rsqrt(mlp_square / full_width + norm_eps)
    quarter = half // 2
    mlp_x, mlp_y, mlp_rstd = after(
        (swap_x(mlp_own), swap_y(mlp_own), mlp_rstd), cot_y_core, cot_x_core
    )
    mlp_xy = (swap_y(mlp_x[:quarter]), swap_x(mlp_y[quarter:]))
    mlp_x_core = swap_core(mlp_x)
    ffns = [ffn_columns(0, whole), ffn_core, ffn_y, ffn_diag]
    downs = [rows_of(w_down, 0, units), down_core, down_gathered]
    ins_own = [mlp_own, swap_core(mlp_own), mlp_y, swap_core(mlp_y)]
    cots_own = [cot_rel, cot_core, cot_y, cot_y_core]
    cots_other = [cot_rel, cot_core, cot_x, cot_x_core]
    rstd_rel = mlp_rstd.reshape(rows, 1)
    first = units_of_half(ins_own, ffns, cots_own, downs, rstd_rel, 0, None)
    mlp_xy, mlp_x_core = after((mlp_xy, mlp_x_core), first)
    mlp_xy = jnp.concatenate(mlp_xy, axis=0)
    ins_other = [mlp_x, mlp_x_core, mlp_xy, swap_core(mlp_xy)]
    hidden, pair, pair_scaled, inner = units_of_half(
        ins_other, ffns, cots_other, downs, rstd_rel, 1, first
    )

    line = LineSums()
    mlp_in, mlp_core = (jnp.concatenate([ins_own[k], ins_other[k]], axis=0) for k in (0, 1))
    line.add("ffn", low(contract_rows(mlp_in, pair_scaled)), 1)
    line.send(line.send())
    pair = after(pair, line.pieces, line.waiting())

    kept = {}

    def started(marker):
        sums = width_total(after(inner[:, 0], marker))
        kept["inner"] = sums
        block = low(contract_rows(mlp_core, after(pair_scaled, marker)))
        kept["core"] = swap_core(block)
        down_core = low(contract_rows(after(hidden, block), cot_core))
        down_own = low(contract_rows(after(hidden, block), cot_rel))
        line.add("down", jnp.concatenate([down_own, swap_core(down_core)], axis=0), 0)
        return (line.send(down_own), sums)

    def turned(marker):
        sums = after(kept["inner"], marker)
        kept["inner"] = sums[:half] + swap_x(sums[half:])
        return (kept["inner"], line.send(marker))

    mlp_in_grad = scatter_all(lambda k: contract_cols(pair, ffns[k]), started, turned)
    inner_total = kept["inner"]
    mlp_hat = residual * mlp_rstd[:half, None]
    mlp_gain_part = jnp.sum(mlp_in_grad * mlp_hat, axis=0)
    residual_grad = cot_rel[:half].astype(f32) + mlp_rstd[:half, None] * (
        mlp_in_grad * mlp_gain[None, :] - mlp_hat * (inner_total / full_width)[:, None]
    )
    residual_low = low(residual_grad)
    res_x = after(swap_x(residual_low), line.send(residual_low))
    res_rel = jnp.concatenate([residual_low, res_x], axis=0)
    head_own, head_y, head_sent = scatter_width(
        lambda k: contract_cols(res_rel, outs[k]), line.send
    )

    line.add("ffn", kept["core"], 1)
    marker = line.send(head_sent)
    out_grads = [low(contract_rows(after(part, marker), res_rel)) for part in atts]
    line.add("out", jnp.concatenate(out_grads, axis=0), 0)
    head_own, head_y = after((head_own, head_y), line.waiting())

    proj_low, q_gain_part, k_gain_part, inner_attn = whole_kernel(
        attend_back_kernel,
        [
            jax.ShapeDtypeStruct((rows, q_width + 2 * k_width), bf16),
            jax.ShapeDtypeStruct((1, head_size), f32),
            jax.ShapeDtypeStruct((1, head_size), f32),
            jax.ShapeDtypeStruct((rows, 1), f32),
        ],
        scratch=[pltpu.VMEM((rows, k_width), f32), pltpu.VMEM((rows, k_width), f32)],
    )(side_word, head_own, head_y, projected, q_low, k_low, v_low, log_totals, *tables)
    proj_y, proj_core = swap_y(proj_low), swap_core(proj_low)

    marker = proj_low
    for _ in range(4):
        marker = line.send(marker)
    proj_y, proj_core = after((proj_y, proj_core), marker)
    pairs = lax.all_gather(after(pair_scaled, proj_y), "tc")
    projs = [proj_low, proj_core, proj_y, swap_core(proj_y)]
    normed_part = low(
        (contract_cols(projs[0], qkv_weights[0]) + contract_cols(projs[1], qkv_weights[1]))
        + (contract_cols(projs[2], qkv_weights[2]) + contract_cols(projs[3], qkv_weights[3]))
    )
    small = jnp.concatenate([inner_attn[:, 0], q_gain_part[0], k_gain_part[0]])
    small = width_total(after(small, normed_part))
    small = jnp.concatenate([small, mlp_gain_part])
    for part in projs:
        line.add("qkv", low(contract_rows(after(normed, normed_part), part)), 1)
    normed_x, small_x = after(
        (swap_x(normed_part), swap_x(small)), line.send((small, line.waiting()))
    )
    small = small + small_x
    inner_attn, gains = small[:rows], small[rows:]
    hiddens = lax.all_gather(after(hidden, inner_attn), "tc", axis=1, tiled=True)
    spare = jnp.pad(low(gains), (0, width * width - gains.shape[0])).reshape(width, width)
    normed_grad = normed_part.astype(f32) + normed_x.astype(f32)
    token_grad = low(
        flip(res_rel).astype(f32)
        + attn_rstd[:, None]
        * (normed_grad * attn_gain[None, :] - attn_hat * (inner_attn / full_width)[:, None])
    )

    marker = line.send((token_grad, line.waiting()), False)
    for _ in range(2):
        marker = line.send(marker, False)
    pairs = after(pairs, marker)
    for k in (2, 3):
        block = lax.dynamic_index_in_dim(pairs, around[k], 0, keepdims=False)
        line.add("ffn", low(contract_rows(mlp_in, block)), 1)
    marker = (marker, line.waiting())
    for _ in range(5):
        marker = line.send(marker, False)

    hiddens = after(hiddens, marker)
    far_down = [low(contract_rows(cols_of(hiddens, k, units), cot_rel)) for k in (2, 3)]
    line.add("down", jnp.concatenate(far_down, axis=0), 0)
    line.add("gains", spare, 0)
    mlp_away = low(dot(hiddens[half:], w_down))
    mlp_x_out = after(swap_x(mlp_away), line.send((mlp_away, line.waiting()), False))
    mixed_half = low(residual + dot(hiddens[:half], w_down) + mlp_x_out.astype(f32))
    mixed_x = after(swap_x(mixed_half), line.send(mixed_half, False))
    mixed = flip(jnp.concatenate([mixed_half, mixed_x], axis=0))
    marker = mixed_x
    while line.queue:
        marker = line.send(marker, False)
    sums_of = line.finish()

    words = jnp.stack([*around, line.middle.astype(jnp.int32)]).astype(jnp.int32)
    everything = slice(None)

    def spread(start, size, extent):
        while size:
            piece, at = divmod(start, extent)
            taken = min(size, extent - at)
            yield (piece, slice(at, at + taken), taken)
            start, size = start + taken, size - taken

    def runs(first, start, size, extent, out, axis, to=0):
        plan = []
        for piece, at, taken in spread(start, size, extent):
            block = slice(to, to + taken)
            pair_of = lambda part: (part, everything) if axis == 0 else (everything, part)
            plan.append((first + piece, pair_of(at), out, pair_of(block)))
            to += taken
        return plan

    out_sums, qkv_sums, ffn_sums = after(
        (sums_of("out"), sums_of("qkv"), sums_of("ffn")), line.last
    )
    ffn_plan = [
        runs(0, 2 * k * units, units, width, 0, 1) + runs(0, (2 * k + 1) * units, units, width, 1, 1)
        for k in range(4)
    ]
    w_gate_grad, w_up_grad = place_sums(words, ffn_sums, [(w_gate.shape, 1), (w_up.shape, 1)], ffn_plan)
    [w_down_grad] = place_sums(
        words,
        sums_of("down"),
        [(w_down.shape, 0)],
        [runs(0, k * units, units, width, 0, 0) for k in range(4)],
    )
    [w_out_grad] = place_sums(
        words,
        out_sums,
        [(w_out.shape, 0)],
        [runs(0, k * q_width, q_width, width, 0, 0) for k in range(4)],
    )
    block_width = q_width + 2 * k_width
    qkv_plan = [
        runs(0, k * block_width, q_width, width, 0, 1)
        + runs(0, k * block_width + q_width, k_width, width, 1, 1)
        + runs(0, k * block_width + q_width + k_width, k_width, width, 2, 1)
        for k in range(4)
    ]
    w_query_grad, w_key_grad, w_value_grad = place_sums(
        words, qkv_sums, [(w_query.shape, 1), (w_key.shape, 1), (w_value.shape, 1)], qkv_plan
    )
    attn_gain_part = sum(
        jnp.sum(w.astype(f32) * g, axis=1)
        for w, g in ((w_query, w_query_grad), (w_key, w_key_grad), (w_value, w_value_grad))
    )
    attn_gain_grad = (attn_gain_part + swap_x(attn_gain_part)) / attn_gain
    [gain_sums] = sums_of("gains")
    gains = jnp.where(line.middle, gain_sums[0], gain_sums[-1]).reshape(-1).astype(f32)
    q_gain_grad = gains[:head_size]
    k_gain_grad = gains[head_size : 2 * head_size]
    mlp_gain_grad = gains[2 * head_size : 2 * head_size + width]
    return (
        mixed,
        token_grad,
        attn_gain_grad,
        q_gain_grad,
        k_gain_grad,
        mlp_gain_grad,
        w_query_grad,
        w_key_grad,
        w_value_grad,
        w_out_grad,
        w_gate_grad,
        w_up_grad,
        w_down_grad,
    )


def solution(mesh):
    in_specs = (
        P("dp", "tc"),
        P("dp", "tc"),
        P("dp"),
        P("tc"),
        P(),
        P(),
        P("tc"),
        P("tc", "tr"),
        P("tc", "tr"),
        P("tc", "tr"),
        P("tr", "tc"),
        P("tc", "tr"),
        P("tc", "tr"),
        P("tr", "tc"),
    )
    out_specs = (
        P("dp", "tc"),
        P("dp", "tc"),
        P("tc"),
        P(),
        P(),
        P("tc"),
        P("tc", "tr"),
        P("tc", "tr"),
        P("tc", "tr"),
        P("tr", "tc"),
        P("tc", "tr"),
        P("tc", "tr"),
        P("tr", "tc"),
    )
    return jax.shard_map(
        on_device, mesh=mesh, in_specs=in_specs, out_specs=out_specs, check_vma=False
    )
```

profile of v0, /device:TPU:0, one launch (start us, length us, event | category | flops | bytes accessed | tf_op | source)
XLA Modules:
  0.0 632.3 jit_solution(9734206565967160406)
XLA Ops:
  9.2 3.0 collective-permute-start
  13.7 3.2 fusion.110
  23.0 2.9 convolution_convert_fusion.4
  26.1 3.1 convolution_convert_fusion.5
  33.2 3.6 add_convert_fusion.4
  44.4 3.7 convert_add_fusion.own
  50.2 22.0 %collective-permute-done.8 = f32[1024]{0:T(1024)S(1)} collective-permute-done((f32[1024]{0:T(1024)S(1)}, f32[1024]{0:T(1024)S(1)}, u32[]{:S(2)}, u32[]{:S(2)}) %collective-permute-start.8) | collective-permute-done | bytes 4128 | tf_op jit(solution)/shard_map/ppermute | solution.py:36
  76.7 9.5 %shard_map.237 = (f32[1024,512]{1,0:T(8,128)}, bf16[1024,256]{1,0:T(8,128)(2,1)S(1)}, bf16[1024,128]{1,0:T(8,128)(2,1)S(1)}, bf16[1024,128]{1,0:T(8,128)(2,1)S(1...) custom-call(s32[1]{0:T(128)} %bitcast.side, f32[1024,512]{1,0:T(8,128)} %convert_add_fusion.own, ...), custom_call_target="tpu_custom_call" | custom-call | bytes 1024 | tf_op jit(solution)/shard_map/pallas_call | solution.py:295
  93.0 6.6 %collective-permute-done.10 = bf16[1024,256]{1,0:T(8,128)(2,1)S(1)} collective-permute-done((bf16[1024,256]{1,0:T(8,128)(2,1)S(1)}, bf16[1024,256]{1,0:T(8,128)(2,1)S(1)}, u32[]{:S(2)}, u32[]{:S(2)}) %collective-permute-start.10) | collective-permute-done | bytes 524320 | tf_op jit(solution)/shard_map/ppermute | solution.py:36
  111.2 9.7 %collective-permute-done.14 = bf16[512,512]{1,0:T(8,128)(2,1)} collective-permute-done((bf16[512,512]{1,0:T(8,128)(2,1)S(1)}, bf16[512,512]{1,0:T(8,128)(2,1)}, u32[]{:S(2)}, u32[]{:S(2)}) %collective-permute-start.14) | collective-permute-done | bytes 524320 | tf_op jit(solution)/shard_map/ppermute | solution.py:44
  129.1 9.4 %collective-permute-done.22 = f32[1024]{0:T(1024)S(1)} collective-permute-done((f32[1024]{0:T(1024)S(1)}, f32[1024]{0:T(1024)S(1)}, u32[]{:S(2)}, u32[]{:S(2)}) %collective-permute-start.22) | collective-permute-done | bytes 4128 | tf_op jit(solution)/shard_map/ppermute | solution.py:36
  149.6 11.4 %shard_map.238 = (bf16[1024,768]{1,0:T(8,128)(2,1)}, bf16[1024,1536]{1,0:T(8,128)(2,1)}, bf16[1024,1536]{1,0:T(8,128)(2,1)}, f32[1024,1]{1,0:T(8,128)S(1)}) custom-call(bf16[512,512]{1,0:T(8,128)(2,1)S(1)} %multiply_convert_fusion.2.refs_0_, bf16[512,512]{1,0:T(8,128)(2,1)} %collective-permute-done.28.refs_1_, bf16[512,512]{1,0:T(8,128)(2,1)S(1)} %copy-done.24, ...), custom_call_target="tpu_custom_call" | custom-call | bytes 1024 | tf_op jit(solution)/shard_map/pallas_call | solution.py:369
  165.0 11.9 %shard_map.239 = (bf16[1024,768]{1,0:T(8,128)(2,1)}, bf16[1024,1536]{1,0:T(8,128)(2,1)}, bf16[1024,1536]{1,0:T(8,128)(2,1)}, f32[1024,1]{1,0:T(8,128)S(1)}) custom-call(bf16[512,512]{1,0:T(8,128)(2,1)} %collective-permute-done.18.refs_0_, ...), custom_call_target="tpu_custom_call", output_to_operand_aliasing={{0}: (17, {}), {1}: (18, {}), {2}: (19, {}), {3}: (20, {})} | custom-call | bytes 1024 | tf_op jit(solution)/shard_map/pallas_call | solution.py:369
  176.9 4.0 convolution_convert_fusion.1
  182.9 2.8 convolution_convert_fusion.2
  187.4 5.1 convolution_convert_fusion.3
  194.5 4.3 fusion.109
  198.8 3.1 add_convert_fusion.2
  205.5 4.2 convolution_convert_fusion
  222.5 2.8 collective-permute-done.37
  235.2 4.1 collective-permute-done.39
  245.8 8.2 %collective-permute-done.42 = bf16[512,512]{1,0:T(8,128)(2,1)S(1)} collective-permute-done((bf16[512,512]{1,0:T(8,128)(2,1)S(1)}, bf16[512,512]{1,0:T(8,128)(2,1)S(1)}, u32[]{:S(2)}, u32[]{:S(2)}) %collective-permute-start.42) | collective-permute-done | bytes 524320 | tf_op jit(solution)/shard_map/ppermute | solution.py:44
  255.2 3.5 collective-permute-start.52
  261.8 9.2 %collective-permute-done.52.refs_1_ = bf16[512,512]{1,0:T(8,128)(2,1)S(1)} collective-permute-done((bf16[512,512]{1,0:T(8,128)(2,1)S(1)}, bf16[512,512]{1,0:T(8,128)(2,1)S(1)}, u32[]{:S(2)}, u32[]{:S(2)}) %collective-permute-start.52) | collective-permute-done | bytes 524320 | tf_op jit(solution)/shard_map/ppermute | solution.py:78
  273.6 11.5 %collective-permute-start.58 = (bf16[512,512]{1,0:T(8,128)(2,1)S(1)}, bf16[512,512]{1,0:T(8,128)(2,1)S(1)}, u32[]{:S(2)}, u32[]{:S(2)}) collective-permute-start(bf16[512,512]{1,0:T(8,128)(2,1)S(1)} %get-tuple-element.433), channel_id=1, source_target_pairs={{0,8},{8,0},{16,24},{24,16},{1,9},{9,1},{17,25},{25,17},{2,10},{10... | collective-permute-start | bytes 1572872 | tf_op jit(solution)/shard_map/ppermute | solution.py:78
  285.8 2.8 collective-permute-start.57
  295.3 12.7 %shard_map.240 = (bf16[1024,512]{1,0:T(8,128)(2,1)}, f32[1,128]{1,0:T(1,128)S(1)}, f32[1,128]{1,0:T(1,128)S(1)}, f32[1024,1]{1,0:T(8,128)S(1)}) custom-call(s32[1]{0:T(128)} %bitcast.side, f32[1024,256]{1,0:T(8,128)} %convert_add_fusion.1.own, bf16[1024,256]{1,0:T(8,128)(2,1)S(1)} %collective-permute-done.50.from_y, f32[1024,512]{1,0:T(8,128)} %get-tuple-element.275.proj, ...), custom_call_target="tpu_custom_call" | custom-call | bytes 1024 | tf_op jit(solution)/shard_map/pallas_call | solution.py:295
  310.0 4.6 collective-permute-start.61
  318.0 7.2 %collective-permute-done.61.refs_1_ = bf16[512,512]{1,0:T(8,128)(2,1)S(1)} collective-permute-done((bf16[512,512]{1,0:T(8,128)(2,1)S(1)}, bf16[512,512]{1,0:T(8,128)(2,1)S(1)}, u32[]{:S(2)}, u32[]{:S(2)}) %collective-permute-start.61) | collective-permute-done | bytes 524320 | tf_op jit(solution)/shard_map/ppermute | solution.py:78
  329.2 7.8 %collective-permute-done.60.refs_3_ = bf16[512,512]{1,0:T(8,128)(2,1)S(1)} collective-permute-done((bf16[512,512]{1,0:T(8,128)(2,1)S(1)}, bf16[512,512]{1,0:T(8,128)(2,1)S(1)}, u32[]{:S(2)}, u32[]{:S(2)}) %collective-permute-start.60) | collective-permute-done | bytes 524320 | tf_op jit(solution)/shard_map/ppermute | solution.py:78
  341.7 2.8 multiply_convert_fusion
  344.5 3.0 fusion.40
  350.2 2.4 collective-permute-start.69
  353.3 2.3 collective-permute-start.73
  370.4 14.2 %collective-permute-done.68 = f32[1792]{0:T(1024)S(1)} collective-permute-done((f32[1792]{0:T(1024)S(1)}, f32[1792]{0:T(1024)S(1)}, u32[]{:S(2)}, u32[]{:S(2)}) %collective-permute-start.68) | collective-permute-done | bytes 7200 | tf_op jit(solution)/shard_map/ppermute | solution.py:44
  387.5 9.9 %collective-permute-done.72.refs_9_ = bf16[512,512]{1,0:T(8,128)(2,1)S(1)} collective-permute-done((bf16[512,512]{1,0:T(8,128)(2,1)S(1)}, bf16[512,512]{1,0:T(8,128)(2,1)S(1)}, u32[]{:S(2)}, u32[]{:S(2)}) %collective-permute-start.72) | collective-permute-done | bytes 524320 | tf_op jit(solution)/shard_map/ppermute | solution.py:78
  402.7 3.4 collective-permute-start.74
  406.1 7.3 %collective-permute-done.76.refs_11_ = bf16[512,512]{1,0:T(8,128)(2,1)S(1)} collective-permute-done((bf16[512,512]{1,0:T(8,128)(2,1)S(1)}, bf16[512,512]{1,0:T(8,128)(2,1)S(1)}, u32[]{:S(2)}, u32[]{:S(2)}) %collective-permute-start.76) | collective-permute-done | bytes 524320 | tf_op jit(solution)/shard_map/ppermute | solution.py:78
  417.2 2.6 collective-permute-start.81
  419.8 3.3 all-gather.15.cloned.1.call-done
  423.1 4.0 fusion.13
  428.4 4.0 fusion.10
  435.5 2.5 broadcast_select_fusion.10
  439.5 2.4 broadcast_select_fusion.7
  447.6 5.3 collective-permute-done.79.refs_1_
  455.2 8.4 %collective-permute-done.84.refs_3_ = bf16[512,512]{1,0:T(8,128)(2,1)} collective-permute-done((bf16[512,512]{1,0:T(8,128)(2,1)}, bf16[512,512]{1,0:T(8,128)(2,1)}, u32[]{:S(2)}, u32[]{:S(2)}) %collective-permute-start.84) | collective-permute-done | bytes 524320 | tf_op jit(solution)/shard_map/ppermute | solution.py:78
  463.6 2.4 broadcast_select_fusion.8
  473.5 4.0 collective-permute-start.87
  477.5 3.3 collective-permute-done.82.refs_5_
  482.6 4.8 fusion.31
  501.3 3.5 collective-permute-start.90
  507.8 9.8 %collective-permute-done.90.refs_13_ = bf16[512,512]{1,0:T(8,128)(2,1)S(1)} collective-permute-done((bf16[512,512]{1,0:T(8,128)(2,1)S(1)}, bf16[512,512]{1,0:T(8,128)(2,1)S(1)}, u32[]{:S(2)}, u32[]{:S(2)}) %collective-permute-start.90) | collective-permute-done | bytes 524320 | tf_op jit(solution)/shard_map/ppermute | solution.py:78
  522.5 6.4 %collective-permute-done.92.refs_15_ = bf16[512,512]{1,0:T(8,128)(2,1)S(1)} collective-permute-done((bf16[512,512]{1,0:T(8,128)(2,1)S(1)}, bf16[512,512]{1,0:T(8,128)(2,1)S(1)}, u32[]{:S(2)}, u32[]{:S(2)}) %collective-permute-start.92) | collective-permute-done | bytes 524320 | tf_op jit(solution)/shard_map/ppermute | solution.py:78
  529.8 6.5 %collective-permute-done.94.refs_17_ = bf16[512,512]{1,0:T(8,128)(2,1)S(1)} collective-permute-done((bf16[512,512]{1,0:T(8,128)(2,1)S(1)}, bf16[512,512]{1,0:T(8,128)(2,1)S(1)}, u32[]{:S(2)}, u32[]{:S(2)}) %collective-permute-start.94) | collective-permute-done | bytes 524320 | tf_op jit(solution)/shard_map/ppermute | solution.py:78
  545.6 8.2 %collective-permute-done.96.refs_19_ = bf16[512,512]{1,0:T(8,128)(2,1)} collective-permute-done((bf16[512,512]{1,0:T(8,128)(2,1)}, bf16[512,512]{1,0:T(8,128)(2,1)}, u32[]{:S(2)}, u32[]{:S(2)}) %collective-permute-start.96) | collective-permute-done | bytes 524320 | tf_op jit(solution)/shard_map/ppermute | solution.py:78
  555.6 4.7 collective-permute-done.98.refs_21_
  562.4 3.0 collective-permute-start.105
  566.5 6.7 %collective-permute-start.100 = (bf16[512,512]{1,0:T(8,128)(2,1)S(1)}, bf16[512,512]{1,0:T(8,128)(2,1)S(1)}, u32[]{:S(2)}, u32[]{:S(2)}) collective-permute-start(bf16[512,512]{1,0:T(8,128)(2,1)S(1)} %get-tuple-element.395), channel_id=1, source_target_pairs={{0,8},{8,0},{16,24},{24,16},{1,9},{9,1},{17,25},{25,17},{2,10},{10... | collective-permute-start | bytes 1572872 | tf_op jit(solution)/shard_map/ppermute | solution.py:78
  573.3 15.9 %collective-permute-start.109 = (bf16[512,512]{1,0:T(8,128)(2,1)S(1)}, bf16[512,512]{1,0:T(8,128)(2,1)}, u32[]{:S(2)}, u32[]{:S(2)}) collective-permute-start(bf16[512,512]{1,0:T(8,128)(2,1)S(1)} %add_convert_fusion.5.refs_10_), channel_id=1, source_target_pairs={{0,8},{8,0},{16,24},{24,16},{1,9},{9,1},{17,25},{25,17},{2,10},{10... | collective-permute-start | bytes 1572872 | tf_op jit(solution)/shard_map/ppermute | solution.py:78
  591.3 4.5 shard_map.241
  600.4 3.8 collective-permute-start.103
  605.8 2.4 shard_map.242
  608.3 9.0 %shard_map.243 = (f32[512,3072]{1,0:T(8,128)}, f32[512,3072]{1,0:T(8,128)}) custom-call(s32[5]{0:T(128)S(1)} %stack.39.words, bf16[512,512]{1,0:T(8,128)(2,1)S(1)} %copy-done.10, bf16[512,512]{1,0:T(8,128)(2,1)S(1)} %collective-permute-done.52.refs_1_, bf16[512,512]{1,0:T(8,128)(2,1)S(1)} %copy-done.11, ...), custom_call_target="tpu_custom_call" | custom-call | bytes 1024 | tf_op jit(solution)/shard_map/pallas_call | solution.py:408
  618.8 5.3 shard_map.244
  (663 shorter events, 236.1 us)
Async XLA Ops:
  7.2 92.5 %all-gather.7.cloned.1.call-start = ((), (), s32[]{:S(2)}) async-start(), calls=%async_computation | async-start | bytes 1966080 | tf_op jit(solution)/shard_map/all_gather | solution.py:473
  29.5 42.7 %collective-permute-start.5 = (bf16[128,1536]{1,0:T(8,128)(2,1)}, bf16[128,1536]{1,0:T(8,128)(2,1)}, u32[]{:S(2)}, u32[]{:S(2)}) collective-permute-start(bf16[128,1536]{1,0:T(8,128)(2,1)} %pad_maximum_fusion.19), channel_id=1, source_target_pairs={{0,2},{1,3},{2,0},{3,1},{4,6},{5,7},{6,4},{7,5},{8,10},{9,11},{10,... | collective-permute-start | bytes 1179656 | tf_op jit(solution)/shard_map/ppermute | solution.py:36
  31.2 41.0 %collective-permute-start.6 = (bf16[128,1536]{1,0:T(8,128)(2,1)}, bf16[128,1536]{1,0:T(8,128)(2,1)}, u32[]{:S(2)}, u32[]{:S(2)}) collective-permute-start(bf16[128,1536]{1,0:T(8,128)(2,1)} %pad_maximum_fusion.20), channel_id=1, source_target_pairs={{0,3},{1,2},{2,1},{3,0},{4,7},{5,6},{6,5},{7,4},{8,11},{9,10},{10,... | collective-permute-start | bytes 1179656 | tf_op jit(solution)/shard_map/ppermute | solution.py:40
  33.2 87.7 %all-gather.9.cloned.1.call-start = ((), (), s32[]{:S(2)}) async-start(), calls=%async_computation.1 | async-start | bytes 1966080 | tf_op jit(solution)/shard_map/all_gather | solution.py:515
  36.8 35.4 %collective-permute-start.4 = (bf16[1024,512]{1,0:T(8,128)(2,1)}, bf16[1024,512]{1,0:T(8,128)(2,1)}, u32[]{:S(2)}, u32[]{:S(2)}) collective-permute-start(bf16[1024,512]{1,0:T(8,128)(2,1)} %add_convert_fusion.4), channel_id=1, source_target_pairs={{0,2},{1,3},{2,0},{3,1},{4,6},{5,7},{6,4},{7,5},{8,10},{9,11},{10,... | collective-permute-start | bytes 3145736 | tf_op jit(solution)/shard_map/ppermute | solution.py:36
  49.6 22.6 %collective-permute-start.8 = (f32[1024]{0:T(1024)S(1)}, f32[1024]{0:T(1024)S(1)}, u32[]{:S(2)}, u32[]{:S(2)}) collective-permute-start(f32[1024]{0:T(1024)S(1)} %add.390), channel_id=1, source_target_pairs={{0,2},{1,3},{2,0},{3,1},{4,6},{5,7},{6,4},{7,5},{8,10},{9,11},{10,... | collective-permute-start | bytes 12296 | tf_op jit(solution)/shard_map/ppermute | solution.py:36
  72.3 76.3 %all-gather.11.cloned.1.call-start = ((), (), s32[]{:S(2)}) async-start(), calls=%async_computation.2 | async-start | bytes 1966080 | tf_op jit(solution)/shard_map/all_gather | solution.py:515
  89.2 22.0 %collective-permute-start.16 = (bf16[512,1536]{1,0:T(8,128)(2,1)}, bf16[512,1536]{1,0:T(8,128)(2,1)}, u32[]{:S(2)}, u32[]{:S(2)}) collective-permute-start(bf16[512,1536]{1,0:T(8,128)(2,1)} %pad_maximum_fusion), channel_id=1, source_target_pairs={{0,1},{1,0},{2,3},{3,2},{4,5},{5,4},{6,7},{7,6},{8,9},{9,8},{10,11... | collective-permute-start | bytes 4718600 | tf_op jit(solution)/shard_map/ppermute | solution.py:32
  89.2 21.9 %collective-permute-start.17 = (bf16[768,512]{1,0:T(8,128)(2,1)}, bf16[768,512]{1,0:T(8,128)(2,1)}, u32[]{:S(2)}, u32[]{:S(2)}) collective-permute-start(bf16[768,512]{1,0:T(8,128)(2,1)} %get-tuple-element.442), channel_id=1, source_target_pairs={{0,1},{1,0},{2,3},{3,2},{4,5},{5,4},{6,7},{7,6},{8,9},{9,8},{10,11... | collective-permute-start | bytes 2359304 | tf_op jit(solution)/shard_map/ppermute | solution.py:32
  101.8 321.3 %all-gather.15.cloned.1.call-start = ((), (), s32[]{:S(2)}) async-start(), calls=%async_computation.4 | async-start | bytes 15728640 | tf_op jit(solution)/shard_map/all_gather | solution.py:639
  102.1 37.0 %collective-permute-start.23 = (bf16[512,512]{1,0:T(8,128)(2,1)}, bf16[512,512]{1,0:T(8,128)(2,1)}, u32[]{:S(2)}, u32[]{:S(2)}) collective-permute-start(bf16[512,512]{1,0:T(8,128)(2,1)} %collective-permute-done.11.refs_10_), channel_id=1, source_target_pairs={{0,1},{1,0},{2,3},{3,2},{4,5},{5,4},{6,7},{7,6},{8,9},{9,8},{10,11... | collective-permute-start | bytes 1572872 | tf_op jit(solution)/shard_map/ppermute | solution.py:32
  111.1 28.0 %collective-permute-start.24 = (bf16[512,512]{1,0:T(8,128)(2,1)}, bf16[512,512]{1,0:T(8,128)(2,1)}, u32[]{:S(2)}, u32[]{:S(2)}) collective-permute-start(bf16[512,512]{1,0:T(8,128)(2,1)} %collective-permute-done.12.refs_10_), channel_id=1, source_target_pairs={{0,1},{1,0},{2,3},{3,2},{4,5},{5,4},{6,7},{7,6},{8,9},{9,8},{10,11... | collective-permute-start | bytes 1572872 | tf_op jit(solution)/shard_map/ppermute | solution.py:32
  139.7 21.4 %collective-permute-start.27 = (bf16[512,512]{1,0:T(8,128)(2,1)}, bf16[512,512]{1,0:T(8,128)(2,1)}, u32[]{:S(2)}, u32[]{:S(2)}) collective-permute-start(bf16[512,512]{1,0:T(8,128)(2,1)} %collective-permute-done.18.refs_0_), channel_id=1, source_target_pairs={{0,1},{1,0},{2,3},{3,2},{4,5},{5,4},{6,7},{7,6},{8,9},{9,8},{10,11... | collective-permute-start | bytes 1572872 | tf_op jit(solution)/shard_map/ppermute | solution.py:32
  142.2 18.9 %collective-permute-start.25 = (bf16[256,512]{1,0:T(8,128)(2,1)}, bf16[256,512]{1,0:T(8,128)(2,1)}, u32[]{:S(2)}, u32[]{:S(2)}) collective-permute-start(bf16[256,512]{1,0:T(8,128)(2,1)} %slice.164), channel_id=1, source_target_pairs={{0,2},{1,3},{2,0},{3,1},{4,6},{5,7},{6,4},{7,5},{8,10},{9,11},{10,... | collective-permute-start | bytes 786440 | tf_op jit(solution)/shard_map/ppermute | solution.py:36
  143.9 17.2 %collective-permute-start.26 = (bf16[256,512]{1,0:T(8,128)(2,1)}, bf16[256,512]{1,0:T(8,128)(2,1)}, u32[]{:S(2)}, u32[]{:S(2)}) collective-permute-start(bf16[256,512]{1,0:T(8,128)(2,1)} %slice.165), channel_id=1, source_target_pairs={{0,4},{4,0},{1,5},{5,1},{2,6},{6,2},{3,7},{7,3},{8,12},{12,8},{9,1... | collective-permute-start | bytes 786440 | tf_op jit(solution)/shard_map/ppermute | solution.py:44
  186.5 33.2 %collective-permute-start.35 = (bf16[512,512]{1,0:T(8,128)(2,1)}, bf16[512,512]{1,0:T(8,128)(2,1)}, u32[]{:S(2)}, u32[]{:S(2)}) collective-permute-start(bf16[512,512]{1,0:T(8,128)(2,1)} %get-tuple-element.244), channel_id=1, source_target_pairs={{0,8},{8,0},{16,24},{24,16},{1,9},{9,1},{17,25},{25,17},{2,10},{10... | collective-permute-start | bytes 1572872 | tf_op jit(solution)/shard_map/ppermute | solution.py:78
  192.6 36.6 %collective-permute-start.41 = (bf16[512,512]{1,0:T(8,128)(2,1)}, bf16[512,512]{1,0:T(8,128)(2,1)}, u32[]{:S(2)}, u32[]{:S(2)}) collective-permute-start(bf16[512,512]{1,0:T(8,128)(2,1)} %get-tuple-element.253), channel_id=1, source_target_pairs={{0,8},{8,0},{16,24},{24,16},{1,9},{9,1},{17,25},{25,17},{2,10},{10... | collective-permute-start | bytes 1572872 | tf_op jit(solution)/shard_map/ppermute | solution.py:78
  221.7 23.1 %collective-permute-start.44 = (bf16[512,512]{1,0:T(8,128)(2,1)S(1)}, bf16[512,512]{1,0:T(8,128)(2,1)S(1)}, u32[]{:S(2)}, u32[]{:S(2)}) collective-permute-start(bf16[512,512]{1,0:T(8,128)(2,1)S(1)} %add_convert_fusion.57), channel_id=1, source_target_pairs={{8,16},{16,8},{9,17},{17,9},{10,18},{18,10},{11,19},{19,11},{12,20... | collective-permute-start | bytes 1572872 | tf_op jit(solution)/shard_map/ppermute | solution.py:73
  225.4 33.8 %collective-permute-start.51 = (bf16[512,1536]{1,0:T(8,128)(2,1)S(1)}, bf16[512,1536]{1,0:T(8,128)(2,1)S(1)}, u32[]{:S(2)}, u32[]{:S(2)}) collective-permute-start(bf16[512,1536]{1,0:T(8,128)(2,1)S(1)} %copy-done.151), channel_id=1, source_target_pairs={{0,1},{1,0},{2,3},{3,2},{4,5},{5,4},{6,7},{7,6},{8,9},{9,8},{10,11... | collective-permute-start | bytes 4718600 | tf_op jit(solution)/shard_map/ppermute | solution.py:32
  227.7 17.0 %collective-permute-start.43 = (bf16[512,512]{1,0:T(8,128)(2,1)S(1)}, bf16[512,512]{1,0:T(8,128)(2,1)S(1)}, u32[]{:S(2)}, u32[]{:S(2)}) collective-permute-start(bf16[512,512]{1,0:T(8,128)(2,1)S(1)} %copy-done.90), channel_id=1, source_target_pairs={{0,8},{8,0},{16,24},{24,16},{1,9},{9,1},{17,25},{25,17},{2,10},{10... | collective-permute-start | bytes 1572872 | tf_op jit(solution)/shard_map/ppermute | solution.py:78
  239.3 20.8 %collective-permute-start.48 = (bf16[512,512]{1,0:T(8,128)(2,1)S(1)}, bf16[512,512]{1,0:T(8,128)(2,1)S(1)}, u32[]{:S(2)}, u32[]{:S(2)}) collective-permute-start(bf16[512,512]{1,0:T(8,128)(2,1)S(1)} %get-tuple-element.262), channel_id=1, source_target_pairs={{0,8},{8,0},{16,24},{24,16},{1,9},{9,1},{17,25},{25,17},{2,10},{10... | collective-permute-start | bytes 1572872 | tf_op jit(solution)/shard_map/ppermute | solution.py:78
  260.0 32.7 %collective-permute-start.46 = (bf16[1024,256]{1,0:T(8,128)(2,1)S(1)}, bf16[1024,256]{1,0:T(8,128)(2,1)S(1)}, u32[]{:S(2)}, u32[]{:S(2)}) collective-permute-start(bf16[1024,256]{1,0:T(8,128)(2,1)S(1)} %convolution_convert_fusion.9), channel_id=1, source_target_pairs={{0,1},{1,0},{2,3},{3,2},{4,5},{5,4},{6,7},{7,6},{8,9},{9,8},{10,11... | collective-permute-start | bytes 1572872 | tf_op jit(solution)/shard_map/ppermute | solution.py:32
  272.2 23.1 %collective-permute-start.50 = (bf16[1024,256]{1,0:T(8,128)(2,1)S(1)}, bf16[1024,256]{1,0:T(8,128)(2,1)S(1)}, u32[]{:S(2)}, u32[]{:S(2)}) collective-permute-start(bf16[1024,256]{1,0:T(8,128)(2,1)S(1)} %add_convert_fusion.50), channel_id=1, source_target_pairs={{0,2},{1,3},{2,0},{3,1},{4,6},{5,7},{6,4},{7,5},{8,10},{9,11},{10,... | collective-permute-start | bytes 1572872 | tf_op jit(solution)/shard_map/ppermute | solution.py:36
  273.6 34.3 %collective-permute-start.58 = (bf16[512,512]{1,0:T(8,128)(2,1)S(1)}, bf16[512,512]{1,0:T(8,128)(2,1)S(1)}, u32[]{:S(2)}, u32[]{:S(2)}) collective-permute-start(bf16[512,512]{1,0:T(8,128)(2,1)S(1)} %get-tuple-element.433), channel_id=1, source_target_pairs={{0,8},{8,0},{16,24},{24,16},{1,9},{9,1},{17,25},{25,17},{2,10},{10... | collective-permute-start | bytes 1572872 | tf_op jit(solution)/shard_map/ppermute | solution.py:78
  285.1 23.9 %collective-permute-start.59 = (bf16[512,512]{1,0:T(8,128)(2,1)S(1)}, bf16[512,512]{1,0:T(8,128)(2,1)S(1)}, u32[]{:S(2)}, u32[]{:S(2)}) collective-permute-start(bf16[512,512]{1,0:T(8,128)(2,1)S(1)} %add_convert_fusion.52), channel_id=1, source_target_pairs={{8,16},{16,8},{9,17},{17,9},{10,18},{18,10},{11,19},{19,11},{12,20... | collective-permute-start | bytes 1572872 | tf_op jit(solution)/shard_map/ppermute | solution.py:73
  285.8 28.9 %collective-permute-start.57 = (bf16[512,512]{1,0:T(8,128)(2,1)S(1)}, bf16[512,512]{1,0:T(8,128)(2,1)S(1)}, u32[]{:S(2)}, u32[]{:S(2)}) collective-permute-start(bf16[512,512]{1,0:T(8,128)(2,1)S(1)} %get-tuple-element.431), channel_id=1, source_target_pairs={{0,8},{8,0},{16,24},{24,16},{1,9},{9,1},{17,25},{25,17},{2,10},{10... | collective-permute-start | bytes 1572872 | tf_op jit(solution)/shard_map/ppermute | solution.py:78
  292.8 24.3 %collective-permute-start.56 = (bf16[512,512]{1,0:T(8,128)(2,1)S(1)}, bf16[512,512]{1,0:T(8,128)(2,1)S(1)}, u32[]{:S(2)}, u32[]{:S(2)}) collective-permute-start(bf16[512,512]{1,0:T(8,128)(2,1)S(1)} %add_convert_fusion.49), channel_id=1, source_target_pairs={{8,16},{16,8},{9,17},{17,9},{10,18},{18,10},{11,19},{19,11},{12,20... | collective-permute-start | bytes 1572872 | tf_op jit(solution)/shard_map/ppermute | solution.py:73
  308.1 19.8 %collective-permute-start.62 = (bf16[512,512]{1,0:T(8,128)(2,1)S(1)}, bf16[512,512]{1,0:T(8,128)(2,1)S(1)}, u32[]{:S(2)}, u32[]{:S(2)}) collective-permute-start(bf16[512,512]{1,0:T(8,128)(2,1)S(1)} %add_convert_fusion.46), channel_id=1, source_target_pairs={{8,16},{16,8},{9,17},{17,9},{10,18},{18,10},{11,19},{19,11},{12,20... | collective-permute-start | bytes 1572872 | tf_op jit(solution)/shard_map/ppermute | solution.py:73
  314.8 23.2 %collective-permute-start.63 = (bf16[512,512]{1,0:T(8,128)(2,1)S(1)}, bf16[512,512]{1,0:T(8,128)(2,1)S(1)}, u32[]{:S(2)}, u32[]{:S(2)}) collective-permute-start(bf16[512,512]{1,0:T(8,128)(2,1)S(1)} %add_convert_fusion.44), channel_id=1, source_target_pairs={{8,16},{16,8},{9,17},{17,9},{10,18},{18,10},{11,19},{19,11},{12,20... | collective-permute-start | bytes 1572872 | tf_op jit(solution)/shard_map/ppermute | solution.py:73
  315.5 23.6 %collective-permute-start.54 = (bf16[1024,512]{1,0:T(8,128)(2,1)S(1)}, bf16[1024,512]{1,0:T(8,128)(2,1)S(1)}, u32[]{:S(2)}, u32[]{:S(2)}) collective-permute-start(bf16[1024,512]{1,0:T(8,128)(2,1)S(1)} %copy-done.116), channel_id=1, source_target_pairs={{0,2},{1,3},{2,0},{3,1},{4,6},{5,7},{6,4},{7,5},{8,10},{9,11},{10,... | collective-permute-start | bytes 3145736 | tf_op jit(solution)/shard_map/ppermute | solution.py:36
  317.0 22.1 %collective-permute-start.55 = (bf16[1024,512]{1,0:T(8,128)(2,1)S(1)}, bf16[1024,512]{1,0:T(8,128)(2,1)S(1)}, u32[]{:S(2)}, u32[]{:S(2)}) collective-permute-start(bf16[1024,512]{1,0:T(8,128)(2,1)S(1)} %copy-done.116), channel_id=1, source_target_pairs={{0,1},{1,0},{2,3},{3,2},{4,5},{5,4},{6,7},{7,6},{8,9},{9,8},{10,11... | collective-permute-start | bytes 3145736 | tf_op jit(solution)/shard_map/ppermute | solution.py:32
  341.1 141.4 %all-gather.13.cloned.1.call-start = ((), (), s32[]{:S(2)}) async-start(), calls=%async_computation.3 | async-start | bytes 7864320 | tf_op jit(solution)/shard_map/all_gather | solution.py:655
  350.2 17.1 %collective-permute-start.69 = (bf16[512,512]{1,0:T(8,128)(2,1)S(1)}, bf16[512,512]{1,0:T(8,128)(2,1)S(1)}, u32[]{:S(2)}, u32[]{:S(2)}) collective-permute-start(bf16[512,512]{1,0:T(8,128)(2,1)S(1)} %copy-done.141), channel_id=1, source_target_pairs={{0,8},{8,0},{16,24},{24,16},{1,9},{9,1},{17,25},{25,17},{2,10},{10... | collective-permute-start | bytes 1572872 | tf_op jit(solution)/shard_map/ppermute | solution.py:78
  353.3 33.3 %collective-permute-start.73 = (bf16[512,512]{1,0:T(8,128)(2,1)S(1)}, bf16[512,512]{1,0:T(8,128)(2,1)S(1)}, u32[]{:S(2)}, u32[]{:S(2)}) collective-permute-start(bf16[512,512]{1,0:T(8,128)(2,1)S(1)} %copy-done.140), channel_id=1, source_target_pairs={{0,8},{8,0},{16,24},{24,16},{1,9},{9,1},{17,25},{25,17},{2,10},{10... | collective-permute-start | bytes 1572872 | tf_op jit(solution)/shard_map/ppermute | solution.py:78
  359.4 25.5 %collective-permute-start.67 = (bf16[1024,512]{1,0:T(8,128)(2,1)S(1)}, bf16[1024,512]{1,0:T(8,128)(2,1)S(1)}, u32[]{:S(2)}, u32[]{:S(2)}) collective-permute-start(bf16[1024,512]{1,0:T(8,128)(2,1)S(1)} %add_convert_fusion.1), channel_id=1, source_target_pairs={{0,4},{4,0},{1,5},{5,1},{2,6},{6,2},{3,7},{7,3},{8,12},{12,8},{9,1... | collective-permute-start | bytes 3145736 | tf_op jit(solution)/shard_map/ppermute | solution.py:44
  366.5 30.9 %collective-permute-start.75 = (bf16[512,512]{1,0:T(8,128)(2,1)S(1)}, bf16[512,512]{1,0:T(8,128)(2,1)S(1)}, u32[]{:S(2)}, u32[]{:S(2)}) collective-permute-start(bf16[512,512]{1,0:T(8,128)(2,1)S(1)} %copy-done.91), channel_id=1, source_target_pairs={{8,16},{16,8},{9,17},{17,9},{10,18},{18,10},{11,19},{19,11},{12,20... | collective-permute-start | bytes 1572872 | tf_op jit(solution)/shard_map/ppermute | solution.py:73
  367.3 17.2 %collective-permute-start.68 = (f32[1792]{0:T(1024)S(1)}, f32[1792]{0:T(1024)S(1)}, u32[]{:S(2)}, u32[]{:S(2)}) collective-permute-start(f32[1792]{0:T(1024)S(1)} %pad_maximum_fusion.38), channel_id=1, source_target_pairs={{0,4},{4,0},{1,5},{5,1},{2,6},{6,2},{3,7},{7,3},{8,12},{12,8},{9,1... | collective-permute-start | bytes 21512 | tf_op jit(solution)/shard_map/ppermute | solution.py:44
  368.6 32.9 %collective-permute-start.71 = (bf16[512,512]{1,0:T(8,128)(2,1)S(1)}, bf16[512,512]{1,0:T(8,128)(2,1)S(1)}, u32[]{:S(2)}, u32[]{:S(2)}) collective-permute-start(bf16[512,512]{1,0:T(8,128)(2,1)S(1)} %add_convert_fusion.39), channel_id=1, source_target_pairs={{8,16},{16,8},{9,17},{17,9},{10,18},{18,10},{11,19},{19,11},{12,20... | collective-permute-start | bytes 1572872 | tf_op jit(solution)/shard_map/ppermute | solution.py:73
  386.8 29.2 %collective-permute-start.80 = (bf16[512,512]{1,0:T(8,128)(2,1)S(1)}, bf16[512,512]{1,0:T(8,128)(2,1)S(1)}, u32[]{:S(2)}, u32[]{:S(2)}) collective-permute-start(bf16[512,512]{1,0:T(8,128)(2,1)S(1)} %add_convert_fusion.36), channel_id=1, source_target_pairs={{8,16},{16,8},{9,17},{17,9},{10,18},{18,10},{11,19},{19,11},{12,20... | collective-permute-start | bytes 1572872 | tf_op jit(solution)/shard_map/ppermute | solution.py:73
  400.0 35.4 %collective-permute-start.78 = (bf16[512,512]{1,0:T(8,128)(2,1)}, bf16[512,512]{1,0:T(8,128)(2,1)}, u32[]{:S(2)}, u32[]{:S(2)}) collective-permute-start(bf16[512,512]{1,0:T(8,128)(2,1)} %add_convert_fusion.35), channel_id=1, source_target_pairs={{8,16},{16,8},{9,17},{17,9},{10,18},{18,10},{11,19},{19,11},{12,20... | collective-permute-start | bytes 1572872 | tf_op jit(solution)/shard_map/ppermute | solution.py:73
  402.7 30.6 %collective-permute-start.74 = (bf16[512,512]{1,0:T(8,128)(2,1)}, bf16[512,512]{1,0:T(8,128)(2,1)S(1)}, u32[]{:S(2)}, u32[]{:S(2)}) collective-permute-start(bf16[512,512]{1,0:T(8,128)(2,1)} %get-tuple-element.419), channel_id=1, source_target_pairs={{0,8},{8,0},{16,24},{24,16},{1,9},{9,1},{17,25},{25,17},{2,10},{10... | collective-permute-start | bytes 1572872 | tf_op jit(solution)/shard_map/ppermute | solution.py:78
  414.3 25.2 %collective-permute-start.83 = (bf16[512,512]{1,0:T(8,128)(2,1)}, bf16[512,512]{1,0:T(8,128)(2,1)}, u32[]{:S(2)}, u32[]{:S(2)}) collective-permute-start(bf16[512,512]{1,0:T(8,128)(2,1)} %add_convert_fusion.33), channel_id=1, source_target_pairs={{8,16},{16,8},{9,17},{17,9},{10,18},{18,10},{11,19},{19,11},{12,20... | collective-permute-start | bytes 1572872 | tf_op jit(solution)/shard_map/ppermute | solution.py:73
  417.2 17.3 %collective-permute-start.81 = (bf16[512,512]{1,0:T(8,128)(2,1)}, bf16[512,512]{1,0:T(8,128)(2,1)S(1)}, u32[]{:S(2)}, u32[]{:S(2)}) collective-permute-start(bf16[512,512]{1,0:T(8,128)(2,1)} %get-tuple-element.413), channel_id=1, source_target_pairs={{0,8},{8,0},{16,24},{24,16},{1,9},{9,1},{17,25},{25,17},{2,10},{10... | collective-permute-start | bytes 1572872 | tf_op jit(solution)/shard_map/ppermute | solution.py:78
  441.9 21.7 %collective-permute-start.84 = (bf16[512,512]{1,0:T(8,128)(2,1)}, bf16[512,512]{1,0:T(8,128)(2,1)}, u32[]{:S(2)}, u32[]{:S(2)}) collective-permute-start(bf16[512,512]{1,0:T(8,128)(2,1)} %get-tuple-element.409), channel_id=1, source_target_pairs={{0,8},{8,0},{16,24},{24,16},{1,9},{9,1},{17,25},{25,17},{2,10},{10... | collective-permute-start | bytes 1572872 | tf_op jit(solution)/shard_map/ppermute | solution.py:78
  442.4 21.2 %collective-permute-start.77 = (bf16[512,512]{1,0:T(8,128)(2,1)}, bf16[512,512]{1,0:T(8,128)(2,1)}, u32[]{:S(2)}, u32[]{:S(2)}) collective-permute-start(bf16[512,512]{1,0:T(8,128)(2,1)} %add_convert_fusion.32), channel_id=1, source_target_pairs={{8,16},{16,8},{9,17},{17,9},{10,18},{18,10},{11,19},{19,11},{12,20... | collective-permute-start | bytes 1572872 | tf_op jit(solution)/shard_map/ppermute | solution.py:73
  446.8 25.5 %collective-permute-start.86 = (bf16[512,512]{1,0:T(8,128)(2,1)}, bf16[512,512]{1,0:T(8,128)(2,1)S(1)}, u32[]{:S(2)}, u32[]{:S(2)}) collective-permute-start(bf16[512,512]{1,0:T(8,128)(2,1)} %add_convert_fusion.28), channel_id=1, source_target_pairs={{8,16},{16,8},{9,17},{17,9},{10,18},{18,10},{11,19},{19,11},{12,20... | collective-permute-start | bytes 1572872 | tf_op jit(solution)/shard_map/ppermute | solution.py:73
  469.3 35.4 %collective-permute-start.91 = (bf16[512,512]{1,0:T(8,128)(2,1)}, bf16[512,512]{1,0:T(8,128)(2,1)}, u32[]{:S(2)}, u32[]{:S(2)}) collective-permute-start(bf16[512,512]{1,0:T(8,128)(2,1)} %add_convert_fusion.25), channel_id=1, source_target_pairs={{8,16},{16,8},{9,17},{17,9},{10,18},{18,10},{11,19},{19,11},{12,20... | collective-permute-start | bytes 1572872 | tf_op jit(solution)/shard_map/ppermute | solution.py:73
  470.8 28.2 %collective-permute-start.89 = (bf16[512,512]{1,0:T(8,128)(2,1)}, bf16[512,512]{1,0:T(8,128)(2,1)}, u32[]{:S(2)}, u32[]{:S(2)}) collective-permute-start(bf16[512,512]{1,0:T(8,128)(2,1)} %add_convert_fusion.27), channel_id=1, source_target_pairs={{8,16},{16,8},{9,17},{17,9},{10,18},{18,10},{11,19},{19,11},{12,20... | collective-permute-start | bytes 1572872 | tf_op jit(solution)/shard_map/ppermute | solution.py:73
  473.5 23.4 %collective-permute-start.87 = (bf16[512,512]{1,0:T(8,128)(2,1)}, bf16[512,512]{1,0:T(8,128)(2,1)}, u32[]{:S(2)}, u32[]{:S(2)}) collective-permute-start(bf16[512,512]{1,0:T(8,128)(2,1)} %get-tuple-element.407), channel_id=1, source_target_pairs={{0,8},{8,0},{16,24},{24,16},{1,9},{9,1},{17,25},{25,17},{2,10},{10... | collective-permute-start | bytes 1572872 | tf_op jit(solution)/shard_map/ppermute | solution.py:78
  490.3 27.5 %collective-permute-start.93 = (bf16[512,512]{1,0:T(8,128)(2,1)S(1)}, bf16[512,512]{1,0:T(8,128)(2,1)S(1)}, u32[]{:S(2)}, u32[]{:S(2)}) collective-permute-start(bf16[512,512]{1,0:T(8,128)(2,1)S(1)} %copy-done.100), channel_id=1, source_target_pairs={{8,16},{16,8},{9,17},{17,9},{10,18},{18,10},{11,19},{19,11},{12,20... | collective-permute-start | bytes 1572872 | tf_op jit(solution)/shard_map/ppermute | solution.py:73
  501.3 16.4 %collective-permute-start.90 = (bf16[512,512]{1,0:T(8,128)(2,1)S(1)}, bf16[512,512]{1,0:T(8,128)(2,1)S(1)}, u32[]{:S(2)}, u32[]{:S(2)}) collective-permute-start(bf16[512,512]{1,0:T(8,128)(2,1)S(1)} %get-tuple-element.405), channel_id=1, source_target_pairs={{0,8},{8,0},{16,24},{24,16},{1,9},{9,1},{17,25},{25,17},{2,10},{10... | collective-permute-start | bytes 1572872 | tf_op jit(solution)/shard_map/ppermute | solution.py:78
  507.0 21.8 %collective-permute-start.92 = (bf16[512,512]{1,0:T(8,128)(2,1)S(1)}, bf16[512,512]{1,0:T(8,128)(2,1)S(1)}, u32[]{:S(2)}, u32[]{:S(2)}) collective-permute-start(bf16[512,512]{1,0:T(8,128)(2,1)S(1)} %get-tuple-element.403), channel_id=1, source_target_pairs={{0,8},{8,0},{16,24},{24,16},{1,9},{9,1},{17,25},{25,17},{2,10},{10... | collective-permute-start | bytes 1572872 | tf_op jit(solution)/shard_map/ppermute | solution.py:78
  518.8 17.5 %collective-permute-start.94 = (bf16[512,512]{1,0:T(8,128)(2,1)S(1)}, bf16[512,512]{1,0:T(8,128)(2,1)S(1)}, u32[]{:S(2)}, u32[]{:S(2)}) collective-permute-start(bf16[512,512]{1,0:T(8,128)(2,1)S(1)} %get-tuple-element.401), channel_id=1, source_target_pairs={{0,8},{8,0},{16,24},{24,16},{1,9},{9,1},{17,25},{25,17},{2,10},{10... | collective-permute-start | bytes 1572872 | tf_op jit(solution)/shard_map/ppermute | solution.py:78
  520.8 16.5 %collective-permute-start.95 = (bf16[512,512]{1,0:T(8,128)(2,1)S(1)}, bf16[512,512]{1,0:T(8,128)(2,1)S(1)}, u32[]{:S(2)}, u32[]{:S(2)}) collective-permute-start(bf16[512,512]{1,0:T(8,128)(2,1)S(1)} %add_convert_fusion.22), channel_id=1, source_target_pairs={{8,16},{16,8},{9,17},{17,9},{10,18},{18,10},{11,19},{19,11},{12,20... | collective-permute-start | bytes 1572872 | tf_op jit(solution)/shard_map/ppermute | solution.py:73
  521.5 18.8 %collective-permute-start.97 = (bf16[512,512]{1,0:T(8,128)(2,1)S(1)}, bf16[512,512]{1,0:T(8,128)(2,1)S(1)}, u32[]{:S(2)}, u32[]{:S(2)}) collective-permute-start(bf16[512,512]{1,0:T(8,128)(2,1)S(1)} %add_convert_fusion.19), channel_id=1, source_target_pairs={{8,16},{16,8},{9,17},{17,9},{10,18},{18,10},{11,19},{19,11},{12,20... | collective-permute-start | bytes 1572872 | tf_op jit(solution)/shard_map/ppermute | solution.py:73
  541.6 18.7 %collective-permute-start.98 = (bf16[512,512]{1,0:T(8,128)(2,1)}, bf16[512,512]{1,0:T(8,128)(2,1)}, u32[]{:S(2)}, u32[]{:S(2)}) collective-permute-start(bf16[512,512]{1,0:T(8,128)(2,1)} %get-tuple-element.397), channel_id=1, source_target_pairs={{0,8},{8,0},{16,24},{24,16},{1,9},{9,1},{17,25},{25,17},{2,10},{10... | collective-permute-start | bytes 1572872 | tf_op jit(solution)/shard_map/ppermute | solution.py:78
  542.0 20.2 %collective-permute-start.104 = (bf16[512,512]{1,0:T(8,128)(2,1)}, bf16[512,512]{1,0:T(8,128)(2,1)S(1)}, u32[]{:S(2)}, u32[]{:S(2)}) collective-permute-start(bf16[512,512]{1,0:T(8,128)(2,1)} %add_convert_fusion.13), channel_id=1, source_target_pairs={{8,16},{16,8},{9,17},{17,9},{10,18},{18,10},{11,19},{19,11},{12,20... | collective-permute-start | bytes 1572872 | tf_op jit(solution)/shard_map/ppermute | solution.py:73
  542.8 22.6 %collective-permute-start.99 = (bf16[512,512]{1,0:T(8,128)(2,1)}, bf16[512,512]{1,0:T(8,128)(2,1)S(1)}, u32[]{:S(2)}, u32[]{:S(2)}) collective-permute-start(bf16[512,512]{1,0:T(8,128)(2,1)} %add_convert_fusion.15), channel_id=1, source_target_pairs={{8,16},{16,8},{9,17},{17,9},{10,18},{18,10},{11,19},{19,11},{12,20... | collective-permute-start | bytes 1572872 | tf_op jit(solution)/shard_map/ppermute | solution.py:73
  554.9 34.3 %collective-permute-start.106 = (bf16[512,512]{1,0:T(8,128)(2,1)S(1)}, bf16[512,512]{1,0:T(8,128)(2,1)S(1)}, u32[]{:S(2)}, u32[]{:S(2)}) collective-permute-start(bf16[512,512]{1,0:T(8,128)(2,1)S(1)} %add_convert_fusion.11), channel_id=1, source_target_pairs={{8,16},{16,8},{9,17},{17,9},{10,18},{18,10},{11,19},{19,11},{12,20... | collective-permute-start | bytes 1572872 | tf_op jit(solution)/shard_map/ppermute | solution.py:73
  562.4 55.6 %collective-permute-start.105 = (bf16[512,512]{1,0:T(8,128)(2,1)S(1)}, bf16[512,512]{1,0:T(8,128)(2,1)S(1)}, u32[]{:S(2)}, u32[]{:S(2)}) collective-permute-start(bf16[512,512]{1,0:T(8,128)(2,1)S(1)} %add_convert_fusion.7.refs_6_), channel_id=1, source_target_pairs={{0,8},{8,0},{16,24},{24,16},{1,9},{9,1},{17,25},{25,17},{2,10},{10... | collective-permute-start | bytes 1572872 | tf_op jit(solution)/shard_map/ppermute | solution.py:78
  566.5 23.0 %collective-permute-start.100 = (bf16[512,512]{1,0:T(8,128)(2,1)S(1)}, bf16[512,512]{1,0:T(8,128)(2,1)S(1)}, u32[]{:S(2)}, u32[]{:S(2)}) collective-permute-start(bf16[512,512]{1,0:T(8,128)(2,1)S(1)} %get-tuple-element.395), channel_id=1, source_target_pairs={{0,8},{8,0},{16,24},{24,16},{1,9},{9,1},{17,25},{25,17},{2,10},{10... | collective-permute-start | bytes 1572872 | tf_op jit(solution)/shard_map/ppermute | solution.py:78
  573.3 44.6 %collective-permute-start.109 = (bf16[512,512]{1,0:T(8,128)(2,1)S(1)}, bf16[512,512]{1,0:T(8,128)(2,1)}, u32[]{:S(2)}, u32[]{:S(2)}) collective-permute-start(bf16[512,512]{1,0:T(8,128)(2,1)S(1)} %add_convert_fusion.5.refs_10_), channel_id=1, source_target_pairs={{0,8},{8,0},{16,24},{24,16},{1,9},{9,1},{17,25},{25,17},{2,10},{10... | collective-permute-start | bytes 1572872 | tf_op jit(solution)/shard_map/ppermute | solution.py:78
  589.4 28.5 %collective-permute-start.107 = (bf16[512,512]{1,0:T(8,128)(2,1)S(1)}, bf16[512,512]{1,0:T(8,128)(2,1)}, u32[]{:S(2)}, u32[]{:S(2)}) collective-permute-start(bf16[512,512]{1,0:T(8,128)(2,1)S(1)} %add_convert_fusion.6.refs_8_), channel_id=1, source_target_pairs={{0,8},{8,0},{16,24},{24,16},{1,9},{9,1},{17,25},{25,17},{2,10},{10... | collective-permute-start | bytes 1572872 | tf_op jit(solution)/shard_map/ppermute | solution.py:78
  600.4 23.7 %collective-permute-start.103 = (bf16[512,512]{1,0:T(8,128)(2,1)S(1)}, bf16[512,512]{1,0:T(8,128)(2,1)S(1)}, u32[]{:S(2)}, u32[]{:S(2)}) collective-permute-start(bf16[512,512]{1,0:T(8,128)(2,1)S(1)} %add_convert_fusion.8), channel_id=1, source_target_pairs={{0,8},{8,0},{16,24},{24,16},{1,9},{9,1},{17,25},{25,17},{2,10},{10... | collective-permute-start | bytes 1572872 | tf_op jit(solution)/shard_map/ppermute | solution.py:78
  (203 other events, 2180.9 us)
Sparse Core Ops, SparseCore 0:
  33.3 38.5 all-gather.6
  73.5 37.5 all-gather.8
  112.6 35.9 all-gather.10
  341.2 81.7 all-gather.14
  424.5 46.3 all-gather.12
where the time goes:
time: 641 us; the launch traced here: 632 us
  waiting for transfers between devices  183 us (29%)
  starting transfers between devices  150 us (23%)
  other arithmetic  91.4 us (14%)
  matrix products  85.7 us (13%)
  Pallas kernels  66.7 us (10%)
  local copies, waits for them, and re-layouts  38.7 us (6%)
  between operations  16.5 us (3%)
    ppermute x29, waiting for transfers between devices, _swap_outer(): lax.ppermute(piece, 'dp', [(0, 1), (1, 0), (2, 3), (3, 2)])  94.1 us
    ppermute x29, starting transfers between devices, _swap_outer(): lax.ppermute(piece, 'dp', [(0, 1), (1, 0), (2, 3), (3, 2)])  84.4 us
    ppermute x15, waiting for transfers between devices, swap_y(): return lax.ppermute(block, 'tc', [(i, i ^ 2) for i in range(4)])  42.2 us
    ppermute x14, waiting for transfers between devices, swap_x(): return lax.ppermute(block, 'tr', [(0, 1), (1, 0)])  39.4 us
    dot_general x16, matrix products, contract_rows(): lax.dot_general(left_side, right_side, (((0,), (0,)), ((), ())), preferre...  32.8 us
    convert_element_type x37, other arithmetic, low(): return array.astype(bf16)  31.6 us
    select_n x21, other arithmetic, send(): out = jnp.where(self.middle, self.total[which - self.lag], out)  29.5 us
    dot_general x14, matrix products, dot(): return jnp.dot(left_side, right_side, preferred_element_type=f32)  28.9 us
  transfers between devices with their start and end apart: 115, of which 30 were waited for; matrix products, arithmetic and copies ran while one was open for 30% of the time, Pallas kernels for 9%

commit v1 on v0

--- a/solution.py
+++ b/solution.py
@@ -52,7 +52,6 @@
 class LineSums:
     def __init__(self, lag=4):
         self.lag = lag
-        self.last = ()
         self.short = lax.axis_size("dp") == 4
         place = lax.axis_index("dp")
         self.middle = (place == 1) | (place == 2)
@@ -92,17 +91,26 @@
         self._swap_outer(out)
         return (marker, out) if strict else marker
 
-    def finish(self):
+    def _named(self, sums):
+        return lambda name: [s for n, s in zip(self.names, sums) if n == name]
+
+    def _ready(self):
+        return [(total, outer) for total, outer in zip(self.total, self.outer[self.lag :])]
+
+    def finish(self, filler):
         count = len(self.pieces)
-        if self.short:
-            self.last = self._consume(count - 2, ())
-            self._consume(count - 1, ())
-            for which in range(count - self.lag, count):
-                self._swap_outer(self.total[which])
-            sums = [(self.total[k], self.outer[k + self.lag]) for k in range(count)]
-        else:
-            sums = [(lax.psum(piece, "dp"),) for piece in self.pieces]
-        return lambda name: [s for n, s in zip(self.names, sums) if n == name]
+        if not self.short:
+            named = self._named([(lax.psum(piece, "dp"),) for piece in self.pieces])
+            filler(named)
+            return named
+        self._consume(count - 2, ())
+        self._consume(count - 1, ())
+        for which in range(count - self.lag, count):
+            piece = self.total[which]
+            if which == count - 2:
+                piece = after(piece, filler(self._named(self._ready())))
+            self._swap_outer(piece)
+        return self._named(self._ready())
 
 
 def after(value, *others):
@@ -684,8 +692,6 @@
     marker = mixed_x
     while line.queue:
         marker = line.send(marker, False)
-    sums_of = line.finish()
-
     words = jnp.stack([*around, line.middle.astype(jnp.int32)]).astype(jnp.int32)
     everything = slice(None)
 
@@ -705,26 +711,6 @@
             to += taken
         return plan
 
-    out_sums, qkv_sums, ffn_sums = after(
-        (sums_of("out"), sums_of("qkv"), sums_of("ffn")), line.last
-    )
-    ffn_plan = [
-        runs(0, 2 * k * units, units, width, 0, 1) + runs(0, (2 * k + 1) * units, units, width, 1, 1)
-        for k in range(4)
-    ]
-    w_gate_grad, w_up_grad = place_sums(words, ffn_sums, [(w_gate.shape, 1), (w_up.shape, 1)], ffn_plan)
-    [w_down_grad] = place_sums(
-        words,
-        sums_of("down"),
-        [(w_down.shape, 0)],
-        [runs(0, k * units, units, width, 0, 0) for k in range(4)],
-    )
-    [w_out_grad] = place_sums(
-        words,
-        out_sums,
-        [(w_out.shape, 0)],
-        [runs(0, k * q_width, q_width, width, 0, 0) for k in range(4)],
-    )
     block_width = q_width + 2 * k_width
     qkv_plan = [
         runs(0, k * block_width, q_width, width, 0, 1)
@@ -732,8 +718,32 @@
         + runs(0, k * block_width + q_width + k_width, k_width, width, 2, 1)
         for k in range(4)
     ]
-    w_query_grad, w_key_grad, w_value_grad = place_sums(
-        words, qkv_sums, [(w_query.shape, 1), (w_key.shape, 1), (w_value.shape, 1)], qkv_plan
+    ffn_plan = [
+        runs(0, 2 * k * units, units, width, 0, 1) + runs(0, (2 * k + 1) * units, units, width, 1, 1)
+        for k in range(4)
+    ]
+    placed = {}
+
+    def fill(sums_of):
+        out_plan = [runs(0, k * q_width, q_width, width, 0, 0) for k in range(4)]
+        placed["out"] = place_sums(words, sums_of("out"), [(w_out.shape, 0)], out_plan)
+        placed["qkv"] = place_sums(
+            words, sums_of("qkv"), [(w.shape, 1) for w in (w_query, w_key, w_value)], qkv_plan
+        )
+        placed["ffn"] = place_sums(
+            words, sums_of("ffn"), [(w.shape, 1) for w in (w_gate, w_up)], ffn_plan
+        )
+        return placed
+
+    sums_of = line.finish(fill)
+    [w_out_grad] = placed["out"]
+    w_query_grad, w_key_grad, w_value_grad = placed["qkv"]
+    w_gate_grad, w_up_grad = placed["ffn"]
+    [w_down_grad] = place_sums(
+        words,
+        sums_of("down"),
+        [(w_down.shape, 0)],
+        [runs(0, k * units, units, width, 0, 0) for k in range(4)],
     )
     attn_gain_part = sum(
         jnp.sum(w.astype(f32) * g, axis=1)

time: 641 us -> 636 us (level)
  waiting for transfers between devices: 183 us -> 172 us
    ppermute x29, waiting for transfers between devices: 94.1 us -> 81 us  [_swap_outer(): lax.ppermute(piece, 'dp', [(0, 1), (1, 0), (2, 3), (3, 2)])]
  transfers between devices with their start and end apart: 115 -> 115, of which waited for: 30 -> 31; matrix products, arithmetic and copies ran while one was open for 30% -> 30% of each run, Pallas kernels for 9% -> 9%
where the time goes in v1:
time: 636 us; the launch traced here: 628 us
  waiting for transfers between devices  172 us (27%)
  starting transfers between devices  156 us (25%)
  other arithmetic  91.2 us (14%)
  matrix products  84.4 us (13%)
  Pallas kernels  66.4 us (10%)
  local copies, waits for them, and re-layouts  41 us (6%)
  between operations  16.8 us (3%)
    ppermute x29, starting transfers between devices, _swap_outer(): lax.ppermute(piece, 'dp', [(0, 1), (1, 0), (2, 3), (3, 2)])  88.2 us
    ppermute x29, waiting for transfers between devices, _swap_outer(): lax.ppermute(piece, 'dp', [(0, 1), (1, 0), (2, 3), (3, 2)])  81 us
    ppermute x15, waiting for transfers between devices, swap_y(): return lax.ppermute(block, 'tc', [(i, i ^ 2) for i in range(4)])  41.9 us
    ppermute x14, waiting for transfers between devices, swap_x(): return lax.ppermute(block, 'tr', [(0, 1), (1, 0)])  41.4 us
    dot_general x16, matrix products, contract_rows(): lax.dot_general(left_side, right_side, (((0,), (0,)), ((), ())), preferre...  32.8 us
    select_n x21, other arithmetic, send(): out = jnp.where(self.middle, self.total[which - self.lag], out)  30.8 us
    convert_element_type x37, other arithmetic, low(): return array.astype(bf16)  30.3 us
    dot_general x14, matrix products, dot(): return jnp.dot(left_side, right_side, preferred_element_type=f32)  27.5 us
  transfers between devices with their start and end apart: 115, of which 31 were waited for; matrix products, arithmetic and copies ran while one was open for 30% of the time, Pallas kernels for 9%

profile of v1, /device:TPU:0, one launch (start us, length us, event | category | flops | bytes accessed | tf_op | source)
XLA Modules:
  0.0 627.6 jit_solution(1636517174973409725)
XLA Ops:
  9.2 3.0 collective-permute-start
  13.7 3.2 fusion.110
  24.9 3.1 convolution_convert_fusion.5
  32.0 3.6 add_convert_fusion.4
  43.6 3.4 convert_add_fusion.own
  49.2 21.8 %collective-permute-done.8 = f32[1024]{0:T(1024)S(1)} collective-permute-done((f32[1024]{0:T(1024)S(1)}, f32[1024]{0:T(1024)S(1)}, u32[]{:S(2)}, u32[]{:S(2)}) %collective-permute-start.8) | collective-permute-done | bytes 4128 | tf_op jit(solution)/shard_map/ppermute | solution.py:36
  75.8 9.5 %shard_map.237 = (f32[1024,512]{1,0:T(8,128)}, bf16[1024,256]{1,0:T(8,128)(2,1)S(1)}, bf16[1024,128]{1,0:T(8,128)(2,1)S(1)}, bf16[1024,128]{1,0:T(8,128)(2,1)S(1...) custom-call(s32[1]{0:T(128)} %bitcast.side, f32[1024,512]{1,0:T(8,128)} %convert_add_fusion.own, ...), custom_call_target="tpu_custom_call" | custom-call | bytes 1024 | tf_op jit(solution)/shard_map/pallas_call | solution.py:303
  92.2 6.5 %collective-permute-done.10 = bf16[1024,256]{1,0:T(8,128)(2,1)S(1)} collective-permute-done((bf16[1024,256]{1,0:T(8,128)(2,1)S(1)}, bf16[1024,256]{1,0:T(8,128)(2,1)S(1)}, u32[]{:S(2)}, u32[]{:S(2)}) %collective-permute-start.10) | collective-permute-done | bytes 524320 | tf_op jit(solution)/shard_map/ppermute | solution.py:36
  110.2 9.7 %collective-permute-done.14 = bf16[512,512]{1,0:T(8,128)(2,1)} collective-permute-done((bf16[512,512]{1,0:T(8,128)(2,1)S(1)}, bf16[512,512]{1,0:T(8,128)(2,1)}, u32[]{:S(2)}, u32[]{:S(2)}) %collective-permute-start.14) | collective-permute-done | bytes 524320 | tf_op jit(solution)/shard_map/ppermute | solution.py:44
  128.1 9.4 %collective-permute-done.22 = f32[1024]{0:T(1024)S(1)} collective-permute-done((f32[1024]{0:T(1024)S(1)}, f32[1024]{0:T(1024)S(1)}, u32[]{:S(2)}, u32[]{:S(2)}) %collective-permute-start.22) | collective-permute-done | bytes 4128 | tf_op jit(solution)/shard_map/ppermute | solution.py:36
  148.4 11.4 %shard_map.238 = (bf16[1024,768]{1,0:T(8,128)(2,1)}, bf16[1024,1536]{1,0:T(8,128)(2,1)}, bf16[1024,1536]{1,0:T(8,128)(2,1)}, f32[1024,1]{1,0:T(8,128)S(1)}) custom-call(bf16[512,512]{1,0:T(8,128)(2,1)S(1)} %multiply_convert_fusion.2.refs_0_, bf16[512,512]{1,0:T(8,128)(2,1)} %collective-permute-done.28.refs_1_, bf16[512,512]{1,0:T(8,128)(2,1)S(1)} %copy-done.24, ...), custom_call_target="tpu_custom_call" | custom-call | bytes 1024 | tf_op jit(solution)/shard_map/pallas_call | solution.py:377
  163.8 11.7 %shard_map.239 = (bf16[1024,768]{1,0:T(8,128)(2,1)}, bf16[1024,1536]{1,0:T(8,128)(2,1)}, bf16[1024,1536]{1,0:T(8,128)(2,1)}, f32[1024,1]{1,0:T(8,128)S(1)}) custom-call(bf16[512,512]{1,0:T(8,128)(2,1)} %collective-permute-done.18.refs_0_, ...), custom_call_target="tpu_custom_call", output_to_operand_aliasing={{0}: (17, {}), {1}: (18, {}), {2}: (19, {}), {3}: (20, {})} | custom-call | bytes 1024 | tf_op jit(solution)/shard_map/pallas_call | solution.py:377
  175.5 4.0 convolution_convert_fusion.1
  181.5 2.8 convolution_convert_fusion.2
  186.2 5.1 convolution_convert_fusion.3
  193.0 4.3 fusion.109
  197.4 3.1 add_convert_fusion.2
  204.0 4.2 convolution_convert_fusion
  221.1 2.8 collective-permute-done.37
  234.0 3.8 collective-permute-done.39
  244.3 8.1 %collective-permute-done.42 = bf16[512,512]{1,0:T(8,128)(2,1)S(1)} collective-permute-done((bf16[512,512]{1,0:T(8,128)(2,1)S(1)}, bf16[512,512]{1,0:T(8,128)(2,1)S(1)}, u32[]{:S(2)}, u32[]{:S(2)}) %collective-permute-start.42) | collective-permute-done | bytes 524320 | tf_op jit(solution)/shard_map/ppermute | solution.py:44
  253.7 3.8 collective-permute-start.52
  260.6 9.2 %collective-permute-done.52.refs_1_ = bf16[512,512]{1,0:T(8,128)(2,1)S(1)} collective-permute-done((bf16[512,512]{1,0:T(8,128)(2,1)S(1)}, bf16[512,512]{1,0:T(8,128)(2,1)S(1)}, u32[]{:S(2)}, u32[]{:S(2)}) %collective-permute-start.52) | collective-permute-done | bytes 524320 | tf_op jit(solution)/shard_map/ppermute | solution.py:77
  272.4 11.3 %collective-permute-start.58 = (bf16[512,512]{1,0:T(8,128)(2,1)S(1)}, bf16[512,512]{1,0:T(8,128)(2,1)S(1)}, u32[]{:S(2)}, u32[]{:S(2)}) collective-permute-start(bf16[512,512]{1,0:T(8,128)(2,1)S(1)} %get-tuple-element.363), channel_id=1, source_target_pairs={{0,8},{8,0},{16,24},{24,16},{1,9},{9,1},{17,25},{25,17},{2,10},{10... | collective-permute-start | bytes 1572872 | tf_op jit(solution)/shard_map/ppermute | solution.py:77
  284.4 3.0 collective-permute-start.57
  294.4 12.7 %shard_map.240 = (bf16[1024,512]{1,0:T(8,128)(2,1)}, f32[1,128]{1,0:T(1,128)S(1)}, f32[1,128]{1,0:T(1,128)S(1)}, f32[1024,1]{1,0:T(8,128)S(1)}) custom-call(s32[1]{0:T(128)} %bitcast.side, f32[1024,256]{1,0:T(8,128)} %convert_add_fusion.1.own, bf16[1024,256]{1,0:T(8,128)(2,1)S(1)} %collective-permute-done.50.from_y, f32[1024,512]{1,0:T(8,128)} %get-tuple-element.240.proj, ...), custom_call_target="tpu_custom_call" | custom-call | bytes 1024 | tf_op jit(solution)/shard_map/pallas_call | solution.py:303
  309.1 4.5 collective-permute-start.61
  316.8 7.3 %collective-permute-done.61.refs_1_ = bf16[512,512]{1,0:T(8,128)(2,1)S(1)} collective-permute-done((bf16[512,512]{1,0:T(8,128)(2,1)S(1)}, bf16[512,512]{1,0:T(8,128)(2,1)S(1)}, u32[]{:S(2)}, u32[]{:S(2)}) %collective-permute-start.61) | collective-permute-done | bytes 524320 | tf_op jit(solution)/shard_map/ppermute | solution.py:77
  328.1 7.9 %collective-permute-done.60.refs_3_ = bf16[512,512]{1,0:T(8,128)(2,1)S(1)} collective-permute-done((bf16[512,512]{1,0:T(8,128)(2,1)S(1)}, bf16[512,512]{1,0:T(8,128)(2,1)S(1)}, u32[]{:S(2)}, u32[]{:S(2)}) %collective-permute-start.60) | collective-permute-done | bytes 524320 | tf_op jit(solution)/shard_map/ppermute | solution.py:77
  340.4 2.8 multiply_convert_fusion
  343.3 3.1 fusion.40
  346.7 2.3 fusion.59
  351.6 2.5 collective-permute-start.73
  368.9 14.3 %collective-permute-done.68 = f32[1792]{0:T(1024)S(1)} collective-permute-done((f32[1792]{0:T(1024)S(1)}, f32[1792]{0:T(1024)S(1)}, u32[]{:S(2)}, u32[]{:S(2)}) %collective-permute-start.68) | collective-permute-done | bytes 7200 | tf_op jit(solution)/shard_map/ppermute | solution.py:44
  386.1 10.1 %collective-permute-done.72.refs_9_ = bf16[512,512]{1,0:T(8,128)(2,1)S(1)} collective-permute-done((bf16[512,512]{1,0:T(8,128)(2,1)S(1)}, bf16[512,512]{1,0:T(8,128)(2,1)S(1)}, u32[]{:S(2)}, u32[]{:S(2)}) %collective-permute-start.72) | collective-permute-done | bytes 524320 | tf_op jit(solution)/shard_map/ppermute | solution.py:77
  401.5 2.8 collective-permute-start.74
  404.3 7.9 %collective-permute-done.76.refs_11_ = bf16[512,512]{1,0:T(8,128)(2,1)S(1)} collective-permute-done((bf16[512,512]{1,0:T(8,128)(2,1)S(1)}, bf16[512,512]{1,0:T(8,128)(2,1)S(1)}, u32[]{:S(2)}, u32[]{:S(2)}) %collective-permute-start.76) | collective-permute-done | bytes 524320 | tf_op jit(solution)/shard_map/ppermute | solution.py:77
  418.0 3.8 all-gather.15.cloned.1.call-done
  421.8 4.0 fusion.13
  427.2 4.0 fusion.10
  434.2 2.5 broadcast_select_fusion.10
  438.2 2.4 broadcast_select_fusion.7
  446.4 5.3 collective-permute-done.79.refs_1_
  455.5 6.8 %collective-permute-done.84.refs_3_ = bf16[512,512]{1,0:T(8,128)(2,1)} collective-permute-done((bf16[512,512]{1,0:T(8,128)(2,1)}, bf16[512,512]{1,0:T(8,128)(2,1)}, u32[]{:S(2)}, u32[]{:S(2)}) %collective-permute-start.84) | collective-permute-done | bytes 524320 | tf_op jit(solution)/shard_map/ppermute | solution.py:77
  462.4 2.4 broadcast_select_fusion.8
  470.7 3.6 collective-permute-start.87
  474.4 5.3 collective-permute-done.82.refs_5_
  483.1 5.0 fusion.28
  493.1 3.3 collective-permute-start.90
  505.4 2.4 broadcast_select_fusion.4
  510.3 2.5 broadcast_select_fusion.2
  517.0 2.4 shard_map.242
  520.2 4.5 shard_map.241
  531.6 6.5 %collective-permute-start.96 = (bf16[512,512]{1,0:T(8,128)(2,1)S(1)}, bf16[512,512]{1,0:T(8,128)(2,1)S(1)}, u32[]{:S(2)}, u32[]{:S(2)}) collective-permute-start(bf16[512,512]{1,0:T(8,128)(2,1)S(1)} %get-tuple-element.331), channel_id=1, source_target_pairs={{0,8},{8,0},{16,24},{24,16},{1,9},{9,1},{17,25},{25,17},{2,10},{10... | collective-permute-start | bytes 1572872 | tf_op jit(solution)/shard_map/ppermute | solution.py:77
  539.1 7.3 %collective-permute-start.103 = (bf16[512,512]{1,0:T(8,128)(2,1)S(1)}, bf16[512,512]{1,0:T(8,128)(2,1)S(1)}, u32[]{:S(2)}, u32[]{:S(2)}) collective-permute-start(bf16[512,512]{1,0:T(8,128)(2,1)S(1)} %get-tuple-element.325), channel_id=1, source_target_pairs={{0,8},{8,0},{16,24},{24,16},{1,9},{9,1},{17,25},{25,17},{2,10},{10... | collective-permute-start | bytes 1572872 | tf_op jit(solution)/shard_map/ppermute | solution.py:77
  550.6 6.5 %collective-permute-done.103.refs_21_ = bf16[512,512]{1,0:T(8,128)(2,1)S(1)} collective-permute-done((bf16[512,512]{1,0:T(8,128)(2,1)S(1)}, bf16[512,512]{1,0:T(8,128)(2,1)S(1)}, u32[]{:S(2)}, u32[]{:S(2)}) %collective-permute-start.103) | collective-permute-done | bytes 524320 | tf_op jit(solution)/shard_map/ppermute | solution.py:77
  558.1 2.4 collective-permute-start.99
  561.5 6.5 %collective-permute-start.105 = (bf16[512,512]{1,0:T(8,128)(2,1)S(1)}, bf16[512,512]{1,0:T(8,128)(2,1)S(1)}, u32[]{:S(2)}, u32[]{:S(2)}) collective-permute-start(bf16[512,512]{1,0:T(8,128)(2,1)S(1)} %add_convert_fusion.8.refs_6_), channel_id=1, source_target_pairs={{0,8},{8,0},{16,24},{24,16},{1,9},{9,1},{17,25},{25,17},{2,10},{10... | collective-permute-start | bytes 1572872 | tf_op jit(solution)/shard_map/ppermute | solution.py:77
  568.0 5.0 collective-permute-done.99.refs_23_
  574.2 9.0 %shard_map.243 = (f32[512,3072]{1,0:T(8,128)}, f32[512,3072]{1,0:T(8,128)}) custom-call(s32[5]{0:T(128)S(1)} %stack.39.words, bf16[512,512]{1,0:T(8,128)(2,1)S(1)} %copy-done.10, bf16[512,512]{1,0:T(8,128)(2,1)S(1)} %collective-permute-done.52.refs_1_, bf16[512,512]{1,0:T(8,128)(2,1)S(1)} %copy-done.11, ...), custom_call_target="tpu_custom_call" | custom-call | bytes 1024 | tf_op jit(solution)/shard_map/pallas_call | solution.py:416
  583.4 7.1 %collective-permute-start.109 = (bf16[512,512]{1,0:T(8,128)(2,1)S(1)}, bf16[512,512]{1,0:T(8,128)(2,1)S(1)}, u32[]{:S(2)}, u32[]{:S(2)}) collective-permute-start(bf16[512,512]{1,0:T(8,128)(2,1)S(1)} %add_convert_fusion.5.refs_10_), channel_id=1, source_target_pairs={{0,8},{8,0},{16,24},{24,16},{1,9},{9,1},{17,25},{25,17},{2,10},{10... | collective-permute-start | bytes 1572872 | tf_op jit(solution)/shard_map/ppermute | solution.py:77
  590.9 7.5 %collective-permute-start.101 = (bf16[512,512]{1,0:T(8,128)(2,1)S(1)}, bf16[512,512]{1,0:T(8,128)(2,1)S(1)}, u32[]{:S(2)}, u32[]{:S(2)}) collective-permute-start(bf16[512,512]{1,0:T(8,128)(2,1)S(1)} %add_convert_fusion.10), channel_id=1, source_target_pairs={{0,8},{8,0},{16,24},{24,16},{1,9},{9,1},{17,25},{25,17},{2,10},{10... | collective-permute-start | bytes 1572872 | tf_op jit(solution)/shard_map/ppermute | solution.py:77
  605.8 7.1 %collective-permute-done.107.refs_9_ = bf16[512,512]{1,0:T(8,128)(2,1)S(1)} collective-permute-done((bf16[512,512]{1,0:T(8,128)(2,1)S(1)}, bf16[512,512]{1,0:T(8,128)(2,1)S(1)}, u32[]{:S(2)}, u32[]{:S(2)}) %collective-permute-start.107) | collective-permute-done | bytes 524320 | tf_op jit(solution)/shard_map/ppermute | solution.py:77
  613.8 5.3 shard_map.244
  (667 shorter events, 240.7 us)
Async XLA Ops:
  7.2 91.6 %all-gather.7.cloned.1.call-start = ((), (), s32[]{:S(2)}) async-start(), calls=%async_computation | async-start | bytes 1966080 | tf_op jit(solution)/shard_map/all_gather | solution.py:481
  28.3 42.7 %collective-permute-start.5 = (bf16[128,1536]{1,0:T(8,128)(2,1)}, bf16[128,1536]{1,0:T(8,128)(2,1)}, u32[]{:S(2)}, u32[]{:S(2)}) collective-permute-start(bf16[128,1536]{1,0:T(8,128)(2,1)} %pad_maximum_fusion.19), channel_id=1, source_target_pairs={{0,2},{1,3},{2,0},{3,1},{4,6},{5,7},{6,4},{7,5},{8,10},{9,11},{10,... | collective-permute-start | bytes 1179656 | tf_op jit(solution)/shard_map/ppermute | solution.py:36
  30.0 41.0 %collective-permute-start.6 = (bf16[128,1536]{1,0:T(8,128)(2,1)}, bf16[128,1536]{1,0:T(8,128)(2,1)}, u32[]{:S(2)}, u32[]{:S(2)}) collective-permute-start(bf16[128,1536]{1,0:T(8,128)(2,1)} %pad_maximum_fusion.20), channel_id=1, source_target_pairs={{0,3},{1,2},{2,1},{3,0},{4,7},{5,6},{6,5},{7,4},{8,11},{9,10},{10,... | collective-permute-start | bytes 1179656 | tf_op jit(solution)/shard_map/ppermute | solution.py:40
  31.9 88.0 %all-gather.9.cloned.1.call-start = ((), (), s32[]{:S(2)}) async-start(), calls=%async_computation.1 | async-start | bytes 1966080 | tf_op jit(solution)/shard_map/all_gather | solution.py:523
  35.6 35.4 %collective-permute-start.4 = (bf16[1024,512]{1,0:T(8,128)(2,1)}, bf16[1024,512]{1,0:T(8,128)(2,1)}, u32[]{:S(2)}, u32[]{:S(2)}) collective-permute-start(bf16[1024,512]{1,0:T(8,128)(2,1)} %add_convert_fusion.4), channel_id=1, source_target_pairs={{0,2},{1,3},{2,0},{3,1},{4,6},{5,7},{6,4},{7,5},{8,10},{9,11},{10,... | collective-permute-start | bytes 3145736 | tf_op jit(solution)/shard_map/ppermute | solution.py:36
  48.5 22.5 %collective-permute-start.8 = (f32[1024]{0:T(1024)S(1)}, f32[1024]{0:T(1024)S(1)}, u32[]{:S(2)}, u32[]{:S(2)}) collective-permute-start(f32[1024]{0:T(1024)S(1)} %add.390), channel_id=1, source_target_pairs={{0,2},{1,3},{2,0},{3,1},{4,6},{5,7},{6,4},{7,5},{8,10},{9,11},{10,... | collective-permute-start | bytes 12296 | tf_op jit(solution)/shard_map/ppermute | solution.py:36
  71.0 76.3 %all-gather.11.cloned.1.call-start = ((), (), s32[]{:S(2)}) async-start(), calls=%async_computation.2 | async-start | bytes 1966080 | tf_op jit(solution)/shard_map/all_gather | solution.py:523
  88.3 21.9 %collective-permute-start.16 = (bf16[512,1536]{1,0:T(8,128)(2,1)}, bf16[512,1536]{1,0:T(8,128)(2,1)}, u32[]{:S(2)}, u32[]{:S(2)}) collective-permute-start(bf16[512,1536]{1,0:T(8,128)(2,1)} %pad_maximum_fusion), channel_id=1, source_target_pairs={{0,1},{1,0},{2,3},{3,2},{4,5},{5,4},{6,7},{7,6},{8,9},{9,8},{10,11... | collective-permute-start | bytes 4718600 | tf_op jit(solution)/shard_map/ppermute | solution.py:32
  88.3 21.8 %collective-permute-start.17 = (bf16[768,512]{1,0:T(8,128)(2,1)}, bf16[768,512]{1,0:T(8,128)(2,1)}, u32[]{:S(2)}, u32[]{:S(2)}) collective-permute-start(bf16[768,512]{1,0:T(8,128)(2,1)} %get-tuple-element.372), channel_id=1, source_target_pairs={{0,1},{1,0},{2,3},{3,2},{4,5},{5,4},{6,7},{7,6},{8,9},{9,8},{10,11... | collective-permute-start | bytes 2359304 | tf_op jit(solution)/shard_map/ppermute | solution.py:32
  100.9 320.9 %all-gather.15.cloned.1.call-start = ((), (), s32[]{:S(2)}) async-start(), calls=%async_computation.4 | async-start | bytes 15728640 | tf_op jit(solution)/shard_map/all_gather | solution.py:647
  101.2 37.0 %collective-permute-start.23 = (bf16[512,512]{1,0:T(8,128)(2,1)}, bf16[512,512]{1,0:T(8,128)(2,1)}, u32[]{:S(2)}, u32[]{:S(2)}) collective-permute-start(bf16[512,512]{1,0:T(8,128)(2,1)} %collective-permute-done.11.refs_10_), channel_id=1, source_target_pairs={{0,1},{1,0},{2,3},{3,2},{4,5},{5,4},{6,7},{7,6},{8,9},{9,8},{10,11... | collective-permute-start | bytes 1572872 | tf_op jit(solution)/shard_map/ppermute | solution.py:32
  110.1 28.1 %collective-permute-start.24 = (bf16[512,512]{1,0:T(8,128)(2,1)}, bf16[512,512]{1,0:T(8,128)(2,1)}, u32[]{:S(2)}, u32[]{:S(2)}) collective-permute-start(bf16[512,512]{1,0:T(8,128)(2,1)} %collective-permute-done.12.refs_10_), channel_id=1, source_target_pairs={{0,1},{1,0},{2,3},{3,2},{4,5},{5,4},{6,7},{7,6},{8,9},{9,8},{10,11... | collective-permute-start | bytes 1572872 | tf_op jit(solution)/shard_map/ppermute | solution.py:32
  138.8 21.1 %collective-permute-start.27 = (bf16[512,512]{1,0:T(8,128)(2,1)}, bf16[512,512]{1,0:T(8,128)(2,1)}, u32[]{:S(2)}, u32[]{:S(2)}) collective-permute-start(bf16[512,512]{1,0:T(8,128)(2,1)} %collective-permute-done.18.refs_0_), channel_id=1, source_target_pairs={{0,1},{1,0},{2,3},{3,2},{4,5},{5,4},{6,7},{7,6},{8,9},{9,8},{10,11... | collective-permute-start | bytes 1572872 | tf_op jit(solution)/shard_map/ppermute | solution.py:32
  141.3 18.6 %collective-permute-start.25 = (bf16[256,512]{1,0:T(8,128)(2,1)}, bf16[256,512]{1,0:T(8,128)(2,1)}, u32[]{:S(2)}, u32[]{:S(2)}) collective-permute-start(bf16[256,512]{1,0:T(8,128)(2,1)} %slice.164), channel_id=1, source_target_pairs={{0,2},{1,3},{2,0},{3,1},{4,6},{5,7},{6,4},{7,5},{8,10},{9,11},{10,... | collective-permute-start | bytes 786440 | tf_op jit(solution)/shard_map/ppermute | solution.py:36
  143.0 16.8 %collective-permute-start.26 = (bf16[256,512]{1,0:T(8,128)(2,1)}, bf16[256,512]{1,0:T(8,128)(2,1)}, u32[]{:S(2)}, u32[]{:S(2)}) collective-permute-start(bf16[256,512]{1,0:T(8,128)(2,1)} %slice.165), channel_id=1, source_target_pairs={{0,4},{4,0},{1,5},{5,1},{2,6},{6,2},{3,7},{7,3},{8,12},{12,8},{9,1... | collective-permute-start | bytes 786440 | tf_op jit(solution)/shard_map/ppermute | solution.py:44
  185.0 33.2 %collective-permute-start.35 = (bf16[512,512]{1,0:T(8,128)(2,1)}, bf16[512,512]{1,0:T(8,128)(2,1)}, u32[]{:S(2)}, u32[]{:S(2)}) collective-permute-start(bf16[512,512]{1,0:T(8,128)(2,1)} %get-tuple-element.209), channel_id=1, source_target_pairs={{0,8},{8,0},{16,24},{24,16},{1,9},{9,1},{17,25},{25,17},{2,10},{10... | collective-permute-start | bytes 1572872 | tf_op jit(solution)/shard_map/ppermute | solution.py:77
  191.4 36.3 %collective-permute-start.41 = (bf16[512,512]{1,0:T(8,128)(2,1)}, bf16[512,512]{1,0:T(8,128)(2,1)}, u32[]{:S(2)}, u32[]{:S(2)}) collective-permute-start(bf16[512,512]{1,0:T(8,128)(2,1)} %get-tuple-element.218), channel_id=1, source_target_pairs={{0,8},{8,0},{16,24},{24,16},{1,9},{9,1},{17,25},{25,17},{2,10},{10... | collective-permute-start | bytes 1572872 | tf_op jit(solution)/shard_map/ppermute | solution.py:77
  220.2 23.1 %collective-permute-start.44 = (bf16[512,512]{1,0:T(8,128)(2,1)S(1)}, bf16[512,512]{1,0:T(8,128)(2,1)S(1)}, u32[]{:S(2)}, u32[]{:S(2)}) collective-permute-start(bf16[512,512]{1,0:T(8,128)(2,1)S(1)} %add_convert_fusion.57), channel_id=1, source_target_pairs={{8,16},{16,8},{9,17},{17,9},{10,18},{18,10},{11,19},{19,11},{12,20... | collective-permute-start | bytes 1572872 | tf_op jit(solution)/shard_map/ppermute | solution.py:72
  223.9 34.1 %collective-permute-start.51 = (bf16[512,1536]{1,0:T(8,128)(2,1)S(1)}, bf16[512,1536]{1,0:T(8,128)(2,1)S(1)}, u32[]{:S(2)}, u32[]{:S(2)}) collective-permute-start(bf16[512,1536]{1,0:T(8,128)(2,1)S(1)} %copy-done.153), channel_id=1, source_target_pairs={{0,1},{1,0},{2,3},{3,2},{4,5},{5,4},{6,7},{7,6},{8,9},{9,8},{10,11... | collective-permute-start | bytes 4718600 | tf_op jit(solution)/shard_map/ppermute | solution.py:32
  226.2 17.0 %collective-permute-start.43 = (bf16[512,512]{1,0:T(8,128)(2,1)S(1)}, bf16[512,512]{1,0:T(8,128)(2,1)S(1)}, u32[]{:S(2)}, u32[]{:S(2)}) collective-permute-start(bf16[512,512]{1,0:T(8,128)(2,1)S(1)} %copy-done.91), channel_id=1, source_target_pairs={{0,8},{8,0},{16,24},{24,16},{1,9},{9,1},{17,25},{25,17},{2,10},{10... | collective-permute-start | bytes 1572872 | tf_op jit(solution)/shard_map/ppermute | solution.py:77
  237.8 21.0 %collective-permute-start.48 = (bf16[512,512]{1,0:T(8,128)(2,1)S(1)}, bf16[512,512]{1,0:T(8,128)(2,1)S(1)}, u32[]{:S(2)}, u32[]{:S(2)}) collective-permute-start(bf16[512,512]{1,0:T(8,128)(2,1)S(1)} %get-tuple-element.227), channel_id=1, source_target_pairs={{0,8},{8,0},{16,24},{24,16},{1,9},{9,1},{17,25},{25,17},{2,10},{10... | collective-permute-start | bytes 1572872 | tf_op jit(solution)/shard_map/ppermute | solution.py:77
  258.8 32.7 %collective-permute-start.46 = (bf16[1024,256]{1,0:T(8,128)(2,1)S(1)}, bf16[1024,256]{1,0:T(8,128)(2,1)S(1)}, u32[]{:S(2)}, u32[]{:S(2)}) collective-permute-start(bf16[1024,256]{1,0:T(8,128)(2,1)S(1)} %convolution_convert_fusion.9), channel_id=1, source_target_pairs={{0,1},{1,0},{2,3},{3,2},{4,5},{5,4},{6,7},{7,6},{8,9},{9,8},{10,11... | collective-permute-start | bytes 1572872 | tf_op jit(solution)/shard_map/ppermute | solution.py:32
  271.0 23.4 %collective-permute-start.50 = (bf16[1024,256]{1,0:T(8,128)(2,1)S(1)}, bf16[1024,256]{1,0:T(8,128)(2,1)S(1)}, u32[]{:S(2)}, u32[]{:S(2)}) collective-permute-start(bf16[1024,256]{1,0:T(8,128)(2,1)S(1)} %add_convert_fusion.50), channel_id=1, source_target_pairs={{0,2},{1,3},{2,0},{3,1},{4,6},{5,7},{6,4},{7,5},{8,10},{9,11},{10,... | collective-permute-start | bytes 1572872 | tf_op jit(solution)/shard_map/ppermute | solution.py:36
  272.4 34.6 %collective-permute-start.58 = (bf16[512,512]{1,0:T(8,128)(2,1)S(1)}, bf16[512,512]{1,0:T(8,128)(2,1)S(1)}, u32[]{:S(2)}, u32[]{:S(2)}) collective-permute-start(bf16[512,512]{1,0:T(8,128)(2,1)S(1)} %get-tuple-element.363), channel_id=1, source_target_pairs={{0,8},{8,0},{16,24},{24,16},{1,9},{9,1},{17,25},{25,17},{2,10},{10... | collective-permute-start | bytes 1572872 | tf_op jit(solution)/shard_map/ppermute | solution.py:77
  283.7 24.3 %collective-permute-start.59 = (bf16[512,512]{1,0:T(8,128)(2,1)S(1)}, bf16[512,512]{1,0:T(8,128)(2,1)S(1)}, u32[]{:S(2)}, u32[]{:S(2)}) collective-permute-start(bf16[512,512]{1,0:T(8,128)(2,1)S(1)} %add_convert_fusion.52), channel_id=1, source_target_pairs={{8,16},{16,8},{9,17},{17,9},{10,18},{18,10},{11,19},{19,11},{12,20... | collective-permute-start | bytes 1572872 | tf_op jit(solution)/shard_map/ppermute | solution.py:72
  284.4 29.1 %collective-permute-start.57 = (bf16[512,512]{1,0:T(8,128)(2,1)S(1)}, bf16[512,512]{1,0:T(8,128)(2,1)S(1)}, u32[]{:S(2)}, u32[]{:S(2)}) collective-permute-start(bf16[512,512]{1,0:T(8,128)(2,1)S(1)} %get-tuple-element.361), channel_id=1, source_target_pairs={{0,8},{8,0},{16,24},{24,16},{1,9},{9,1},{17,25},{25,17},{2,10},{10... | collective-permute-start | bytes 1572872 | tf_op jit(solution)/shard_map/ppermute | solution.py:77
  291.6 24.2 %collective-permute-start.56 = (bf16[512,512]{1,0:T(8,128)(2,1)S(1)}, bf16[512,512]{1,0:T(8,128)(2,1)S(1)}, u32[]{:S(2)}, u32[]{:S(2)}) collective-permute-start(bf16[512,512]{1,0:T(8,128)(2,1)S(1)} %add_convert_fusion.49), channel_id=1, source_target_pairs={{8,16},{16,8},{9,17},{17,9},{10,18},{18,10},{11,19},{19,11},{12,20... | collective-permute-start | bytes 1572872 | tf_op jit(solution)/shard_map/ppermute | solution.py:72
  307.2 19.7 %collective-permute-start.62 = (bf16[512,512]{1,0:T(8,128)(2,1)S(1)}, bf16[512,512]{1,0:T(8,128)(2,1)S(1)}, u32[]{:S(2)}, u32[]{:S(2)}) collective-permute-start(bf16[512,512]{1,0:T(8,128)(2,1)S(1)} %add_convert_fusion.46), channel_id=1, source_target_pairs={{8,16},{16,8},{9,17},{17,9},{10,18},{18,10},{11,19},{19,11},{12,20... | collective-permute-start | bytes 1572872 | tf_op jit(solution)/shard_map/ppermute | solution.py:72
  313.7 23.2 %collective-permute-start.63 = (bf16[512,512]{1,0:T(8,128)(2,1)S(1)}, bf16[512,512]{1,0:T(8,128)(2,1)S(1)}, u32[]{:S(2)}, u32[]{:S(2)}) collective-permute-start(bf16[512,512]{1,0:T(8,128)(2,1)S(1)} %add_convert_fusion.44), channel_id=1, source_target_pairs={{8,16},{16,8},{9,17},{17,9},{10,18},{18,10},{11,19},{19,11},{12,20... | collective-permute-start | bytes 1572872 | tf_op jit(solution)/shard_map/ppermute | solution.py:72
  314.4 23.7 %collective-permute-start.54 = (bf16[1024,512]{1,0:T(8,128)(2,1)S(1)}, bf16[1024,512]{1,0:T(8,128)(2,1)S(1)}, u32[]{:S(2)}, u32[]{:S(2)}) collective-permute-start(bf16[1024,512]{1,0:T(8,128)(2,1)S(1)} %copy-done.116), channel_id=1, source_target_pairs={{0,2},{1,3},{2,0},{3,1},{4,6},{5,7},{6,4},{7,5},{8,10},{9,11},{10,... | collective-permute-start | bytes 3145736 | tf_op jit(solution)/shard_map/ppermute | solution.py:36
  315.8 22.3 %collective-permute-start.55 = (bf16[1024,512]{1,0:T(8,128)(2,1)S(1)}, bf16[1024,512]{1,0:T(8,128)(2,1)S(1)}, u32[]{:S(2)}, u32[]{:S(2)}) collective-permute-start(bf16[1024,512]{1,0:T(8,128)(2,1)S(1)} %copy-done.116), channel_id=1, source_target_pairs={{0,1},{1,0},{2,3},{3,2},{4,5},{5,4},{6,7},{7,6},{8,9},{9,8},{10,11... | collective-permute-start | bytes 3145736 | tf_op jit(solution)/shard_map/ppermute | solution.py:32
  340.1 143.0 %all-gather.13.cloned.1.call-start = ((), (), s32[]{:S(2)}) async-start(), calls=%async_computation.3 | async-start | bytes 7864320 | tf_op jit(solution)/shard_map/all_gather | solution.py:663
  349.0 16.9 %collective-permute-start.69 = (bf16[512,512]{1,0:T(8,128)(2,1)S(1)}, bf16[512,512]{1,0:T(8,128)(2,1)S(1)}, u32[]{:S(2)}, u32[]{:S(2)}) collective-permute-start(bf16[512,512]{1,0:T(8,128)(2,1)S(1)} %copy-done.144), channel_id=1, source_target_pairs={{0,8},{8,0},{16,24},{24,16},{1,9},{9,1},{17,25},{25,17},{2,10},{10... | collective-permute-start | bytes 1572872 | tf_op jit(solution)/shard_map/ppermute | solution.py:77
  350.9 16.3 %collective-permute-start.70 = (bf16[512,512]{1,0:T(8,128)(2,1)S(1)}, bf16[512,512]{1,0:T(8,128)(2,1)S(1)}, u32[]{:S(2)}, u32[]{:S(2)}) collective-permute-start(bf16[512,512]{1,0:T(8,128)(2,1)S(1)} %copy-done.95), channel_id=1, source_target_pairs={{8,16},{16,8},{9,17},{17,9},{10,18},{18,10},{11,19},{19,11},{12,20... | collective-permute-start | bytes 1572872 | tf_op jit(solution)/shard_map/ppermute | solution.py:72
  351.6 33.7 %collective-permute-start.73 = (bf16[512,512]{1,0:T(8,128)(2,1)S(1)}, bf16[512,512]{1,0:T(8,128)(2,1)S(1)}, u32[]{:S(2)}, u32[]{:S(2)}) collective-permute-start(bf16[512,512]{1,0:T(8,128)(2,1)S(1)} %copy-done.143), channel_id=1, source_target_pairs={{0,8},{8,0},{16,24},{24,16},{1,9},{9,1},{17,25},{25,17},{2,10},{10... | collective-permute-start | bytes 1572872 | tf_op jit(solution)/shard_map/ppermute | solution.py:77
  357.9 25.6 %collective-permute-start.67 = (bf16[1024,512]{1,0:T(8,128)(2,1)S(1)}, bf16[1024,512]{1,0:T(8,128)(2,1)S(1)}, u32[]{:S(2)}, u32[]{:S(2)}) collective-permute-start(bf16[1024,512]{1,0:T(8,128)(2,1)S(1)} %add_convert_fusion.1), channel_id=1, source_target_pairs={{0,4},{4,0},{1,5},{5,1},{2,6},{6,2},{3,7},{7,3},{8,12},{12,8},{9,1... | collective-permute-start | bytes 3145736 | tf_op jit(solution)/shard_map/ppermute | solution.py:44
  365.1 31.1 %collective-permute-start.75 = (bf16[512,512]{1,0:T(8,128)(2,1)S(1)}, bf16[512,512]{1,0:T(8,128)(2,1)S(1)}, u32[]{:S(2)}, u32[]{:S(2)}) collective-permute-start(bf16[512,512]{1,0:T(8,128)(2,1)S(1)} %copy-done.92), channel_id=1, source_target_pairs={{8,16},{16,8},{9,17},{17,9},{10,18},{18,10},{11,19},{19,11},{12,20... | collective-permute-start | bytes 1572872 | tf_op jit(solution)/shard_map/ppermute | solution.py:72
  365.9 17.3 %collective-permute-start.68 = (f32[1792]{0:T(1024)S(1)}, f32[1792]{0:T(1024)S(1)}, u32[]{:S(2)}, u32[]{:S(2)}) collective-permute-start(f32[1792]{0:T(1024)S(1)} %pad_maximum_fusion.38), channel_id=1, source_target_pairs={{0,4},{4,0},{1,5},{5,1},{2,6},{6,2},{3,7},{7,3},{8,12},{12,8},{9,1... | collective-permute-start | bytes 21512 | tf_op jit(solution)/shard_map/ppermute | solution.py:44
  367.2 33.1 %collective-permute-start.71 = (bf16[512,512]{1,0:T(8,128)(2,1)S(1)}, bf16[512,512]{1,0:T(8,128)(2,1)S(1)}, u32[]{:S(2)}, u32[]{:S(2)}) collective-permute-start(bf16[512,512]{1,0:T(8,128)(2,1)S(1)} %add_convert_fusion.39), channel_id=1, source_target_pairs={{8,16},{16,8},{9,17},{17,9},{10,18},{18,10},{11,19},{19,11},{12,20... | collective-permute-start | bytes 1572872 | tf_op jit(solution)/shard_map/ppermute | solution.py:72
  385.4 29.3 %collective-permute-start.80 = (bf16[512,512]{1,0:T(8,128)(2,1)S(1)}, bf16[512,512]{1,0:T(8,128)(2,1)S(1)}, u32[]{:S(2)}, u32[]{:S(2)}) collective-permute-start(bf16[512,512]{1,0:T(8,128)(2,1)S(1)} %add_convert_fusion.36), channel_id=1, source_target_pairs={{8,16},{16,8},{9,17},{17,9},{10,18},{18,10},{11,19},{19,11},{12,20... | collective-permute-start | bytes 1572872 | tf_op jit(solution)/shard_map/ppermute | solution.py:72
  398.8 35.4 %collective-permute-start.78 = (bf16[512,512]{1,0:T(8,128)(2,1)}, bf16[512,512]{1,0:T(8,128)(2,1)}, u32[]{:S(2)}, u32[]{:S(2)}) collective-permute-start(bf16[512,512]{1,0:T(8,128)(2,1)} %add_convert_fusion.35), channel_id=1, source_target_pairs={{8,16},{16,8},{9,17},{17,9},{10,18},{18,10},{11,19},{19,11},{12,20... | collective-permute-start | bytes 1572872 | tf_op jit(solution)/shard_map/ppermute | solution.py:72
  401.5 30.6 %collective-permute-start.74 = (bf16[512,512]{1,0:T(8,128)(2,1)}, bf16[512,512]{1,0:T(8,128)(2,1)S(1)}, u32[]{:S(2)}, u32[]{:S(2)}) collective-permute-start(bf16[512,512]{1,0:T(8,128)(2,1)} %get-tuple-element.349), channel_id=1, source_target_pairs={{0,8},{8,0},{16,24},{24,16},{1,9},{9,1},{17,25},{25,17},{2,10},{10... | collective-permute-start | bytes 1572872 | tf_op jit(solution)/shard_map/ppermute | solution.py:77
  413.1 25.1 %collective-permute-start.83 = (bf16[512,512]{1,0:T(8,128)(2,1)}, bf16[512,512]{1,0:T(8,128)(2,1)}, u32[]{:S(2)}, u32[]{:S(2)}) collective-permute-start(bf16[512,512]{1,0:T(8,128)(2,1)} %add_convert_fusion.33), channel_id=1, source_target_pairs={{8,16},{16,8},{9,17},{17,9},{10,18},{18,10},{11,19},{19,11},{12,20... | collective-permute-start | bytes 1572872 | tf_op jit(solution)/shard_map/ppermute | solution.py:72
  416.0 17.3 %collective-permute-start.81 = (bf16[512,512]{1,0:T(8,128)(2,1)}, bf16[512,512]{1,0:T(8,128)(2,1)S(1)}, u32[]{:S(2)}, u32[]{:S(2)}) collective-permute-start(bf16[512,512]{1,0:T(8,128)(2,1)} %get-tuple-element.343), channel_id=1, source_target_pairs={{0,8},{8,0},{16,24},{24,16},{1,9},{9,1},{17,25},{25,17},{2,10},{10... | collective-permute-start | bytes 1572872 | tf_op jit(solution)/shard_map/ppermute | solution.py:77
  440.6 21.7 %collective-permute-start.84 = (bf16[512,512]{1,0:T(8,128)(2,1)}, bf16[512,512]{1,0:T(8,128)(2,1)}, u32[]{:S(2)}, u32[]{:S(2)}) collective-permute-start(bf16[512,512]{1,0:T(8,128)(2,1)} %get-tuple-element.339), channel_id=1, source_target_pairs={{0,8},{8,0},{16,24},{24,16},{1,9},{9,1},{17,25},{25,17},{2,10},{10... | collective-permute-start | bytes 1572872 | tf_op jit(solution)/shard_map/ppermute | solution.py:77
  441.1 21.3 %collective-permute-start.77 = (bf16[512,512]{1,0:T(8,128)(2,1)}, bf16[512,512]{1,0:T(8,128)(2,1)}, u32[]{:S(2)}, u32[]{:S(2)}) collective-permute-start(bf16[512,512]{1,0:T(8,128)(2,1)} %add_convert_fusion.32), channel_id=1, source_target_pairs={{8,16},{16,8},{9,17},{17,9},{10,18},{18,10},{11,19},{19,11},{12,20... | collective-permute-start | bytes 1572872 | tf_op jit(solution)/shard_map/ppermute | solution.py:72
  445.6 23.9 %collective-permute-start.86 = (bf16[512,512]{1,0:T(8,128)(2,1)}, bf16[512,512]{1,0:T(8,128)(2,1)S(1)}, u32[]{:S(2)}, u32[]{:S(2)}) collective-permute-start(bf16[512,512]{1,0:T(8,128)(2,1)} %add_convert_fusion.28), channel_id=1, source_target_pairs={{8,16},{16,8},{9,17},{17,9},{10,18},{18,10},{11,19},{19,11},{12,20... | collective-permute-start | bytes 1572872 | tf_op jit(solution)/shard_map/ppermute | solution.py:72
  453.9 36.9 %collective-permute-start.89 = (bf16[512,512]{1,0:T(8,128)(2,1)}, bf16[512,512]{1,0:T(8,128)(2,1)}, u32[]{:S(2)}, u32[]{:S(2)}) collective-permute-start(bf16[512,512]{1,0:T(8,128)(2,1)} %add_convert_fusion.27), channel_id=1, source_target_pairs={{8,16},{16,8},{9,17},{17,9},{10,18},{18,10},{11,19},{19,11},{12,20... | collective-permute-start | bytes 1572872 | tf_op jit(solution)/shard_map/ppermute | solution.py:72
  468.1 37.3 %collective-permute-start.92 = (bf16[512,512]{1,0:T(8,128)(2,1)}, bf16[512,512]{1,0:T(8,128)(2,1)}, u32[]{:S(2)}, u32[]{:S(2)}) collective-permute-start(bf16[512,512]{1,0:T(8,128)(2,1)} %add_convert_fusion.25), channel_id=1, source_target_pairs={{8,16},{16,8},{9,17},{17,9},{10,18},{18,10},{11,19},{19,11},{12,20... | collective-permute-start | bytes 1572872 | tf_op jit(solution)/shard_map/ppermute | solution.py:72
  470.7 32.5 %collective-permute-start.87 = (bf16[512,512]{1,0:T(8,128)(2,1)}, bf16[512,512]{1,0:T(8,128)(2,1)}, u32[]{:S(2)}, u32[]{:S(2)}) collective-permute-start(bf16[512,512]{1,0:T(8,128)(2,1)} %get-tuple-element.337), channel_id=1, source_target_pairs={{0,8},{8,0},{16,24},{24,16},{1,9},{9,1},{17,25},{25,17},{2,10},{10... | collective-permute-start | bytes 1572872 | tf_op jit(solution)/shard_map/ppermute | solution.py:77
  481.4 28.9 %collective-permute-start.97 = (bf16[512,512]{1,0:T(8,128)(2,1)}, bf16[512,512]{1,0:T(8,128)(2,1)}, u32[]{:S(2)}, u32[]{:S(2)}) collective-permute-start(bf16[512,512]{1,0:T(8,128)(2,1)} %add_convert_fusion.24), channel_id=1, source_target_pairs={{8,16},{16,8},{9,17},{17,9},{10,18},{18,10},{11,19},{19,11},{12,20... | collective-permute-start | bytes 1572872 | tf_op jit(solution)/shard_map/ppermute | solution.py:72
  507.8 19.1 %collective-permute-start.93 = (bf16[512,512]{1,0:T(8,128)(2,1)}, bf16[512,512]{1,0:T(8,128)(2,1)}, u32[]{:S(2)}, u32[]{:S(2)}) collective-permute-start(bf16[512,512]{1,0:T(8,128)(2,1)} %get-tuple-element.333), channel_id=1, source_target_pairs={{0,8},{8,0},{16,24},{24,16},{1,9},{9,1},{17,25},{25,17},{2,10},{10... | collective-permute-start | bytes 1572872 | tf_op jit(solution)/shard_map/ppermute | solution.py:77
  508.7 18.1 %collective-permute-start.88 = (bf16[512,512]{1,0:T(8,128)(2,1)}, bf16[512,512]{1,0:T(8,128)(2,1)}, u32[]{:S(2)}, u32[]{:S(2)}) collective-permute-start(bf16[512,512]{1,0:T(8,128)(2,1)} %add_convert_fusion.21), channel_id=1, source_target_pairs={{0,4},{4,0},{1,5},{5,1},{2,6},{6,2},{3,7},{7,3},{8,12},{12,8},{9,1... | collective-permute-start | bytes 1572872 | tf_op jit(solution)/shard_map/ppermute | solution.py:44
  512.8 16.6 %collective-permute-start.98 = (bf16[512,512]{1,0:T(8,128)(2,1)}, bf16[512,512]{1,0:T(8,128)(2,1)}, u32[]{:S(2)}, u32[]{:S(2)}) collective-permute-start(bf16[512,512]{1,0:T(8,128)(2,1)} %get-tuple-element.329), channel_id=1, source_target_pairs={{0,8},{8,0},{16,24},{24,16},{1,9},{9,1},{17,25},{25,17},{2,10},{10... | collective-permute-start | bytes 1572872 | tf_op jit(solution)/shard_map/ppermute | solution.py:77
  528.1 29.0 %collective-permute-start.94 = (bf16[512,512]{1,0:T(8,128)(2,1)S(1)}, bf16[512,512]{1,0:T(8,128)(2,1)S(1)}, u32[]{:S(2)}, u32[]{:S(2)}) collective-permute-start(bf16[512,512]{1,0:T(8,128)(2,1)S(1)} %add_convert_fusion.17), channel_id=1, source_target_pairs={{8,16},{16,8},{9,17},{17,9},{10,18},{18,10},{11,19},{19,11},{12,20... | collective-permute-start | bytes 1572872 | tf_op jit(solution)/shard_map/ppermute | solution.py:72
  531.6 18.1 %collective-permute-start.96 = (bf16[512,512]{1,0:T(8,128)(2,1)S(1)}, bf16[512,512]{1,0:T(8,128)(2,1)S(1)}, u32[]{:S(2)}, u32[]{:S(2)}) collective-permute-start(bf16[512,512]{1,0:T(8,128)(2,1)S(1)} %get-tuple-element.331), channel_id=1, source_target_pairs={{0,8},{8,0},{16,24},{24,16},{1,9},{9,1},{17,25},{25,17},{2,10},{10... | collective-permute-start | bytes 1572872 | tf_op jit(solution)/shard_map/ppermute | solution.py:77
  539.1 18.0 %collective-permute-start.103 = (bf16[512,512]{1,0:T(8,128)(2,1)S(1)}, bf16[512,512]{1,0:T(8,128)(2,1)S(1)}, u32[]{:S(2)}, u32[]{:S(2)}) collective-permute-start(bf16[512,512]{1,0:T(8,128)(2,1)S(1)} %get-tuple-element.325), channel_id=1, source_target_pairs={{0,8},{8,0},{16,24},{24,16},{1,9},{9,1},{17,25},{25,17},{2,10},{10... | collective-permute-start | bytes 1572872 | tf_op jit(solution)/shard_map/ppermute | solution.py:77
  549.9 40.6 %collective-permute-start.106 = (bf16[512,512]{1,0:T(8,128)(2,1)S(1)}, bf16[512,512]{1,0:T(8,128)(2,1)S(1)}, u32[]{:S(2)}, u32[]{:S(2)}) collective-permute-start(bf16[512,512]{1,0:T(8,128)(2,1)S(1)} %add_convert_fusion.12), channel_id=1, source_target_pairs={{8,16},{16,8},{9,17},{17,9},{10,18},{18,10},{11,19},{19,11},{12,20... | collective-permute-start | bytes 1572872 | tf_op jit(solution)/shard_map/ppermute | solution.py:72
  560.7 22.5 %collective-permute-start.108 = (bf16[512,512]{1,0:T(8,128)(2,1)S(1)}, bf16[512,512]{1,0:T(8,128)(2,1)S(1)}, u32[]{:S(2)}, u32[]{:S(2)}) collective-permute-start(bf16[512,512]{1,0:T(8,128)(2,1)S(1)} %add_convert_fusion.6), channel_id=1, source_target_pairs={{8,16},{16,8},{9,17},{17,9},{10,18},{18,10},{11,19},{19,11},{12,20... | collective-permute-start | bytes 1572872 | tf_op jit(solution)/shard_map/ppermute | solution.py:72
  561.5 44.3 %collective-permute-start.105 = (bf16[512,512]{1,0:T(8,128)(2,1)S(1)}, bf16[512,512]{1,0:T(8,128)(2,1)S(1)}, u32[]{:S(2)}, u32[]{:S(2)}) collective-permute-start(bf16[512,512]{1,0:T(8,128)(2,1)S(1)} %add_convert_fusion.8.refs_6_), channel_id=1, source_target_pairs={{0,8},{8,0},{16,24},{24,16},{1,9},{9,1},{17,25},{25,17},{2,10},{10... | collective-permute-start | bytes 1572872 | tf_op jit(solution)/shard_map/ppermute | solution.py:77
  573.2 17.6 %collective-permute-start.100 = (bf16[512,512]{1,0:T(8,128)(2,1)S(1)}, bf16[512,512]{1,0:T(8,128)(2,1)S(1)}, u32[]{:S(2)}, u32[]{:S(2)}) collective-permute-start(bf16[512,512]{1,0:T(8,128)(2,1)S(1)} %add_convert_fusion.11), channel_id=1, source_target_pairs={{8,16},{16,8},{9,17},{17,9},{10,18},{18,10},{11,19},{19,11},{12,20... | collective-permute-start | bytes 1572872 | tf_op jit(solution)/shard_map/ppermute | solution.py:72
  583.4 22.5 %collective-permute-start.109 = (bf16[512,512]{1,0:T(8,128)(2,1)S(1)}, bf16[512,512]{1,0:T(8,128)(2,1)S(1)}, u32[]{:S(2)}, u32[]{:S(2)}) collective-permute-start(bf16[512,512]{1,0:T(8,128)(2,1)S(1)} %add_convert_fusion.5.refs_10_), channel_id=1, source_target_pairs={{0,8},{8,0},{16,24},{24,16},{1,9},{9,1},{17,25},{25,17},{2,10},{10... | collective-permute-start | bytes 1572872 | tf_op jit(solution)/shard_map/ppermute | solution.py:77
  590.6 22.3 %collective-permute-start.107 = (bf16[512,512]{1,0:T(8,128)(2,1)S(1)}, bf16[512,512]{1,0:T(8,128)(2,1)S(1)}, u32[]{:S(2)}, u32[]{:S(2)}) collective-permute-start(bf16[512,512]{1,0:T(8,128)(2,1)S(1)} %add_convert_fusion.7.refs_8_), channel_id=1, source_target_pairs={{0,8},{8,0},{16,24},{24,16},{1,9},{9,1},{17,25},{25,17},{2,10},{10... | collective-permute-start | bytes 1572872 | tf_op jit(solution)/shard_map/ppermute | solution.py:77
  590.9 28.2 %collective-permute-start.101 = (bf16[512,512]{1,0:T(8,128)(2,1)S(1)}, bf16[512,512]{1,0:T(8,128)(2,1)S(1)}, u32[]{:S(2)}, u32[]{:S(2)}) collective-permute-start(bf16[512,512]{1,0:T(8,128)(2,1)S(1)} %add_convert_fusion.10), channel_id=1, source_target_pairs={{0,8},{8,0},{16,24},{24,16},{1,9},{9,1},{17,25},{25,17},{2,10},{10... | collective-permute-start | bytes 1572872 | tf_op jit(solution)/shard_map/ppermute | solution.py:77
  (205 other events, 2024.8 us)
Sparse Core Ops, SparseCore 0:
  32.1 38.5 all-gather.6
  72.2 37.4 all-gather.8
  111.3 35.9 all-gather.10
  340.2 81.5 all-gather.14
  423.3 46.3 all-gather.12

commit v2 on v1

--- a/solution.py
+++ b/solution.py
@@ -640,8 +640,9 @@
     )(side_word, head_own, head_y, projected, q_low, k_low, v_low, log_totals, *tables)
     proj_y, proj_core = swap_y(proj_low), swap_core(proj_low)
 
+    line.add("qkv", low(contract_rows(after(normed, proj_low), proj_low)), 1)
     marker = proj_low
-    for _ in range(4):
+    for _ in range(5):
         marker = line.send(marker)
     proj_y, proj_core = after((proj_y, proj_core), marker)
     pairs = lax.all_gather(after(pair_scaled, proj_y), "tc")
@@ -653,7 +654,7 @@
     small = jnp.concatenate([inner_attn[:, 0], q_gain_part[0], k_gain_part[0]])
     small = width_total(after(small, normed_part))
     small = jnp.concatenate([small, mlp_gain_part])
-    for part in projs:
+    for part in projs[1:]:
         line.add("qkv", low(contract_rows(after(normed, normed_part), part)), 1)
     normed_x, small_x = after(
         (swap_x(normed_part), swap_x(small)), line.send((small, line.waiting()))
@@ -670,8 +671,7 @@
     )
 
     marker = line.send((token_grad, line.waiting()), False)
-    for _ in range(2):
-        marker = line.send(marker, False)
+    marker = line.send(marker, False)
     pairs = after(pairs, marker)
     for k in (2, 3):
         block = lax.dynamic_index_in_dim(pairs, around[k], 0, keepdims=False)

time: 636 us -> 648 us (1.019)
  waiting for transfers between devices: 172 us -> 186 us
    all_gather x1, waiting for transfers between devices: 3.8 us -> 18.4 us  [on_device(): pairs = lax.all_gather(after(pair_scaled, proj_y), 'tc')]
  transfers between devices with their start and end apart: 115 -> 115, of which waited for: 31 -> 31; matrix products, arithmetic and copies ran while one was open for 30% -> 29% of each run, Pallas kernels for 9% -> 9%
where the time goes in v2:
time: 648 us; the launch traced here: 640 us
  waiting for transfers between devices  186 us (29%)
  starting transfers between devices  156 us (24%)
  other arithmetic  89.6 us (14%)
  matrix products  85.9 us (13%)
  Pallas kernels  66.8 us (10%)
  local copies, waits for them, and re-layouts  39.6 us (6%)
  between operations  16.5 us (3%)
    ppermute x29, starting transfers between devices, _swap_outer(): lax.ppermute(piece, 'dp', [(0, 1), (1, 0), (2, 3), (3, 2)])  88.1 us
    ppermute x29, waiting for transfers between devices, _swap_outer(): lax.ppermute(piece, 'dp', [(0, 1), (1, 0), (2, 3), (3, 2)])  79.3 us
    ppermute x14, waiting for transfers between devices, swap_x(): return lax.ppermute(block, 'tr', [(0, 1), (1, 0)])  42.2 us
    ppermute x15, waiting for transfers between devices, swap_y(): return lax.ppermute(block, 'tc', [(i, i ^ 2) for i in range(4)])  41.8 us
    dot_general x16, matrix products, contract_rows(): lax.dot_general(left_side, right_side, (((0,), (0,)), ((), ())), preferre...  32.8 us
    select_n x21, other arithmetic, send(): out = jnp.where(self.middle, self.total[which - self.lag], out)  30.8 us
    dot_general x14, matrix products, dot(): return jnp.dot(left_side, right_side, preferred_element_type=f32)  29.1 us
    convert_element_type x37, other arithmetic, low(): return array.astype(bf16)  28.8 us
  transfers between devices with their start and end apart: 115, of which 31 were waited for; matrix products, arithmetic and copies ran while one was open for 29% of the time, Pallas kernels for 9%

profile of v2, /device:TPU:0, one launch (start us, length us, event | category | flops | bytes accessed | tf_op | source)
XLA Modules:
  0.0 639.7 jit_solution(739325063561954127)
XLA Ops:
  9.2 3.0 collective-permute-start
  13.7 3.2 fusion.110
  23.0 2.9 convolution_convert_fusion.4
  26.1 3.1 convolution_convert_fusion.5
  33.2 3.6 add_convert_fusion.4
  44.4 3.7 convert_add_fusion.own
  50.2 22.0 %collective-permute-done.8 = f32[1024]{0:T(1024)S(1)} collective-permute-done((f32[1024]{0:T(1024)S(1)}, f32[1024]{0:T(1024)S(1)}, u32[]{:S(2)}, u32[]{:S(2)}) %collective-permute-start.8) | collective-permute-done | bytes 4128 | tf_op jit(solution)/shard_map/ppermute | solution.py:36
  76.7 9.5 %shard_map.237 = (f32[1024,512]{1,0:T(8,128)}, bf16[1024,256]{1,0:T(8,128)(2,1)S(1)}, bf16[1024,128]{1,0:T(8,128)(2,1)S(1)}, bf16[1024,128]{1,0:T(8,128)(2,1)S(1...) custom-call(s32[1]{0:T(128)} %bitcast.side, f32[1024,512]{1,0:T(8,128)} %convert_add_fusion.own, ...), custom_call_target="tpu_custom_call" | custom-call | bytes 1024 | tf_op jit(solution)/shard_map/pallas_call | solution.py:303
  93.1 6.5 %collective-permute-done.10 = bf16[1024,256]{1,0:T(8,128)(2,1)S(1)} collective-permute-done((bf16[1024,256]{1,0:T(8,128)(2,1)S(1)}, bf16[1024,256]{1,0:T(8,128)(2,1)S(1)}, u32[]{:S(2)}, u32[]{:S(2)}) %collective-permute-start.10) | collective-permute-done | bytes 524320 | tf_op jit(solution)/shard_map/ppermute | solution.py:36
  111.3 9.7 %collective-permute-done.14 = bf16[512,512]{1,0:T(8,128)(2,1)} collective-permute-done((bf16[512,512]{1,0:T(8,128)(2,1)S(1)}, bf16[512,512]{1,0:T(8,128)(2,1)}, u32[]{:S(2)}, u32[]{:S(2)}) %collective-permute-start.14) | collective-permute-done | bytes 524320 | tf_op jit(solution)/shard_map/ppermute | solution.py:44
  129.2 9.4 %collective-permute-done.22 = f32[1024]{0:T(1024)S(1)} collective-permute-done((f32[1024]{0:T(1024)S(1)}, f32[1024]{0:T(1024)S(1)}, u32[]{:S(2)}, u32[]{:S(2)}) %collective-permute-start.22) | collective-permute-done | bytes 4128 | tf_op jit(solution)/shard_map/ppermute | solution.py:36
  149.6 11.4 %shard_map.238 = (bf16[1024,768]{1,0:T(8,128)(2,1)}, bf16[1024,1536]{1,0:T(8,128)(2,1)}, bf16[1024,1536]{1,0:T(8,128)(2,1)}, f32[1024,1]{1,0:T(8,128)S(1)}) custom-call(bf16[512,512]{1,0:T(8,128)(2,1)S(1)} %multiply_convert_fusion.2.refs_0_, bf16[512,512]{1,0:T(8,128)(2,1)} %collective-permute-done.28.refs_1_, bf16[512,512]{1,0:T(8,128)(2,1)S(1)} %copy-done.24, ...), custom_call_target="tpu_custom_call" | custom-call | bytes 1024 | tf_op jit(solution)/shard_map/pallas_call | solution.py:377
  165.0 12.0 %shard_map.239 = (bf16[1024,768]{1,0:T(8,128)(2,1)}, bf16[1024,1536]{1,0:T(8,128)(2,1)}, bf16[1024,1536]{1,0:T(8,128)(2,1)}, f32[1024,1]{1,0:T(8,128)S(1)}) custom-call(bf16[512,512]{1,0:T(8,128)(2,1)} %collective-permute-done.18.refs_0_, ...), custom_call_target="tpu_custom_call", output_to_operand_aliasing={{0}: (17, {}), {1}: (18, {}), {2}: (19, {}), {3}: (20, {})} | custom-call | bytes 1024 | tf_op jit(solution)/shard_map/pallas_call | solution.py:377
  177.0 4.0 convolution_convert_fusion.1
  183.0 2.8 convolution_convert_fusion.2
  187.6 5.1 convolution_convert_fusion.3
  194.6 4.3 fusion.109
  198.9 3.1 add_convert_fusion.2
  205.6 4.2 convolution_convert_fusion
  222.6 2.8 collective-permute-done.37
  235.4 3.9 collective-permute-done.39
  245.9 8.1 %collective-permute-done.42 = bf16[512,512]{1,0:T(8,128)(2,1)S(1)} collective-permute-done((bf16[512,512]{1,0:T(8,128)(2,1)S(1)}, bf16[512,512]{1,0:T(8,128)(2,1)S(1)}, u32[]{:S(2)}, u32[]{:S(2)}) %collective-permute-start.42) | collective-permute-done | bytes 524320 | tf_op jit(solution)/shard_map/ppermute | solution.py:44
  255.6 3.7 collective-permute-start.52
  262.4 9.2 %collective-permute-done.52.refs_1_ = bf16[512,512]{1,0:T(8,128)(2,1)S(1)} collective-permute-done((bf16[512,512]{1,0:T(8,128)(2,1)S(1)}, bf16[512,512]{1,0:T(8,128)(2,1)S(1)}, u32[]{:S(2)}, u32[]{:S(2)}) %collective-permute-start.52) | collective-permute-done | bytes 524320 | tf_op jit(solution)/shard_map/ppermute | solution.py:77
  274.2 11.3 %collective-permute-start.56 = (bf16[512,512]{1,0:T(8,128)(2,1)S(1)}, bf16[512,512]{1,0:T(8,128)(2,1)S(1)}, u32[]{:S(2)}, u32[]{:S(2)}) collective-permute-start(bf16[512,512]{1,0:T(8,128)(2,1)S(1)} %get-tuple-element.365), channel_id=1, source_target_pairs={{0,8},{8,0},{16,24},{24,16},{1,9},{9,1},{17,25},{25,17},{2,10},{10... | collective-permute-start | bytes 1572872 | tf_op jit(solution)/shard_map/ppermute | solution.py:77
  286.1 3.0 collective-permute-start.60
  295.8 12.7 %shard_map.240 = (bf16[1024,512]{1,0:T(8,128)(2,1)}, f32[1,128]{1,0:T(1,128)S(1)}, f32[1,128]{1,0:T(1,128)S(1)}, f32[1024,1]{1,0:T(8,128)S(1)}) custom-call(s32[1]{0:T(128)} %bitcast.side, f32[1024,256]{1,0:T(8,128)} %convert_add_fusion.1.own, bf16[1024,256]{1,0:T(8,128)(2,1)S(1)} %collective-permute-done.50.from_y, f32[1024,512]{1,0:T(8,128)} %get-tuple-element.241.proj, ...), custom_call_target="tpu_custom_call" | custom-call | bytes 1024 | tf_op jit(solution)/shard_map/pallas_call | solution.py:303
  310.5 4.6 collective-permute-start.59
  319.4 6.4 collective-permute-done.59.refs_1_
  329.4 8.5 %collective-permute-done.63.refs_3_ = bf16[512,512]{1,0:T(8,128)(2,1)S(1)} collective-permute-done((bf16[512,512]{1,0:T(8,128)(2,1)S(1)}, bf16[512,512]{1,0:T(8,128)(2,1)S(1)}, u32[]{:S(2)}, u32[]{:S(2)}) %collective-permute-start.63) | collective-permute-done | bytes 524320 | tf_op jit(solution)/shard_map/ppermute | solution.py:77
  341.8 7.0 %collective-permute-done.62.refs_5_ = bf16[512,512]{1,0:T(8,128)(2,1)S(1)} collective-permute-done((bf16[512,512]{1,0:T(8,128)(2,1)S(1)}, bf16[512,512]{1,0:T(8,128)(2,1)S(1)}, u32[]{:S(2)}, u32[]{:S(2)}) %collective-permute-start.62) | collective-permute-done | bytes 524320 | tf_op jit(solution)/shard_map/ppermute | solution.py:77
  353.7 3.0 fusion.40
  361.4 2.9 collective-permute-start.74
  378.4 15.0 %collective-permute-done.70 = f32[1792]{0:T(1024)S(1)} collective-permute-done((f32[1792]{0:T(1024)S(1)}, f32[1792]{0:T(1024)S(1)}, u32[]{:S(2)}, u32[]{:S(2)}) %collective-permute-start.70) | collective-permute-done | bytes 7200 | tf_op jit(solution)/shard_map/ppermute | solution.py:44
  396.1 10.2 %collective-permute-done.76.refs_11_ = bf16[512,512]{1,0:T(8,128)(2,1)S(1)} collective-permute-done((bf16[512,512]{1,0:T(8,128)(2,1)S(1)}, bf16[512,512]{1,0:T(8,128)(2,1)S(1)}, u32[]{:S(2)}, u32[]{:S(2)}) %collective-permute-start.76) | collective-permute-done | bytes 524320 | tf_op jit(solution)/shard_map/ppermute | solution.py:77
  411.4 3.2 collective-permute-start.81
  415.9 18.4 %all-gather.15.cloned.1.call-done = bf16[4096,1536]{1,0:T(8,128)(2,1)} async-done(((bf16[1024,1536]{1,0:T(8,128)(2,1)}), bf16[4096,1536]{1,0:T(8,128)(2,1)}) %all-gather.15.cloned.1.call-update) | async-done | bytes 12582928 | tf_op jit(solution)/shard_map/all_gather | solution.py:648
  434.3 4.0 fusion.13
  439.6 3.9 fusion.10
  446.7 2.5 broadcast_select_fusion.10
  450.7 2.4 broadcast_select_fusion.7
  459.1 5.1 collective-permute-done.79.refs_1_
  468.0 6.8 %collective-permute-done.84.refs_3_ = bf16[512,512]{1,0:T(8,128)(2,1)} collective-permute-done((bf16[512,512]{1,0:T(8,128)(2,1)}, bf16[512,512]{1,0:T(8,128)(2,1)}, u32[]{:S(2)}, u32[]{:S(2)}) %collective-permute-start.84) | collective-permute-done | bytes 524320 | tf_op jit(solution)/shard_map/ppermute | solution.py:77
  474.8 2.4 broadcast_select_fusion.8
  483.3 3.6 collective-permute-start.87
  486.8 5.3 collective-permute-done.82.refs_5_
  495.3 5.0 fusion.28
  503.0 2.3 broadcast_select_fusion.5
  505.3 3.3 collective-permute-start.90
  517.6 2.4 broadcast_select_fusion.4
  522.6 2.5 broadcast_select_fusion.2
  529.3 2.4 shard_map.242
  532.5 4.5 shard_map.241
  543.9 6.4 %collective-permute-start.96 = (bf16[512,512]{1,0:T(8,128)(2,1)S(1)}, bf16[512,512]{1,0:T(8,128)(2,1)S(1)}, u32[]{:S(2)}, u32[]{:S(2)}) collective-permute-start(bf16[512,512]{1,0:T(8,128)(2,1)S(1)} %get-tuple-element.333), channel_id=1, source_target_pairs={{0,8},{8,0},{16,24},{24,16},{1,9},{9,1},{17,25},{25,17},{2,10},{10... | collective-permute-start | bytes 1572872 | tf_op jit(solution)/shard_map/ppermute | solution.py:77
  551.3 7.3 %collective-permute-start.103 = (bf16[512,512]{1,0:T(8,128)(2,1)S(1)}, bf16[512,512]{1,0:T(8,128)(2,1)S(1)}, u32[]{:S(2)}, u32[]{:S(2)}) collective-permute-start(bf16[512,512]{1,0:T(8,128)(2,1)S(1)} %get-tuple-element.327), channel_id=1, source_target_pairs={{0,8},{8,0},{16,24},{24,16},{1,9},{9,1},{17,25},{25,17},{2,10},{10... | collective-permute-start | bytes 1572872 | tf_op jit(solution)/shard_map/ppermute | solution.py:77
  562.5 6.5 %collective-permute-done.103.refs_21_ = bf16[512,512]{1,0:T(8,128)(2,1)S(1)} collective-permute-done((bf16[512,512]{1,0:T(8,128)(2,1)S(1)}, bf16[512,512]{1,0:T(8,128)(2,1)S(1)}, u32[]{:S(2)}, u32[]{:S(2)}) %collective-permute-start.103) | collective-permute-done | bytes 524320 | tf_op jit(solution)/shard_map/ppermute | solution.py:77
  570.0 2.4 collective-permute-start.99
  573.5 6.7 %collective-permute-start.105 = (bf16[512,512]{1,0:T(8,128)(2,1)S(1)}, bf16[512,512]{1,0:T(8,128)(2,1)S(1)}, u32[]{:S(2)}, u32[]{:S(2)}) collective-permute-start(bf16[512,512]{1,0:T(8,128)(2,1)S(1)} %add_convert_fusion.8.refs_6_), channel_id=1, source_target_pairs={{0,8},{8,0},{16,24},{24,16},{1,9},{9,1},{17,25},{25,17},{2,10},{10... | collective-permute-start | bytes 1572872 | tf_op jit(solution)/shard_map/ppermute | solution.py:77
  580.2 4.8 collective-permute-done.99.refs_23_
  586.1 9.0 %shard_map.243 = (f32[512,3072]{1,0:T(8,128)}, f32[512,3072]{1,0:T(8,128)}) custom-call(s32[5]{0:T(128)S(1)} %stack.39.words, bf16[512,512]{1,0:T(8,128)(2,1)S(1)} %copy-done.10, bf16[512,512]{1,0:T(8,128)(2,1)S(1)} %collective-permute-done.52.refs_1_, bf16[512,512]{1,0:T(8,128)(2,1)S(1)} %copy-done.11, ...), custom_call_target="tpu_custom_call" | custom-call | bytes 1024 | tf_op jit(solution)/shard_map/pallas_call | solution.py:416
  595.3 7.4 %collective-permute-start.109 = (bf16[512,512]{1,0:T(8,128)(2,1)S(1)}, bf16[512,512]{1,0:T(8,128)(2,1)S(1)}, u32[]{:S(2)}, u32[]{:S(2)}) collective-permute-start(bf16[512,512]{1,0:T(8,128)(2,1)S(1)} %add_convert_fusion.5.refs_10_), channel_id=1, source_target_pairs={{0,8},{8,0},{16,24},{24,16},{1,9},{9,1},{17,25},{25,17},{2,10},{10... | collective-permute-start | bytes 1572872 | tf_op jit(solution)/shard_map/ppermute | solution.py:77
  603.1 7.7 %collective-permute-start.101 = (bf16[512,512]{1,0:T(8,128)(2,1)S(1)}, bf16[512,512]{1,0:T(8,128)(2,1)S(1)}, u32[]{:S(2)}, u32[]{:S(2)}) collective-permute-start(bf16[512,512]{1,0:T(8,128)(2,1)S(1)} %add_convert_fusion.10), channel_id=1, source_target_pairs={{0,8},{8,0},{16,24},{24,16},{1,9},{9,1},{17,25},{25,17},{2,10},{10... | collective-permute-start | bytes 1572872 | tf_op jit(solution)/shard_map/ppermute | solution.py:77
  618.1 7.2 %collective-permute-done.107.refs_9_ = bf16[512,512]{1,0:T(8,128)(2,1)S(1)} collective-permute-done((bf16[512,512]{1,0:T(8,128)(2,1)S(1)}, bf16[512,512]{1,0:T(8,128)(2,1)S(1)}, u32[]{:S(2)}, u32[]{:S(2)}) %collective-permute-start.107) | collective-permute-done | bytes 524320 | tf_op jit(solution)/shard_map/ppermute | solution.py:77
  626.2 5.3 shard_map.244
  (667 shorter events, 236.8 us)
Async XLA Ops:
  7.2 92.6 %all-gather.7.cloned.1.call-start = ((), (), s32[]{:S(2)}) async-start(), calls=%async_computation | async-start | bytes 1966080 | tf_op jit(solution)/shard_map/all_gather | solution.py:481
  29.5 42.7 %collective-permute-start.5 = (bf16[128,1536]{1,0:T(8,128)(2,1)}, bf16[128,1536]{1,0:T(8,128)(2,1)}, u32[]{:S(2)}, u32[]{:S(2)}) collective-permute-start(bf16[128,1536]{1,0:T(8,128)(2,1)} %pad_maximum_fusion.19), channel_id=1, source_target_pairs={{0,2},{1,3},{2,0},{3,1},{4,6},{5,7},{6,4},{7,5},{8,10},{9,11},{10,... | collective-permute-start | bytes 1179656 | tf_op jit(solution)/shard_map/ppermute | solution.py:36
  31.2 41.0 %collective-permute-start.6 = (bf16[128,1536]{1,0:T(8,128)(2,1)}, bf16[128,1536]{1,0:T(8,128)(2,1)}, u32[]{:S(2)}, u32[]{:S(2)}) collective-permute-start(bf16[128,1536]{1,0:T(8,128)(2,1)} %pad_maximum_fusion.20), channel_id=1, source_target_pairs={{0,3},{1,2},{2,1},{3,0},{4,7},{5,6},{6,5},{7,4},{8,11},{9,10},{10,... | collective-permute-start | bytes 1179656 | tf_op jit(solution)/shard_map/ppermute | solution.py:40
  33.2 87.8 %all-gather.9.cloned.1.call-start = ((), (), s32[]{:S(2)}) async-start(), calls=%async_computation.1 | async-start | bytes 1966080 | tf_op jit(solution)/shard_map/all_gather | solution.py:523
  36.8 35.4 %collective-permute-start.4 = (bf16[1024,512]{1,0:T(8,128)(2,1)}, bf16[1024,512]{1,0:T(8,128)(2,1)}, u32[]{:S(2)}, u32[]{:S(2)}) collective-permute-start(bf16[1024,512]{1,0:T(8,128)(2,1)} %add_convert_fusion.4), channel_id=1, source_target_pairs={{0,2},{1,3},{2,0},{3,1},{4,6},{5,7},{6,4},{7,5},{8,10},{9,11},{10,... | collective-permute-start | bytes 3145736 | tf_op jit(solution)/shard_map/ppermute | solution.py:36
  49.6 22.6 %collective-permute-start.8 = (f32[1024]{0:T(1024)S(1)}, f32[1024]{0:T(1024)S(1)}, u32[]{:S(2)}, u32[]{:S(2)}) collective-permute-start(f32[1024]{0:T(1024)S(1)} %add.390), channel_id=1, source_target_pairs={{0,2},{1,3},{2,0},{3,1},{4,6},{5,7},{6,4},{7,5},{8,10},{9,11},{10,... | collective-permute-start | bytes 12296 | tf_op jit(solution)/shard_map/ppermute | solution.py:36
  72.3 76.3 %all-gather.11.cloned.1.call-start = ((), (), s32[]{:S(2)}) async-start(), calls=%async_computation.2 | async-start | bytes 1966080 | tf_op jit(solution)/shard_map/all_gather | solution.py:523
  89.2 22.1 %collective-permute-start.16 = (bf16[512,1536]{1,0:T(8,128)(2,1)}, bf16[512,1536]{1,0:T(8,128)(2,1)}, u32[]{:S(2)}, u32[]{:S(2)}) collective-permute-start(bf16[512,1536]{1,0:T(8,128)(2,1)} %pad_maximum_fusion), channel_id=1, source_target_pairs={{0,1},{1,0},{2,3},{3,2},{4,5},{5,4},{6,7},{7,6},{8,9},{9,8},{10,11... | collective-permute-start | bytes 4718600 | tf_op jit(solution)/shard_map/ppermute | solution.py:32
  89.2 22.0 %collective-permute-start.17 = (bf16[768,512]{1,0:T(8,128)(2,1)}, bf16[768,512]{1,0:T(8,128)(2,1)}, u32[]{:S(2)}, u32[]{:S(2)}) collective-permute-start(bf16[768,512]{1,0:T(8,128)(2,1)} %get-tuple-element.374), channel_id=1, source_target_pairs={{0,1},{1,0},{2,3},{3,2},{4,5},{5,4},{6,7},{7,6},{8,9},{9,8},{10,11... | collective-permute-start | bytes 2359304 | tf_op jit(solution)/shard_map/ppermute | solution.py:32
  101.9 332.5 %all-gather.15.cloned.1.call-start = ((), (), s32[]{:S(2)}) async-start(), calls=%async_computation.4 | async-start | bytes 15728640 | tf_op jit(solution)/shard_map/all_gather | solution.py:648
  102.3 36.9 %collective-permute-start.23 = (bf16[512,512]{1,0:T(8,128)(2,1)}, bf16[512,512]{1,0:T(8,128)(2,1)}, u32[]{:S(2)}, u32[]{:S(2)}) collective-permute-start(bf16[512,512]{1,0:T(8,128)(2,1)} %collective-permute-done.11.refs_10_), channel_id=1, source_target_pairs={{0,1},{1,0},{2,3},{3,2},{4,5},{5,4},{6,7},{7,6},{8,9},{9,8},{10,11... | collective-permute-start | bytes 1572872 | tf_op jit(solution)/shard_map/ppermute | solution.py:32
  111.2 28.0 %collective-permute-start.24 = (bf16[512,512]{1,0:T(8,128)(2,1)}, bf16[512,512]{1,0:T(8,128)(2,1)}, u32[]{:S(2)}, u32[]{:S(2)}) collective-permute-start(bf16[512,512]{1,0:T(8,128)(2,1)} %collective-permute-done.12.refs_10_), channel_id=1, source_target_pairs={{0,1},{1,0},{2,3},{3,2},{4,5},{5,4},{6,7},{7,6},{8,9},{9,8},{10,11... | collective-permute-start | bytes 1572872 | tf_op jit(solution)/shard_map/ppermute | solution.py:32
  139.8 21.2 %collective-permute-start.27 = (bf16[512,512]{1,0:T(8,128)(2,1)}, bf16[512,512]{1,0:T(8,128)(2,1)}, u32[]{:S(2)}, u32[]{:S(2)}) collective-permute-start(bf16[512,512]{1,0:T(8,128)(2,1)} %collective-permute-done.18.refs_0_), channel_id=1, source_target_pairs={{0,1},{1,0},{2,3},{3,2},{4,5},{5,4},{6,7},{7,6},{8,9},{9,8},{10,11... | collective-permute-start | bytes 1572872 | tf_op jit(solution)/shard_map/ppermute | solution.py:32
  142.3 18.7 %collective-permute-start.25 = (bf16[256,512]{1,0:T(8,128)(2,1)}, bf16[256,512]{1,0:T(8,128)(2,1)}, u32[]{:S(2)}, u32[]{:S(2)}) collective-permute-start(bf16[256,512]{1,0:T(8,128)(2,1)} %slice.164), channel_id=1, source_target_pairs={{0,2},{1,3},{2,0},{3,1},{4,6},{5,7},{6,4},{7,5},{8,10},{9,11},{10,... | collective-permute-start | bytes 786440 | tf_op jit(solution)/shard_map/ppermute | solution.py:36
  144.1 17.0 %collective-permute-start.26 = (bf16[256,512]{1,0:T(8,128)(2,1)}, bf16[256,512]{1,0:T(8,128)(2,1)}, u32[]{:S(2)}, u32[]{:S(2)}) collective-permute-start(bf16[256,512]{1,0:T(8,128)(2,1)} %slice.165), channel_id=1, source_target_pairs={{0,4},{4,0},{1,5},{5,1},{2,6},{6,2},{3,7},{7,3},{8,12},{12,8},{9,1... | collective-permute-start | bytes 786440 | tf_op jit(solution)/shard_map/ppermute | solution.py:44
  186.5 33.2 %collective-permute-start.35 = (bf16[512,512]{1,0:T(8,128)(2,1)}, bf16[512,512]{1,0:T(8,128)(2,1)}, u32[]{:S(2)}, u32[]{:S(2)}) collective-permute-start(bf16[512,512]{1,0:T(8,128)(2,1)} %get-tuple-element.210), channel_id=1, source_target_pairs={{0,8},{8,0},{16,24},{24,16},{1,9},{9,1},{17,25},{25,17},{2,10},{10... | collective-permute-start | bytes 1572872 | tf_op jit(solution)/shard_map/ppermute | solution.py:77
  192.9 36.4 %collective-permute-start.41 = (bf16[512,512]{1,0:T(8,128)(2,1)}, bf16[512,512]{1,0:T(8,128)(2,1)}, u32[]{:S(2)}, u32[]{:S(2)}) collective-permute-start(bf16[512,512]{1,0:T(8,128)(2,1)} %get-tuple-element.219), channel_id=1, source_target_pairs={{0,8},{8,0},{16,24},{24,16},{1,9},{9,1},{17,25},{25,17},{2,10},{10... | collective-permute-start | bytes 1572872 | tf_op jit(solution)/shard_map/ppermute | solution.py:77
  221.8 23.1 %collective-permute-start.44 = (bf16[512,512]{1,0:T(8,128)(2,1)S(1)}, bf16[512,512]{1,0:T(8,128)(2,1)S(1)}, u32[]{:S(2)}, u32[]{:S(2)}) collective-permute-start(bf16[512,512]{1,0:T(8,128)(2,1)S(1)} %add_convert_fusion.57), channel_id=1, source_target_pairs={{8,16},{16,8},{9,17},{17,9},{10,18},{18,10},{11,19},{19,11},{12,20... | collective-permute-start | bytes 1572872 | tf_op jit(solution)/shard_map/ppermute | solution.py:72
  225.5 34.3 %collective-permute-start.51 = (bf16[512,1536]{1,0:T(8,128)(2,1)S(1)}, bf16[512,1536]{1,0:T(8,128)(2,1)S(1)}, u32[]{:S(2)}, u32[]{:S(2)}) collective-permute-start(bf16[512,1536]{1,0:T(8,128)(2,1)S(1)} %copy-done.153), channel_id=1, source_target_pairs={{0,1},{1,0},{2,3},{3,2},{4,5},{5,4},{6,7},{7,6},{8,9},{9,8},{10,11... | collective-permute-start | bytes 4718600 | tf_op jit(solution)/shard_map/ppermute | solution.py:32
  227.7 17.0 %collective-permute-start.43 = (bf16[512,512]{1,0:T(8,128)(2,1)S(1)}, bf16[512,512]{1,0:T(8,128)(2,1)S(1)}, u32[]{:S(2)}, u32[]{:S(2)}) collective-permute-start(bf16[512,512]{1,0:T(8,128)(2,1)S(1)} %copy-done.91), channel_id=1, source_target_pairs={{0,8},{8,0},{16,24},{24,16},{1,9},{9,1},{17,25},{25,17},{2,10},{10... | collective-permute-start | bytes 1572872 | tf_op jit(solution)/shard_map/ppermute | solution.py:77
  239.4 21.2 %collective-permute-start.48 = (bf16[512,512]{1,0:T(8,128)(2,1)S(1)}, bf16[512,512]{1,0:T(8,128)(2,1)S(1)}, u32[]{:S(2)}, u32[]{:S(2)}) collective-permute-start(bf16[512,512]{1,0:T(8,128)(2,1)S(1)} %get-tuple-element.228), channel_id=1, source_target_pairs={{0,8},{8,0},{16,24},{24,16},{1,9},{9,1},{17,25},{25,17},{2,10},{10... | collective-permute-start | bytes 1572872 | tf_op jit(solution)/shard_map/ppermute | solution.py:77
  260.6 32.7 %collective-permute-start.46 = (bf16[1024,256]{1,0:T(8,128)(2,1)S(1)}, bf16[1024,256]{1,0:T(8,128)(2,1)S(1)}, u32[]{:S(2)}, u32[]{:S(2)}) collective-permute-start(bf16[1024,256]{1,0:T(8,128)(2,1)S(1)} %convolution_convert_fusion.9), channel_id=1, source_target_pairs={{0,1},{1,0},{2,3},{3,2},{4,5},{5,4},{6,7},{7,6},{8,9},{9,8},{10,11... | collective-permute-start | bytes 1572872 | tf_op jit(solution)/shard_map/ppermute | solution.py:32
  272.7 23.1 %collective-permute-start.50 = (bf16[1024,256]{1,0:T(8,128)(2,1)S(1)}, bf16[1024,256]{1,0:T(8,128)(2,1)S(1)}, u32[]{:S(2)}, u32[]{:S(2)}) collective-permute-start(bf16[1024,256]{1,0:T(8,128)(2,1)S(1)} %add_convert_fusion.50), channel_id=1, source_target_pairs={{0,2},{1,3},{2,0},{3,1},{4,6},{5,7},{6,4},{7,5},{8,10},{9,11},{10,... | collective-permute-start | bytes 1572872 | tf_op jit(solution)/shard_map/ppermute | solution.py:36
  274.2 34.3 %collective-permute-start.56 = (bf16[512,512]{1,0:T(8,128)(2,1)S(1)}, bf16[512,512]{1,0:T(8,128)(2,1)S(1)}, u32[]{:S(2)}, u32[]{:S(2)}) collective-permute-start(bf16[512,512]{1,0:T(8,128)(2,1)S(1)} %get-tuple-element.365), channel_id=1, source_target_pairs={{0,8},{8,0},{16,24},{24,16},{1,9},{9,1},{17,25},{25,17},{2,10},{10... | collective-permute-start | bytes 1572872 | tf_op jit(solution)/shard_map/ppermute | solution.py:77
  285.5 24.0 %collective-permute-start.58 = (bf16[512,512]{1,0:T(8,128)(2,1)S(1)}, bf16[512,512]{1,0:T(8,128)(2,1)S(1)}, u32[]{:S(2)}, u32[]{:S(2)}) collective-permute-start(bf16[512,512]{1,0:T(8,128)(2,1)S(1)} %add_convert_fusion.52), channel_id=1, source_target_pairs={{8,16},{16,8},{9,17},{17,9},{10,18},{18,10},{11,19},{19,11},{12,20... | collective-permute-start | bytes 1572872 | tf_op jit(solution)/shard_map/ppermute | solution.py:72
  286.1 29.0 %collective-permute-start.60 = (bf16[512,512]{1,0:T(8,128)(2,1)S(1)}, bf16[512,512]{1,0:T(8,128)(2,1)S(1)}, u32[]{:S(2)}, u32[]{:S(2)}) collective-permute-start(bf16[512,512]{1,0:T(8,128)(2,1)S(1)} %get-tuple-element.363), channel_id=1, source_target_pairs={{0,8},{8,0},{16,24},{24,16},{1,9},{9,1},{17,25},{25,17},{2,10},{10... | collective-permute-start | bytes 1572872 | tf_op jit(solution)/shard_map/ppermute | solution.py:77
  293.3 25.0 %collective-permute-start.61 = (bf16[512,512]{1,0:T(8,128)(2,1)S(1)}, bf16[512,512]{1,0:T(8,128)(2,1)S(1)}, u32[]{:S(2)}, u32[]{:S(2)}) collective-permute-start(bf16[512,512]{1,0:T(8,128)(2,1)S(1)} %add_convert_fusion.49), channel_id=1, source_target_pairs={{8,16},{16,8},{9,17},{17,9},{10,18},{18,10},{11,19},{19,11},{12,20... | collective-permute-start | bytes 1572872 | tf_op jit(solution)/shard_map/ppermute | solution.py:72
  308.6 19.0 %collective-permute-start.57 = (bf16[512,512]{1,0:T(8,128)(2,1)S(1)}, bf16[512,512]{1,0:T(8,128)(2,1)S(1)}, u32[]{:S(2)}, u32[]{:S(2)}) collective-permute-start(bf16[512,512]{1,0:T(8,128)(2,1)S(1)} %add_convert_fusion.47), channel_id=1, source_target_pairs={{8,16},{16,8},{9,17},{17,9},{10,18},{18,10},{11,19},{19,11},{12,20... | collective-permute-start | bytes 1572872 | tf_op jit(solution)/shard_map/ppermute | solution.py:72
  315.3 25.3 %collective-permute-start.64 = (bf16[512,512]{1,0:T(8,128)(2,1)S(1)}, bf16[512,512]{1,0:T(8,128)(2,1)S(1)}, u32[]{:S(2)}, u32[]{:S(2)}) collective-permute-start(bf16[512,512]{1,0:T(8,128)(2,1)S(1)} %add_convert_fusion.44), channel_id=1, source_target_pairs={{8,16},{16,8},{9,17},{17,9},{10,18},{18,10},{11,19},{19,11},{12,20... | collective-permute-start | bytes 1572872 | tf_op jit(solution)/shard_map/ppermute | solution.py:72
  316.0 34.9 %collective-permute-start.54 = (bf16[1024,512]{1,0:T(8,128)(2,1)S(1)}, bf16[1024,512]{1,0:T(8,128)(2,1)S(1)}, u32[]{:S(2)}, u32[]{:S(2)}) collective-permute-start(bf16[1024,512]{1,0:T(8,128)(2,1)S(1)} %copy-done.115), channel_id=1, source_target_pairs={{0,2},{1,3},{2,0},{3,1},{4,6},{5,7},{6,4},{7,5},{8,10},{9,11},{10,... | collective-permute-start | bytes 3145736 | tf_op jit(solution)/shard_map/ppermute | solution.py:36
  318.3 32.7 %collective-permute-start.55 = (bf16[1024,512]{1,0:T(8,128)(2,1)S(1)}, bf16[1024,512]{1,0:T(8,128)(2,1)S(1)}, u32[]{:S(2)}, u32[]{:S(2)}) collective-permute-start(bf16[1024,512]{1,0:T(8,128)(2,1)S(1)} %copy-done.115), channel_id=1, source_target_pairs={{0,1},{1,0},{2,3},{3,2},{4,5},{5,4},{6,7},{7,6},{8,9},{9,8},{10,11... | collective-permute-start | bytes 3145736 | tf_op jit(solution)/shard_map/ppermute | solution.py:32
  327.7 22.1 %collective-permute-start.65 = (bf16[512,512]{1,0:T(8,128)(2,1)S(1)}, bf16[512,512]{1,0:T(8,128)(2,1)S(1)}, u32[]{:S(2)}, u32[]{:S(2)}) collective-permute-start(bf16[512,512]{1,0:T(8,128)(2,1)S(1)} %add_convert_fusion.42), channel_id=1, source_target_pairs={{8,16},{16,8},{9,17},{17,9},{10,18},{18,10},{11,19},{19,11},{12,20... | collective-permute-start | bytes 1572872 | tf_op jit(solution)/shard_map/ppermute | solution.py:72
  353.0 142.4 %all-gather.13.cloned.1.call-start = ((), (), s32[]{:S(2)}) async-start(), calls=%async_computation.3 | async-start | bytes 7864320 | tf_op jit(solution)/shard_map/all_gather | solution.py:664
  359.2 16.0 %collective-permute-start.71 = (bf16[512,512]{1,0:T(8,128)(2,1)S(1)}, bf16[512,512]{1,0:T(8,128)(2,1)S(1)}, u32[]{:S(2)}, u32[]{:S(2)}) collective-permute-start(bf16[512,512]{1,0:T(8,128)(2,1)S(1)} %copy-done.143), channel_id=1, source_target_pairs={{0,8},{8,0},{16,24},{24,16},{1,9},{9,1},{17,25},{25,17},{2,10},{10... | collective-permute-start | bytes 1572872 | tf_op jit(solution)/shard_map/ppermute | solution.py:77
  361.4 33.7 %collective-permute-start.74 = (bf16[512,512]{1,0:T(8,128)(2,1)S(1)}, bf16[512,512]{1,0:T(8,128)(2,1)S(1)}, u32[]{:S(2)}, u32[]{:S(2)}) collective-permute-start(bf16[512,512]{1,0:T(8,128)(2,1)S(1)} %copy-done.142), channel_id=1, source_target_pairs={{0,8},{8,0},{16,24},{24,16},{1,9},{9,1},{17,25},{25,17},{2,10},{10... | collective-permute-start | bytes 1572872 | tf_op jit(solution)/shard_map/ppermute | solution.py:77
  368.1 25.2 %collective-permute-start.69 = (bf16[1024,512]{1,0:T(8,128)(2,1)S(1)}, bf16[1024,512]{1,0:T(8,128)(2,1)S(1)}, u32[]{:S(2)}, u32[]{:S(2)}) collective-permute-start(bf16[1024,512]{1,0:T(8,128)(2,1)S(1)} %add_convert_fusion.1), channel_id=1, source_target_pairs={{0,4},{4,0},{1,5},{5,1},{2,6},{6,2},{3,7},{7,3},{8,12},{12,8},{9,1... | collective-permute-start | bytes 3145736 | tf_op jit(solution)/shard_map/ppermute | solution.py:44
  374.4 40.2 %collective-permute-start.73 = (bf16[512,512]{1,0:T(8,128)(2,1)S(1)}, bf16[512,512]{1,0:T(8,128)(2,1)S(1)}, u32[]{:S(2)}, u32[]{:S(2)}) collective-permute-start(bf16[512,512]{1,0:T(8,128)(2,1)S(1)} %copy-done.90), channel_id=1, source_target_pairs={{8,16},{16,8},{9,17},{17,9},{10,18},{18,10},{11,19},{19,11},{12,20... | collective-permute-start | bytes 1572872 | tf_op jit(solution)/shard_map/ppermute | solution.py:72
  375.2 18.1 %collective-permute-start.70 = (f32[1792]{0:T(1024)S(1)}, f32[1792]{0:T(1024)S(1)}, u32[]{:S(2)}, u32[]{:S(2)}) collective-permute-start(f32[1792]{0:T(1024)S(1)} %pad_maximum_fusion.38), channel_id=1, source_target_pairs={{0,4},{4,0},{1,5},{5,1},{2,6},{6,2},{3,7},{7,3},{8,12},{12,8},{9,1... | collective-permute-start | bytes 21512 | tf_op jit(solution)/shard_map/ppermute | solution.py:44
  376.7 33.5 %collective-permute-start.80 = (bf16[512,512]{1,0:T(8,128)(2,1)S(1)}, bf16[512,512]{1,0:T(8,128)(2,1)S(1)}, u32[]{:S(2)}, u32[]{:S(2)}) collective-permute-start(bf16[512,512]{1,0:T(8,128)(2,1)S(1)} %add_convert_fusion.37), channel_id=1, source_target_pairs={{8,16},{16,8},{9,17},{17,9},{10,18},{18,10},{11,19},{19,11},{12,20... | collective-permute-start | bytes 1572872 | tf_op jit(solution)/shard_map/ppermute | solution.py:72
  407.3 43.4 %collective-permute-start.83 = (bf16[512,512]{1,0:T(8,128)(2,1)}, bf16[512,512]{1,0:T(8,128)(2,1)}, u32[]{:S(2)}, u32[]{:S(2)}) collective-permute-start(bf16[512,512]{1,0:T(8,128)(2,1)} %add_convert_fusion.33), channel_id=1, source_target_pairs={{8,16},{16,8},{9,17},{17,9},{10,18},{18,10},{11,19},{19,11},{12,20... | collective-permute-start | bytes 1572872 | tf_op jit(solution)/shard_map/ppermute | solution.py:72
  408.7 38.0 %collective-permute-start.78 = (bf16[512,512]{1,0:T(8,128)(2,1)}, bf16[512,512]{1,0:T(8,128)(2,1)}, u32[]{:S(2)}, u32[]{:S(2)}) collective-permute-start(bf16[512,512]{1,0:T(8,128)(2,1)} %add_convert_fusion.34), channel_id=1, source_target_pairs={{8,16},{16,8},{9,17},{17,9},{10,18},{18,10},{11,19},{19,11},{12,20... | collective-permute-start | bytes 1572872 | tf_op jit(solution)/shard_map/ppermute | solution.py:72
  411.4 34.3 %collective-permute-start.81 = (bf16[512,512]{1,0:T(8,128)(2,1)}, bf16[512,512]{1,0:T(8,128)(2,1)S(1)}, u32[]{:S(2)}, u32[]{:S(2)}) collective-permute-start(bf16[512,512]{1,0:T(8,128)(2,1)} %get-tuple-element.345), channel_id=1, source_target_pairs={{0,8},{8,0},{16,24},{24,16},{1,9},{9,1},{17,25},{25,17},{2,10},{10... | collective-permute-start | bytes 1572872 | tf_op jit(solution)/shard_map/ppermute | solution.py:77
  415.9 28.7 %collective-permute-start.75 = (bf16[512,512]{1,0:T(8,128)(2,1)}, bf16[512,512]{1,0:T(8,128)(2,1)S(1)}, u32[]{:S(2)}, u32[]{:S(2)}) collective-permute-start(bf16[512,512]{1,0:T(8,128)(2,1)} %get-tuple-element.349), channel_id=1, source_target_pairs={{0,8},{8,0},{16,24},{24,16},{1,9},{9,1},{17,25},{25,17},{2,10},{10... | collective-permute-start | bytes 1572872 | tf_op jit(solution)/shard_map/ppermute | solution.py:77
  453.1 21.8 %collective-permute-start.84 = (bf16[512,512]{1,0:T(8,128)(2,1)}, bf16[512,512]{1,0:T(8,128)(2,1)}, u32[]{:S(2)}, u32[]{:S(2)}) collective-permute-start(bf16[512,512]{1,0:T(8,128)(2,1)} %get-tuple-element.341), channel_id=1, source_target_pairs={{0,8},{8,0},{16,24},{24,16},{1,9},{9,1},{17,25},{25,17},{2,10},{10... | collective-permute-start | bytes 1572872 | tf_op jit(solution)/shard_map/ppermute | solution.py:77
  453.6 21.3 %collective-permute-start.77 = (bf16[512,512]{1,0:T(8,128)(2,1)}, bf16[512,512]{1,0:T(8,128)(2,1)}, u32[]{:S(2)}, u32[]{:S(2)}) collective-permute-start(bf16[512,512]{1,0:T(8,128)(2,1)} %add_convert_fusion.32), channel_id=1, source_target_pairs={{8,16},{16,8},{9,17},{17,9},{10,18},{18,10},{11,19},{19,11},{12,20... | collective-permute-start | bytes 1572872 | tf_op jit(solution)/shard_map/ppermute | solution.py:72
  458.3 23.8 %collective-permute-start.86 = (bf16[512,512]{1,0:T(8,128)(2,1)}, bf16[512,512]{1,0:T(8,128)(2,1)S(1)}, u32[]{:S(2)}, u32[]{:S(2)}) collective-permute-start(bf16[512,512]{1,0:T(8,128)(2,1)} %add_convert_fusion.28), channel_id=1, source_target_pairs={{8,16},{16,8},{9,17},{17,9},{10,18},{18,10},{11,19},{19,11},{12,20... | collective-permute-start | bytes 1572872 | tf_op jit(solution)/shard_map/ppermute | solution.py:72
  466.4 36.6 %collective-permute-start.89 = (bf16[512,512]{1,0:T(8,128)(2,1)}, bf16[512,512]{1,0:T(8,128)(2,1)}, u32[]{:S(2)}, u32[]{:S(2)}) collective-permute-start(bf16[512,512]{1,0:T(8,128)(2,1)} %add_convert_fusion.27), channel_id=1, source_target_pairs={{8,16},{16,8},{9,17},{17,9},{10,18},{18,10},{11,19},{19,11},{12,20... | collective-permute-start | bytes 1572872 | tf_op jit(solution)/shard_map/ppermute | solution.py:72
  480.6 37.0 %collective-permute-start.92 = (bf16[512,512]{1,0:T(8,128)(2,1)}, bf16[512,512]{1,0:T(8,128)(2,1)}, u32[]{:S(2)}, u32[]{:S(2)}) collective-permute-start(bf16[512,512]{1,0:T(8,128)(2,1)} %add_convert_fusion.25), channel_id=1, source_target_pairs={{8,16},{16,8},{9,17},{17,9},{10,18},{18,10},{11,19},{19,11},{12,20... | collective-permute-start | bytes 1572872 | tf_op jit(solution)/shard_map/ppermute | solution.py:72
  483.3 32.2 %collective-permute-start.87 = (bf16[512,512]{1,0:T(8,128)(2,1)}, bf16[512,512]{1,0:T(8,128)(2,1)}, u32[]{:S(2)}, u32[]{:S(2)}) collective-permute-start(bf16[512,512]{1,0:T(8,128)(2,1)} %get-tuple-element.339), channel_id=1, source_target_pairs={{0,8},{8,0},{16,24},{24,16},{1,9},{9,1},{17,25},{25,17},{2,10},{10... | collective-permute-start | bytes 1572872 | tf_op jit(solution)/shard_map/ppermute | solution.py:77
  493.9 28.7 %collective-permute-start.97 = (bf16[512,512]{1,0:T(8,128)(2,1)}, bf16[512,512]{1,0:T(8,128)(2,1)}, u32[]{:S(2)}, u32[]{:S(2)}) collective-permute-start(bf16[512,512]{1,0:T(8,128)(2,1)} %add_convert_fusion.24), channel_id=1, source_target_pairs={{8,16},{16,8},{9,17},{17,9},{10,18},{18,10},{11,19},{19,11},{12,20... | collective-permute-start | bytes 1572872 | tf_op jit(solution)/shard_map/ppermute | solution.py:72
  505.3 16.2 %collective-permute-start.90 = (bf16[512,512]{1,0:T(8,128)(2,1)S(1)}, bf16[512,512]{1,0:T(8,128)(2,1)S(1)}, u32[]{:S(2)}, u32[]{:S(2)}) collective-permute-start(bf16[512,512]{1,0:T(8,128)(2,1)S(1)} %get-tuple-element.337), channel_id=1, source_target_pairs={{0,8},{8,0},{16,24},{24,16},{1,9},{9,1},{17,25},{25,17},{2,10},{10... | collective-permute-start | bytes 1572872 | tf_op jit(solution)/shard_map/ppermute | solution.py:77
  520.0 19.1 %collective-permute-start.93 = (bf16[512,512]{1,0:T(8,128)(2,1)}, bf16[512,512]{1,0:T(8,128)(2,1)}, u32[]{:S(2)}, u32[]{:S(2)}) collective-permute-start(bf16[512,512]{1,0:T(8,128)(2,1)} %get-tuple-element.335), channel_id=1, source_target_pairs={{0,8},{8,0},{16,24},{24,16},{1,9},{9,1},{17,25},{25,17},{2,10},{10... | collective-permute-start | bytes 1572872 | tf_op jit(solution)/shard_map/ppermute | solution.py:77
  521.0 18.2 %collective-permute-start.88 = (bf16[512,512]{1,0:T(8,128)(2,1)}, bf16[512,512]{1,0:T(8,128)(2,1)}, u32[]{:S(2)}, u32[]{:S(2)}) collective-permute-start(bf16[512,512]{1,0:T(8,128)(2,1)} %add_convert_fusion.21), channel_id=1, source_target_pairs={{0,4},{4,0},{1,5},{5,1},{2,6},{6,2},{3,7},{7,3},{8,12},{12,8},{9,1... | collective-permute-start | bytes 1572872 | tf_op jit(solution)/shard_map/ppermute | solution.py:44
  525.0 16.6 %collective-permute-start.98 = (bf16[512,512]{1,0:T(8,128)(2,1)}, bf16[512,512]{1,0:T(8,128)(2,1)}, u32[]{:S(2)}, u32[]{:S(2)}) collective-permute-start(bf16[512,512]{1,0:T(8,128)(2,1)} %get-tuple-element.331), channel_id=1, source_target_pairs={{0,8},{8,0},{16,24},{24,16},{1,9},{9,1},{17,25},{25,17},{2,10},{10... | collective-permute-start | bytes 1572872 | tf_op jit(solution)/shard_map/ppermute | solution.py:77
  540.3 28.6 %collective-permute-start.94 = (bf16[512,512]{1,0:T(8,128)(2,1)S(1)}, bf16[512,512]{1,0:T(8,128)(2,1)S(1)}, u32[]{:S(2)}, u32[]{:S(2)}) collective-permute-start(bf16[512,512]{1,0:T(8,128)(2,1)S(1)} %add_convert_fusion.17), channel_id=1, source_target_pairs={{8,16},{16,8},{9,17},{17,9},{10,18},{18,10},{11,19},{19,11},{12,20... | collective-permute-start | bytes 1572872 | tf_op jit(solution)/shard_map/ppermute | solution.py:72
  543.9 17.8 %collective-permute-start.96 = (bf16[512,512]{1,0:T(8,128)(2,1)S(1)}, bf16[512,512]{1,0:T(8,128)(2,1)S(1)}, u32[]{:S(2)}, u32[]{:S(2)}) collective-permute-start(bf16[512,512]{1,0:T(8,128)(2,1)S(1)} %get-tuple-element.333), channel_id=1, source_target_pairs={{0,8},{8,0},{16,24},{24,16},{1,9},{9,1},{17,25},{25,17},{2,10},{10... | collective-permute-start | bytes 1572872 | tf_op jit(solution)/shard_map/ppermute | solution.py:77
  551.3 17.7 %collective-permute-start.103 = (bf16[512,512]{1,0:T(8,128)(2,1)S(1)}, bf16[512,512]{1,0:T(8,128)(2,1)S(1)}, u32[]{:S(2)}, u32[]{:S(2)}) collective-permute-start(bf16[512,512]{1,0:T(8,128)(2,1)S(1)} %get-tuple-element.327), channel_id=1, source_target_pairs={{0,8},{8,0},{16,24},{24,16},{1,9},{9,1},{17,25},{25,17},{2,10},{10... | collective-permute-start | bytes 1572872 | tf_op jit(solution)/shard_map/ppermute | solution.py:77
  561.8 40.9 %collective-permute-start.106 = (bf16[512,512]{1,0:T(8,128)(2,1)S(1)}, bf16[512,512]{1,0:T(8,128)(2,1)S(1)}, u32[]{:S(2)}, u32[]{:S(2)}) collective-permute-start(bf16[512,512]{1,0:T(8,128)(2,1)S(1)} %add_convert_fusion.12), channel_id=1, source_target_pairs={{8,16},{16,8},{9,17},{17,9},{10,18},{18,10},{11,19},{19,11},{12,20... | collective-permute-start | bytes 1572872 | tf_op jit(solution)/shard_map/ppermute | solution.py:72
  572.6 22.5 %collective-permute-start.108 = (bf16[512,512]{1,0:T(8,128)(2,1)S(1)}, bf16[512,512]{1,0:T(8,128)(2,1)S(1)}, u32[]{:S(2)}, u32[]{:S(2)}) collective-permute-start(bf16[512,512]{1,0:T(8,128)(2,1)S(1)} %add_convert_fusion.6), channel_id=1, source_target_pairs={{8,16},{16,8},{9,17},{17,9},{10,18},{18,10},{11,19},{19,11},{12,20... | collective-permute-start | bytes 1572872 | tf_op jit(solution)/shard_map/ppermute | solution.py:72
  573.5 44.6 %collective-permute-start.105 = (bf16[512,512]{1,0:T(8,128)(2,1)S(1)}, bf16[512,512]{1,0:T(8,128)(2,1)S(1)}, u32[]{:S(2)}, u32[]{:S(2)}) collective-permute-start(bf16[512,512]{1,0:T(8,128)(2,1)S(1)} %add_convert_fusion.8.refs_6_), channel_id=1, source_target_pairs={{0,8},{8,0},{16,24},{24,16},{1,9},{9,1},{17,25},{25,17},{2,10},{10... | collective-permute-start | bytes 1572872 | tf_op jit(solution)/shard_map/ppermute | solution.py:77
  585.2 17.8 %collective-permute-start.100 = (bf16[512,512]{1,0:T(8,128)(2,1)S(1)}, bf16[512,512]{1,0:T(8,128)(2,1)S(1)}, u32[]{:S(2)}, u32[]{:S(2)}) collective-permute-start(bf16[512,512]{1,0:T(8,128)(2,1)S(1)} %add_convert_fusion.11), channel_id=1, source_target_pairs={{8,16},{16,8},{9,17},{17,9},{10,18},{18,10},{11,19},{19,11},{12,20... | collective-permute-start | bytes 1572872 | tf_op jit(solution)/shard_map/ppermute | solution.py:72
  595.3 22.9 %collective-permute-start.109 = (bf16[512,512]{1,0:T(8,128)(2,1)S(1)}, bf16[512,512]{1,0:T(8,128)(2,1)S(1)}, u32[]{:S(2)}, u32[]{:S(2)}) collective-permute-start(bf16[512,512]{1,0:T(8,128)(2,1)S(1)} %add_convert_fusion.5.refs_10_), channel_id=1, source_target_pairs={{0,8},{8,0},{16,24},{24,16},{1,9},{9,1},{17,25},{25,17},{2,10},{10... | collective-permute-start | bytes 1572872 | tf_op jit(solution)/shard_map/ppermute | solution.py:77
  602.8 22.5 %collective-permute-start.107 = (bf16[512,512]{1,0:T(8,128)(2,1)S(1)}, bf16[512,512]{1,0:T(8,128)(2,1)S(1)}, u32[]{:S(2)}, u32[]{:S(2)}) collective-permute-start(bf16[512,512]{1,0:T(8,128)(2,1)S(1)} %add_convert_fusion.7.refs_8_), channel_id=1, source_target_pairs={{0,8},{8,0},{16,24},{24,16},{1,9},{9,1},{17,25},{25,17},{2,10},{10... | collective-permute-start | bytes 1572872 | tf_op jit(solution)/shard_map/ppermute | solution.py:77
  603.1 28.5 %collective-permute-start.101 = (bf16[512,512]{1,0:T(8,128)(2,1)S(1)}, bf16[512,512]{1,0:T(8,128)(2,1)S(1)}, u32[]{:S(2)}, u32[]{:S(2)}) collective-permute-start(bf16[512,512]{1,0:T(8,128)(2,1)S(1)} %add_convert_fusion.10), channel_id=1, source_target_pairs={{0,8},{8,0},{16,24},{24,16},{1,9},{9,1},{17,25},{25,17},{2,10},{10... | collective-permute-start | bytes 1572872 | tf_op jit(solution)/shard_map/ppermute | solution.py:77
  (205 other events, 2113.3 us)
Sparse Core Ops, SparseCore 0:
  33.3 38.5 all-gather.6
  73.4 37.4 all-gather.8
  112.5 35.9 all-gather.10
  353.1 81.2 all-gather.14
  435.7 46.4 all-gather.12

commit v3 on v1

--- a/solution.py
+++ b/solution.py
@@ -50,7 +50,7 @@
 
 
 class LineSums:
-    def __init__(self, lag=4):
+    def __init__(self, lag=3):
         self.lag = lag
         self.short = lax.axis_size("dp") == 4
         place = lax.axis_index("dp")

time: 636 us -> 641 us (level)
  starting transfers between devices: 156 us -> 194 us
  waiting for transfers between devices: 172 us -> 138 us
  Pallas kernels: 66.4 us -> 77.7 us
    ppermute x29 -> x28, starting transfers between devices: 88.2 us -> 126 us  [_swap_outer(): lax.ppermute(piece, 'dp', [(0, 1), (1, 0), (2, 3), (3, 2)])]
    ppermute x29 -> x28, waiting for transfers between devices: 81 us -> 53.5 us  [_swap_outer(): lax.ppermute(piece, 'dp', [(0, 1), (1, 0), (2, 3), (3, 2)])]
    pallas_call x2, Pallas kernels: 23.1 us -> 33.1 us  [units_of_half(): pl.pallas_call(units_kernel, grid=(half // block,), out_shape=outs, in_sp...]
    convert_element_type x37 -> x36, other arithmetic: 30.3 us -> 27.6 us  [low(): return array.astype(bf16)]
    select_n x21 -> x22, other arithmetic: 30.8 us -> 30.9 us  [send(): out = jnp.where(self.middle, self.total[which - self.lag], out)]
  transfers between devices with their start and end apart: 115 -> 114, of which waited for: 31 -> 27; matrix products, arithmetic and copies ran while one was open for 30% -> 29% of each run, Pallas kernels for 9% -> 9%
where the time goes in v3:
time: 641 us; the launch traced here: 638 us
  starting transfers between devices  194 us (30%)
  waiting for transfers between devices  138 us (22%)
  matrix products  88.4 us (14%)
  other arithmetic  85.6 us (13%)
  Pallas kernels  77.7 us (12%)
  local copies, waits for them, and re-layouts  37.4 us (6%)
  between operations  16.5 us (3%)
    ppermute x28, starting transfers between devices, _swap_outer(): lax.ppermute(piece, 'dp', [(0, 1), (1, 0), (2, 3), (3, 2)])  126 us
    ppermute x28, waiting for transfers between devices, _swap_outer(): lax.ppermute(piece, 'dp', [(0, 1), (1, 0), (2, 3), (3, 2)])  53.5 us
    ppermute x15, waiting for transfers between devices, swap_y(): return lax.ppermute(block, 'tc', [(i, i ^ 2) for i in range(4)])  40.6 us
    ppermute x14, waiting for transfers between devices, swap_x(): return lax.ppermute(block, 'tr', [(0, 1), (1, 0)])  37.3 us
    dot_general x16, matrix products, contract_rows(): lax.dot_general(left_side, right_side, (((0,), (0,)), ((), ())), preferre...  35.7 us
    pallas_call x2, Pallas kernels, units_of_half(): pl.pallas_call(units_kernel, grid=(half // block,), out_shape=outs, in_sp...  33.1 us
    select_n x22, other arithmetic, send(): out = jnp.where(self.middle, self.total[which - self.lag], out)  30.9 us
    convert_element_type x36, other arithmetic, low(): return array.astype(bf16)  27.6 us
  transfers between devices with their start and end apart: 114, of which 27 were waited for; matrix products, arithmetic and copies ran while one was open for 29% of the time, Pallas kernels for 9%

profile of v3, /device:TPU:0, one launch (start us, length us, event | category | flops | bytes accessed | tf_op | source)
XLA Modules:
  0.0 637.6 jit_solution(7759328883370385932)
XLA Ops:
  9.2 3.0 collective-permute-start
  13.7 3.2 fusion.110
  24.9 3.1 convolution_convert_fusion.5
  32.0 3.6 add_convert_fusion.4
  43.7 3.4 convert_add_fusion.own
  49.2 21.8 %collective-permute-done.8 = f32[1024]{0:T(1024)S(1)} collective-permute-done((f32[1024]{0:T(1024)S(1)}, f32[1024]{0:T(1024)S(1)}, u32[]{:S(2)}, u32[]{:S(2)}) %collective-permute-start.8) | collective-permute-done | bytes 4128 | tf_op jit(solution)/shard_map/ppermute | solution.py:36
  75.5 9.5 %shard_map.237 = (f32[1024,512]{1,0:T(8,128)}, bf16[1024,256]{1,0:T(8,128)(2,1)S(1)}, bf16[1024,128]{1,0:T(8,128)(2,1)S(1)}, bf16[1024,128]{1,0:T(8,128)(2,1)S(1...) custom-call(s32[1]{0:T(128)} %bitcast.side, f32[1024,512]{1,0:T(8,128)} %convert_add_fusion.own, ...), custom_call_target="tpu_custom_call" | custom-call | bytes 1024 | tf_op jit(solution)/shard_map/pallas_call | solution.py:303
  91.8 6.5 %collective-permute-done.10 = bf16[1024,256]{1,0:T(8,128)(2,1)S(1)} collective-permute-done((bf16[1024,256]{1,0:T(8,128)(2,1)S(1)}, bf16[1024,256]{1,0:T(8,128)(2,1)S(1)}, u32[]{:S(2)}, u32[]{:S(2)}) %collective-permute-start.10) | collective-permute-done | bytes 524320 | tf_op jit(solution)/shard_map/ppermute | solution.py:36
  110.0 9.7 %collective-permute-done.14 = bf16[512,512]{1,0:T(8,128)(2,1)} collective-permute-done((bf16[512,512]{1,0:T(8,128)(2,1)S(1)}, bf16[512,512]{1,0:T(8,128)(2,1)}, u32[]{:S(2)}, u32[]{:S(2)}) %collective-permute-start.14) | collective-permute-done | bytes 524320 | tf_op jit(solution)/shard_map/ppermute | solution.py:44
  127.9 8.3 %collective-permute-done.22 = f32[1024]{0:T(1024)S(1)} collective-permute-done((f32[1024]{0:T(1024)S(1)}, f32[1024]{0:T(1024)S(1)}, u32[]{:S(2)}, u32[]{:S(2)}) %collective-permute-start.22) | collective-permute-done | bytes 4128 | tf_op jit(solution)/shard_map/ppermute | solution.py:36
  144.8 2.5 all-gather.11.cloned.1.call-done.refs_7_
  148.4 11.4 %shard_map.238 = (bf16[1024,768]{1,0:T(8,128)(2,1)}, bf16[1024,1536]{1,0:T(8,128)(2,1)}, bf16[1024,1536]{1,0:T(8,128)(2,1)}, f32[1024,1]{1,0:T(8,128)S(1)}) custom-call(bf16[512,512]{1,0:T(8,128)(2,1)S(1)} %multiply_convert_fusion.2.refs_0_, bf16[512,512]{1,0:T(8,128)(2,1)} %collective-permute-done.28.refs_1_, bf16[512,512]{1,0:T(8,128)(2,1)S(1)} %copy-done.24, ...), custom_call_target="tpu_custom_call" | custom-call | bytes 1024 | tf_op jit(solution)/shard_map/pallas_call | solution.py:377
  163.8 21.7 %shard_map.239 = (bf16[1024,768]{1,0:T(8,128)(2,1)}, bf16[1024,1536]{1,0:T(8,128)(2,1)}, bf16[1024,1536]{1,0:T(8,128)(2,1)}, f32[1024,1]{1,0:T(8,128)S(1)}) custom-call(bf16[512,512]{1,0:T(8,128)(2,1)} %collective-permute-done.18.refs_0_, ...), custom_call_target="tpu_custom_call", output_to_operand_aliasing={{0}: (17, {}), {1}: (18, {}), {2}: (19, {}), {3}: (20, {})} | custom-call | bytes 1024 | tf_op jit(solution)/shard_map/pallas_call | solution.py:377
  185.5 4.0 convolution_convert_fusion.1
  191.5 2.8 convolution_convert_fusion.2
  194.9 5.1 convolution_convert_fusion.3
  201.9 4.3 fusion.109
  206.2 3.1 add_convert_fusion.2
  212.9 4.2 convolution_convert_fusion
  229.7 3.0 collective-permute-done.37
  244.3 2.4 collective-permute-done.39
  246.6 2.4 collective-permute-start.49
  252.6 10.1 %collective-permute-done.43 = bf16[512,512]{1,0:T(8,128)(2,1)S(1)} collective-permute-done((bf16[512,512]{1,0:T(8,128)(2,1)S(1)}, bf16[512,512]{1,0:T(8,128)(2,1)S(1)}, u32[]{:S(2)}, u32[]{:S(2)}) %collective-permute-start.43) | collective-permute-done | bytes 524320 | tf_op jit(solution)/shard_map/ppermute | solution.py:44
  268.8 12.4 %collective-permute-start.57 = (bf16[512,512]{1,0:T(8,128)(2,1)S(1)}, bf16[512,512]{1,0:T(8,128)(2,1)S(1)}, u32[]{:S(2)}, u32[]{:S(2)}) collective-permute-start(bf16[512,512]{1,0:T(8,128)(2,1)S(1)} %get-tuple-element.363), channel_id=1, source_target_pairs={{0,8},{8,0},{16,24},{24,16},{1,9},{9,1},{17,25},{25,17},{2,10},{10... | collective-permute-start | bytes 1572872 | tf_op jit(solution)/shard_map/ppermute | solution.py:77
  286.7 5.6 collective-permute-start.59
  296.7 12.9 %shard_map.240 = (bf16[1024,512]{1,0:T(8,128)(2,1)}, f32[1,128]{1,0:T(1,128)S(1)}, f32[1,128]{1,0:T(1,128)S(1)}, f32[1024,1]{1,0:T(8,128)S(1)}) custom-call(s32[1]{0:T(128)} %bitcast.side, f32[1024,256]{1,0:T(8,128)} %convert_add_fusion.1.own, bf16[1024,256]{1,0:T(8,128)(2,1)S(1)} %collective-permute-done.51.from_y, f32[1024,512]{1,0:T(8,128)} %get-tuple-element.240.proj, ...), custom_call_target="tpu_custom_call" | custom-call | bytes 1024 | tf_op jit(solution)/shard_map/pallas_call | solution.py:303
  316.8 10.7 %collective-permute-start.61 = (bf16[512,512]{1,0:T(8,128)(2,1)S(1)}, bf16[512,512]{1,0:T(8,128)(2,1)S(1)}, u32[]{:S(2)}, u32[]{:S(2)}) collective-permute-start(bf16[512,512]{1,0:T(8,128)(2,1)S(1)} %get-tuple-element.357), channel_id=1, source_target_pairs={{0,8},{8,0},{16,24},{24,16},{1,9},{9,1},{17,25},{25,17},{2,10},{10... | collective-permute-start | bytes 1572872 | tf_op jit(solution)/shard_map/ppermute | solution.py:77
  330.3 8.4 %collective-permute-done.61.refs_5_ = bf16[512,512]{1,0:T(8,128)(2,1)S(1)} collective-permute-done((bf16[512,512]{1,0:T(8,128)(2,1)S(1)}, bf16[512,512]{1,0:T(8,128)(2,1)S(1)}, u32[]{:S(2)}, u32[]{:S(2)}) %collective-permute-start.61) | collective-permute-done | bytes 524320 | tf_op jit(solution)/shard_map/ppermute | solution.py:77
  342.0 2.8 multiply_convert_fusion
  344.8 3.3 fusion.40
  350.7 7.8 %collective-permute-start.70 = (bf16[512,512]{1,0:T(8,128)(2,1)S(1)}, bf16[512,512]{1,0:T(8,128)(2,1)S(1)}, u32[]{:S(2)}, u32[]{:S(2)}) collective-permute-start(bf16[512,512]{1,0:T(8,128)(2,1)S(1)} %copy-done.140), channel_id=1, source_target_pairs={{0,8},{8,0},{16,24},{24,16},{1,9},{9,1},{17,25},{25,17},{2,10},{10... | collective-permute-start | bytes 1572872 | tf_op jit(solution)/shard_map/ppermute | solution.py:77
  372.8 2.8 convolution_convert_fusion.10
  379.1 2.7 collective-permute-start.72
  381.8 9.8 %collective-permute-done.69 = f32[1792]{0:T(1024)S(1)} collective-permute-done((f32[1792]{0:T(1024)S(1)}, f32[1792]{0:T(1024)S(1)}, u32[]{:S(2)}, u32[]{:S(2)}) %collective-permute-start.69) | collective-permute-done | bytes 7200 | tf_op jit(solution)/shard_map/ppermute | solution.py:44
  399.2 9.5 %collective-permute-done.76.refs_1_ = bf16[512,512]{1,0:T(8,128)(2,1)S(1)} collective-permute-done((bf16[512,512]{1,0:T(8,128)(2,1)}, bf16[512,512]{1,0:T(8,128)(2,1)S(1)}, u32[]{:S(2)}, u32[]{:S(2)}) %collective-permute-start.76) | collective-permute-done | bytes 524320 | tf_op jit(solution)/shard_map/ppermute | solution.py:77
  412.3 2.6 broadcast_select_fusion.11
  414.9 3.1 collective-permute-start.77
  419.2 8.7 %collective-permute-start.79 = (bf16[512,512]{1,0:T(8,128)(2,1)}, bf16[512,512]{1,0:T(8,128)(2,1)}, u32[]{:S(2)}, u32[]{:S(2)}) collective-permute-start(bf16[512,512]{1,0:T(8,128)(2,1)} %get-tuple-element.345), channel_id=1, source_target_pairs={{0,8},{8,0},{16,24},{24,16},{1,9},{9,1},{17,25},{25,17},{2,10},{10... | collective-permute-start | bytes 1572872 | tf_op jit(solution)/shard_map/ppermute | solution.py:77
  428.6 4.0 fusion.13
  433.9 4.0 fusion.10
  443.6 3.8 collective-permute-start.82
  449.5 10.8 %collective-permute-start.85 = (bf16[512,512]{1,0:T(8,128)(2,1)}, bf16[512,512]{1,0:T(8,128)(2,1)}, u32[]{:S(2)}, u32[]{:S(2)}) collective-permute-start(bf16[512,512]{1,0:T(8,128)(2,1)} %get-tuple-element.339), channel_id=1, source_target_pairs={{0,8},{8,0},{16,24},{24,16},{1,9},{9,1},{17,25},{25,17},{2,10},{10... | collective-permute-start | bytes 1572872 | tf_op jit(solution)/shard_map/ppermute | solution.py:77
  462.6 7.7 %collective-permute-start.83 = (bf16[512,512]{1,0:T(8,128)(2,1)}, bf16[512,512]{1,0:T(8,128)(2,1)}, u32[]{:S(2)}, u32[]{:S(2)}) collective-permute-start(bf16[512,512]{1,0:T(8,128)(2,1)} %get-tuple-element.341), channel_id=1, source_target_pairs={{0,8},{8,0},{16,24},{24,16},{1,9},{9,1},{17,25},{25,17},{2,10},{10... | collective-permute-start | bytes 1572872 | tf_op jit(solution)/shard_map/ppermute | solution.py:77
  478.3 3.8 collective-permute-done.83.refs_7_
  485.7 5.0 fusion.28
  495.5 3.8 collective-permute-start.88
  505.1 4.7 collective-permute-done.88.refs_13_
  511.0 2.2 broadcast_select_fusion.5
  513.2 3.3 collective-permute-start.91
  516.5 2.2 broadcast_select_fusion.3
  520.7 8.7 %collective-permute-done.91.refs_15_ = bf16[512,512]{1,0:T(8,128)(2,1)S(1)} collective-permute-done((bf16[512,512]{1,0:T(8,128)(2,1)S(1)}, bf16[512,512]{1,0:T(8,128)(2,1)S(1)}, u32[]{:S(2)}, u32[]{:S(2)}) %collective-permute-start.91) | collective-permute-done | bytes 524320 | tf_op jit(solution)/shard_map/ppermute | solution.py:77
  532.6 8.0 %collective-permute-done.96.refs_17_ = bf16[512,512]{1,0:T(8,128)(2,1)S(1)} collective-permute-done((bf16[512,512]{1,0:T(8,128)(2,1)S(1)}, bf16[512,512]{1,0:T(8,128)(2,1)S(1)}, u32[]{:S(2)}, u32[]{:S(2)}) %collective-permute-start.96) | collective-permute-done | bytes 524320 | tf_op jit(solution)/shard_map/ppermute | solution.py:77
  542.1 6.1 collective-permute-done.94.refs_19_
  550.6 7.4 %collective-permute-start.104 = (bf16[512,512]{1,0:T(8,128)(2,1)}, bf16[512,512]{1,0:T(8,128)(2,1)}, u32[]{:S(2)}, u32[]{:S(2)}) collective-permute-start(bf16[512,512]{1,0:T(8,128)(2,1)} %get-tuple-element.325), channel_id=1, source_target_pairs={{0,8},{8,0},{16,24},{24,16},{1,9},{9,1},{17,25},{25,17},{2,10},{10... | collective-permute-start | bytes 1572872 | tf_op jit(solution)/shard_map/ppermute | solution.py:77
  559.2 6.7 %collective-permute-start.99 = (bf16[512,512]{1,0:T(8,128)(2,1)}, bf16[512,512]{1,0:T(8,128)(2,1)}, u32[]{:S(2)}, u32[]{:S(2)}) collective-permute-start(bf16[512,512]{1,0:T(8,128)(2,1)} %get-tuple-element.329), channel_id=1, source_target_pairs={{0,8},{8,0},{16,24},{24,16},{1,9},{9,1},{17,25},{25,17},{2,10},{10... | collective-permute-start | bytes 1572872 | tf_op jit(solution)/shard_map/ppermute | solution.py:77
  569.5 3.7 shard_map.242
  573.2 4.3 shard_map.241
  581.8 2.3 collective-permute-start.100
  587.8 9.0 %shard_map.243 = (f32[512,3072]{1,0:T(8,128)}, f32[512,3072]{1,0:T(8,128)}) custom-call(s32[5]{0:T(128)S(1)} %stack.39.words, bf16[512,512]{1,0:T(8,128)(2,1)S(1)} %copy-done.10, bf16[512,512]{1,0:T(8,128)(2,1)S(1)} %collective-permute-done.49.refs_1_, bf16[512,512]{1,0:T(8,128)(2,1)S(1)} %copy-done.12, bf16[512,512]{1,0:T(8,128)(2,1)S(1)} %copy-done.3, ...), custom_call_target="tpu_custom_call" | custom-call | bytes 1024 | tf_op jit(solution)/shard_map/pallas_call | solution.py:416
  598.0 6.9 %collective-permute-start.108 = (bf16[512,512]{1,0:T(8,128)(2,1)S(1)}, bf16[512,512]{1,0:T(8,128)(2,1)S(1)}, u32[]{:S(2)}, u32[]{:S(2)}) collective-permute-start(bf16[512,512]{1,0:T(8,128)(2,1)S(1)} %add_convert_fusion.5.refs_10_), channel_id=1, source_target_pairs={{0,8},{8,0},{16,24},{24,16},{1,9},{9,1},{17,25},{25,17},{2,10},{10... | collective-permute-start | bytes 1572872 | tf_op jit(solution)/shard_map/ppermute | solution.py:77
  605.0 2.9 collective-permute-start.106
  608.1 5.5 collective-permute-start.102
  620.6 2.7 collective-permute-done.106.refs_9_
  624.1 5.3 shard_map.244
  (647 shorter events, 234.3 us)
Async XLA Ops:
  7.2 91.3 %all-gather.7.cloned.1.call-start = ((), (), s32[]{:S(2)}) async-start(), calls=%async_computation | async-start | bytes 1966080 | tf_op jit(solution)/shard_map/all_gather | solution.py:481
  28.0 15.2 %collective-permute-start.2 = (bf16[1024,512]{1,0:T(8,128)(2,1)}, bf16[1024,512]{1,0:T(8,128)(2,1)}, u32[]{:S(2)}, u32[]{:S(2)}) collective-permute-start(bf16[1024,512]{1,0:T(8,128)(2,1)} %convolution_convert_fusion.5), channel_id=1, source_target_pairs={{0,1},{1,0},{2,3},{3,2},{4,5},{5,4},{6,7},{7,6},{8,9},{9,8},{10,11... | collective-permute-start | bytes 3145736 | tf_op jit(solution)/shard_map/ppermute | solution.py:32
  28.3 42.7 %collective-permute-start.5 = (bf16[128,1536]{1,0:T(8,128)(2,1)}, bf16[128,1536]{1,0:T(8,128)(2,1)}, u32[]{:S(2)}, u32[]{:S(2)}) collective-permute-start(bf16[128,1536]{1,0:T(8,128)(2,1)} %pad_maximum_fusion.19), channel_id=1, source_target_pairs={{0,2},{1,3},{2,0},{3,1},{4,6},{5,7},{6,4},{7,5},{8,10},{9,11},{10,... | collective-permute-start | bytes 1179656 | tf_op jit(solution)/shard_map/ppermute | solution.py:36
  30.0 41.0 %collective-permute-start.6 = (bf16[128,1536]{1,0:T(8,128)(2,1)}, bf16[128,1536]{1,0:T(8,128)(2,1)}, u32[]{:S(2)}, u32[]{:S(2)}) collective-permute-start(bf16[128,1536]{1,0:T(8,128)(2,1)} %pad_maximum_fusion.20), channel_id=1, source_target_pairs={{0,3},{1,2},{2,1},{3,0},{4,7},{5,6},{6,5},{7,4},{8,11},{9,10},{10,... | collective-permute-start | bytes 1179656 | tf_op jit(solution)/shard_map/ppermute | solution.py:40
  32.0 87.8 %all-gather.9.cloned.1.call-start = ((), (), s32[]{:S(2)}) async-start(), calls=%async_computation.1 | async-start | bytes 1966080 | tf_op jit(solution)/shard_map/all_gather | solution.py:523
  35.6 35.5 %collective-permute-start.4 = (bf16[1024,512]{1,0:T(8,128)(2,1)}, bf16[1024,512]{1,0:T(8,128)(2,1)}, u32[]{:S(2)}, u32[]{:S(2)}) collective-permute-start(bf16[1024,512]{1,0:T(8,128)(2,1)} %add_convert_fusion.4), channel_id=1, source_target_pairs={{0,2},{1,3},{2,0},{3,1},{4,6},{5,7},{6,4},{7,5},{8,10},{9,11},{10,... | collective-permute-start | bytes 3145736 | tf_op jit(solution)/shard_map/ppermute | solution.py:36
  48.5 22.5 %collective-permute-start.8 = (f32[1024]{0:T(1024)S(1)}, f32[1024]{0:T(1024)S(1)}, u32[]{:S(2)}, u32[]{:S(2)}) collective-permute-start(f32[1024]{0:T(1024)S(1)} %add.390), channel_id=1, source_target_pairs={{0,2},{1,3},{2,0},{3,1},{4,6},{5,7},{6,4},{7,5},{8,10},{9,11},{10,... | collective-permute-start | bytes 12296 | tf_op jit(solution)/shard_map/ppermute | solution.py:36
  71.1 76.3 %all-gather.11.cloned.1.call-start = ((), (), s32[]{:S(2)}) async-start(), calls=%async_computation.2 | async-start | bytes 1966080 | tf_op jit(solution)/shard_map/all_gather | solution.py:523
  88.0 22.1 %collective-permute-start.16 = (bf16[512,1536]{1,0:T(8,128)(2,1)}, bf16[512,1536]{1,0:T(8,128)(2,1)}, u32[]{:S(2)}, u32[]{:S(2)}) collective-permute-start(bf16[512,1536]{1,0:T(8,128)(2,1)} %pad_maximum_fusion), channel_id=1, source_target_pairs={{0,1},{1,0},{2,3},{3,2},{4,5},{5,4},{6,7},{7,6},{8,9},{9,8},{10,11... | collective-permute-start | bytes 4718600 | tf_op jit(solution)/shard_map/ppermute | solution.py:32
  88.0 21.9 %collective-permute-start.17 = (bf16[768,512]{1,0:T(8,128)(2,1)}, bf16[768,512]{1,0:T(8,128)(2,1)}, u32[]{:S(2)}, u32[]{:S(2)}) collective-permute-start(bf16[768,512]{1,0:T(8,128)(2,1)} %get-tuple-element.374), channel_id=1, source_target_pairs={{0,1},{1,0},{2,3},{3,2},{4,5},{5,4},{6,7},{7,6},{8,9},{9,8},{10,11... | collective-permute-start | bytes 2359304 | tf_op jit(solution)/shard_map/ppermute | solution.py:32
  100.6 328.0 %all-gather.15.cloned.1.call-start = ((), (), s32[]{:S(2)}) async-start(), calls=%async_computation.4 | async-start | bytes 15728640 | tf_op jit(solution)/shard_map/all_gather | solution.py:647
  101.0 35.2 %collective-permute-start.23 = (bf16[512,512]{1,0:T(8,128)(2,1)}, bf16[512,512]{1,0:T(8,128)(2,1)}, u32[]{:S(2)}, u32[]{:S(2)}) collective-permute-start(bf16[512,512]{1,0:T(8,128)(2,1)} %collective-permute-done.11.refs_10_), channel_id=1, source_target_pairs={{0,1},{1,0},{2,3},{3,2},{4,5},{5,4},{6,7},{7,6},{8,9},{9,8},{10,11... | collective-permute-start | bytes 1572872 | tf_op jit(solution)/shard_map/ppermute | solution.py:32
  109.9 26.3 %collective-permute-start.24 = (bf16[512,512]{1,0:T(8,128)(2,1)}, bf16[512,512]{1,0:T(8,128)(2,1)}, u32[]{:S(2)}, u32[]{:S(2)}) collective-permute-start(bf16[512,512]{1,0:T(8,128)(2,1)} %collective-permute-done.12.refs_10_), channel_id=1, source_target_pairs={{0,1},{1,0},{2,3},{3,2},{4,5},{5,4},{6,7},{7,6},{8,9},{9,8},{10,11... | collective-permute-start | bytes 1572872 | tf_op jit(solution)/shard_map/ppermute | solution.py:32
  136.8 23.0 %collective-permute-start.27 = (bf16[512,512]{1,0:T(8,128)(2,1)}, bf16[512,512]{1,0:T(8,128)(2,1)}, u32[]{:S(2)}, u32[]{:S(2)}) collective-permute-start(bf16[512,512]{1,0:T(8,128)(2,1)} %collective-permute-done.18.refs_0_), channel_id=1, source_target_pairs={{0,1},{1,0},{2,3},{3,2},{4,5},{5,4},{6,7},{7,6},{8,9},{9,8},{10,11... | collective-permute-start | bytes 1572872 | tf_op jit(solution)/shard_map/ppermute | solution.py:32
  139.3 20.5 %collective-permute-start.25 = (bf16[256,512]{1,0:T(8,128)(2,1)}, bf16[256,512]{1,0:T(8,128)(2,1)}, u32[]{:S(2)}, u32[]{:S(2)}) collective-permute-start(bf16[256,512]{1,0:T(8,128)(2,1)} %slice.164), channel_id=1, source_target_pairs={{0,2},{1,3},{2,0},{3,1},{4,6},{5,7},{6,4},{7,5},{8,10},{9,11},{10,... | collective-permute-start | bytes 786440 | tf_op jit(solution)/shard_map/ppermute | solution.py:36
  141.0 18.8 %collective-permute-start.26 = (bf16[256,512]{1,0:T(8,128)(2,1)}, bf16[256,512]{1,0:T(8,128)(2,1)}, u32[]{:S(2)}, u32[]{:S(2)}) collective-permute-start(bf16[256,512]{1,0:T(8,128)(2,1)} %slice.165), channel_id=1, source_target_pairs={{0,4},{4,0},{1,5},{5,1},{2,6},{6,2},{3,7},{7,3},{8,12},{12,8},{9,1... | collective-permute-start | bytes 786440 | tf_op jit(solution)/shard_map/ppermute | solution.py:44
  194.4 32.6 %collective-permute-start.35 = (bf16[512,512]{1,0:T(8,128)(2,1)}, bf16[512,512]{1,0:T(8,128)(2,1)}, u32[]{:S(2)}, u32[]{:S(2)}) collective-permute-start(bf16[512,512]{1,0:T(8,128)(2,1)} %get-tuple-element.209), channel_id=1, source_target_pairs={{0,8},{8,0},{16,24},{24,16},{1,9},{9,1},{17,25},{25,17},{2,10},{10... | collective-permute-start | bytes 1572872 | tf_op jit(solution)/shard_map/ppermute | solution.py:77
  200.1 36.5 %collective-permute-start.41 = (bf16[512,512]{1,0:T(8,128)(2,1)}, bf16[512,512]{1,0:T(8,128)(2,1)}, u32[]{:S(2)}, u32[]{:S(2)}) collective-permute-start(bf16[512,512]{1,0:T(8,128)(2,1)} %get-tuple-element.218), channel_id=1, source_target_pairs={{0,8},{8,0},{16,24},{24,16},{1,9},{9,1},{17,25},{25,17},{2,10},{10... | collective-permute-start | bytes 1572872 | tf_op jit(solution)/shard_map/ppermute | solution.py:77
  232.7 33.9 %collective-permute-start.52 = (bf16[512,1536]{1,0:T(8,128)(2,1)S(1)}, bf16[512,1536]{1,0:T(8,128)(2,1)S(1)}, u32[]{:S(2)}, u32[]{:S(2)}) collective-permute-start(bf16[512,1536]{1,0:T(8,128)(2,1)S(1)} %copy-done.144), channel_id=1, source_target_pairs={{0,1},{1,0},{2,3},{3,2},{4,5},{5,4},{6,7},{7,6},{8,9},{9,8},{10,11... | collective-permute-start | bytes 4718600 | tf_op jit(solution)/shard_map/ppermute | solution.py:32
  235.0 16.5 %collective-permute-start.44 = (bf16[512,512]{1,0:T(8,128)(2,1)S(1)}, bf16[512,512]{1,0:T(8,128)(2,1)S(1)}, u32[]{:S(2)}, u32[]{:S(2)}) collective-permute-start(bf16[512,512]{1,0:T(8,128)(2,1)S(1)} %copy-done.88), channel_id=1, source_target_pairs={{0,8},{8,0},{16,24},{24,16},{1,9},{9,1},{17,25},{25,17},{2,10},{10... | collective-permute-start | bytes 1572872 | tf_op jit(solution)/shard_map/ppermute | solution.py:77
  246.6 20.2 %collective-permute-start.49 = (bf16[512,512]{1,0:T(8,128)(2,1)S(1)}, bf16[512,512]{1,0:T(8,128)(2,1)S(1)}, u32[]{:S(2)}, u32[]{:S(2)}) collective-permute-start(bf16[512,512]{1,0:T(8,128)(2,1)S(1)} %get-tuple-element.369), channel_id=1, source_target_pairs={{0,8},{8,0},{16,24},{24,16},{1,9},{9,1},{17,25},{25,17},{2,10},{10... | collective-permute-start | bytes 1572872 | tf_op jit(solution)/shard_map/ppermute | solution.py:77
  263.9 19.3 %collective-permute-start.53 = (bf16[512,512]{1,0:T(8,128)(2,1)S(1)}, bf16[512,512]{1,0:T(8,128)(2,1)S(1)}, u32[]{:S(2)}, u32[]{:S(2)}) collective-permute-start(bf16[512,512]{1,0:T(8,128)(2,1)S(1)} %get-tuple-element.365), channel_id=1, source_target_pairs={{0,8},{8,0},{16,24},{24,16},{1,9},{9,1},{17,25},{25,17},{2,10},{10... | collective-permute-start | bytes 1572872 | tf_op jit(solution)/shard_map/ppermute | solution.py:77
  266.6 17.6 %collective-permute-start.47 = (bf16[1024,256]{1,0:T(8,128)(2,1)S(1)}, bf16[1024,256]{1,0:T(8,128)(2,1)S(1)}, u32[]{:S(2)}, u32[]{:S(2)}) collective-permute-start(bf16[1024,256]{1,0:T(8,128)(2,1)S(1)} %convolution_convert_fusion.9), channel_id=1, source_target_pairs={{0,1},{1,0},{2,3},{3,2},{4,5},{5,4},{6,7},{7,6},{8,9},{9,8},{10,11... | collective-permute-start | bytes 1572872 | tf_op jit(solution)/shard_map/ppermute | solution.py:32
  267.0 18.7 %collective-permute-start.54 = (bf16[512,512]{1,0:T(8,128)(2,1)S(1)}, bf16[512,512]{1,0:T(8,128)(2,1)S(1)}, u32[]{:S(2)}, u32[]{:S(2)}) collective-permute-start(bf16[512,512]{1,0:T(8,128)(2,1)S(1)} %add_convert_fusion.51), channel_id=1, source_target_pairs={{8,16},{16,8},{9,17},{17,9},{10,18},{18,10},{11,19},{19,11},{12,20... | collective-permute-start | bytes 1572872 | tf_op jit(solution)/shard_map/ppermute | solution.py:72
  268.8 40.7 %collective-permute-start.57 = (bf16[512,512]{1,0:T(8,128)(2,1)S(1)}, bf16[512,512]{1,0:T(8,128)(2,1)S(1)}, u32[]{:S(2)}, u32[]{:S(2)}) collective-permute-start(bf16[512,512]{1,0:T(8,128)(2,1)S(1)} %get-tuple-element.363), channel_id=1, source_target_pairs={{0,8},{8,0},{16,24},{24,16},{1,9},{9,1},{17,25},{25,17},{2,10},{10... | collective-permute-start | bytes 1572872 | tf_op jit(solution)/shard_map/ppermute | solution.py:77
  281.7 15.0 %collective-permute-start.51 = (bf16[1024,256]{1,0:T(8,128)(2,1)S(1)}, bf16[1024,256]{1,0:T(8,128)(2,1)S(1)}, u32[]{:S(2)}, u32[]{:S(2)}) collective-permute-start(bf16[1024,256]{1,0:T(8,128)(2,1)S(1)} %add_convert_fusion.49), channel_id=1, source_target_pairs={{0,2},{1,3},{2,0},{3,1},{4,6},{5,7},{6,4},{7,5},{8,10},{9,11},{10,... | collective-permute-start | bytes 1572872 | tf_op jit(solution)/shard_map/ppermute | solution.py:36
  283.3 28.6 %collective-permute-start.60 = (bf16[512,512]{1,0:T(8,128)(2,1)S(1)}, bf16[512,512]{1,0:T(8,128)(2,1)S(1)}, u32[]{:S(2)}, u32[]{:S(2)}) collective-permute-start(bf16[512,512]{1,0:T(8,128)(2,1)S(1)} %add_convert_fusion.48), channel_id=1, source_target_pairs={{8,16},{16,8},{9,17},{17,9},{10,18},{18,10},{11,19},{19,11},{12,20... | collective-permute-start | bytes 1572872 | tf_op jit(solution)/shard_map/ppermute | solution.py:72
  286.7 28.1 %collective-permute-start.59 = (bf16[512,512]{1,0:T(8,128)(2,1)S(1)}, bf16[512,512]{1,0:T(8,128)(2,1)S(1)}, u32[]{:S(2)}, u32[]{:S(2)}) collective-permute-start(bf16[512,512]{1,0:T(8,128)(2,1)S(1)} %get-tuple-element.361), channel_id=1, source_target_pairs={{0,8},{8,0},{16,24},{24,16},{1,9},{9,1},{17,25},{25,17},{2,10},{10... | collective-permute-start | bytes 1572872 | tf_op jit(solution)/shard_map/ppermute | solution.py:77
  310.4 30.4 %collective-permute-start.55 = (bf16[1024,512]{1,0:T(8,128)(2,1)}, bf16[1024,512]{1,0:T(8,128)(2,1)S(1)}, u32[]{:S(2)}, u32[]{:S(2)}) collective-permute-start(bf16[1024,512]{1,0:T(8,128)(2,1)} %get-tuple-element.248), channel_id=1, source_target_pairs={{0,2},{1,3},{2,0},{3,1},{4,6},{5,7},{6,4},{7,5},{8,10},{9,11},{10,... | collective-permute-start | bytes 3145736 | tf_op jit(solution)/shard_map/ppermute | solution.py:36
  311.9 28.9 %collective-permute-start.56 = (bf16[1024,512]{1,0:T(8,128)(2,1)}, bf16[1024,512]{1,0:T(8,128)(2,1)}, u32[]{:S(2)}, u32[]{:S(2)}) collective-permute-start(bf16[1024,512]{1,0:T(8,128)(2,1)} %get-tuple-element.248), channel_id=1, source_target_pairs={{0,1},{1,0},{2,3},{3,2},{4,5},{5,4},{6,7},{7,6},{8,9},{9,8},{10,11... | collective-permute-start | bytes 3145736 | tf_op jit(solution)/shard_map/ppermute | solution.py:32
  316.8 21.9 %collective-permute-start.61 = (bf16[512,512]{1,0:T(8,128)(2,1)S(1)}, bf16[512,512]{1,0:T(8,128)(2,1)S(1)}, u32[]{:S(2)}, u32[]{:S(2)}) collective-permute-start(bf16[512,512]{1,0:T(8,128)(2,1)S(1)} %get-tuple-element.357), channel_id=1, source_target_pairs={{0,8},{8,0},{16,24},{24,16},{1,9},{9,1},{17,25},{25,17},{2,10},{10... | collective-permute-start | bytes 1572872 | tf_op jit(solution)/shard_map/ppermute | solution.py:77
  341.8 143.8 %all-gather.13.cloned.1.call-start = ((), (), s32[]{:S(2)}) async-start(), calls=%async_computation.3 | async-start | bytes 7864320 | tf_op jit(solution)/shard_map/all_gather | solution.py:663
  341.9 21.5 %collective-permute-start.65 = (bf16[1024,512]{1,0:T(8,128)(2,1)}, bf16[1024,512]{1,0:T(8,128)(2,1)}, u32[]{:S(2)}, u32[]{:S(2)}) collective-permute-start(bf16[1024,512]{1,0:T(8,128)(2,1)} %copy-done.115), channel_id=1, source_target_pairs={{0,1},{1,0},{2,3},{3,2},{4,5},{5,4},{6,7},{7,6},{8,9},{9,8},{10,11... | collective-permute-start | bytes 3145736 | tf_op jit(solution)/shard_map/ppermute | solution.py:32
  350.7 26.5 %collective-permute-start.70 = (bf16[512,512]{1,0:T(8,128)(2,1)S(1)}, bf16[512,512]{1,0:T(8,128)(2,1)S(1)}, u32[]{:S(2)}, u32[]{:S(2)}) collective-permute-start(bf16[512,512]{1,0:T(8,128)(2,1)S(1)} %copy-done.140), channel_id=1, source_target_pairs={{0,8},{8,0},{16,24},{24,16},{1,9},{9,1},{17,25},{25,17},{2,10},{10... | collective-permute-start | bytes 1572872 | tf_op jit(solution)/shard_map/ppermute | solution.py:77
  358.5 19.5 %collective-permute-start.71 = (bf16[512,512]{1,0:T(8,128)(2,1)S(1)}, bf16[512,512]{1,0:T(8,128)(2,1)S(1)}, u32[]{:S(2)}, u32[]{:S(2)}) collective-permute-start(bf16[512,512]{1,0:T(8,128)(2,1)S(1)} %copy-done.92), channel_id=1, source_target_pairs={{8,16},{16,8},{9,17},{17,9},{10,18},{18,10},{11,19},{19,11},{12,20... | collective-permute-start | bytes 1572872 | tf_op jit(solution)/shard_map/ppermute | solution.py:72
  359.2 34.1 %collective-permute-start.73 = (bf16[512,512]{1,0:T(8,128)(2,1)S(1)}, bf16[512,512]{1,0:T(8,128)(2,1)S(1)}, u32[]{:S(2)}, u32[]{:S(2)}) collective-permute-start(bf16[512,512]{1,0:T(8,128)(2,1)S(1)} %copy-done.139), channel_id=1, source_target_pairs={{0,8},{8,0},{16,24},{24,16},{1,9},{9,1},{17,25},{25,17},{2,10},{10... | collective-permute-start | bytes 1572872 | tf_op jit(solution)/shard_map/ppermute | solution.py:77
  366.4 25.2 %collective-permute-start.68 = (bf16[1024,512]{1,0:T(8,128)(2,1)S(1)}, bf16[1024,512]{1,0:T(8,128)(2,1)S(1)}, u32[]{:S(2)}, u32[]{:S(2)}) collective-permute-start(bf16[1024,512]{1,0:T(8,128)(2,1)S(1)} %add_convert_fusion.1), channel_id=1, source_target_pairs={{0,4},{4,0},{1,5},{5,1},{2,6},{6,2},{3,7},{7,3},{8,12},{12,8},{9,1... | collective-permute-start | bytes 3145736 | tf_op jit(solution)/shard_map/ppermute | solution.py:44
  375.6 16.0 %collective-permute-start.69 = (f32[1792]{0:T(1024)S(1)}, f32[1792]{0:T(1024)S(1)}, u32[]{:S(2)}, u32[]{:S(2)}) collective-permute-start(f32[1792]{0:T(1024)S(1)} %pad_maximum_fusion.38), channel_id=1, source_target_pairs={{0,4},{4,0},{1,5},{5,1},{2,6},{6,2},{3,7},{7,3},{8,12},{12,8},{9,1... | collective-permute-start | bytes 21512 | tf_op jit(solution)/shard_map/ppermute | solution.py:44
  377.3 17.0 %collective-permute-start.75 = (bf16[512,512]{1,0:T(8,128)(2,1)S(1)}, bf16[512,512]{1,0:T(8,128)(2,1)S(1)}, u32[]{:S(2)}, u32[]{:S(2)}) collective-permute-start(bf16[512,512]{1,0:T(8,128)(2,1)S(1)} %add_convert_fusion.38), channel_id=1, source_target_pairs={{8,16},{16,8},{9,17},{17,9},{10,18},{18,10},{11,19},{19,11},{12,20... | collective-permute-start | bytes 1572872 | tf_op jit(solution)/shard_map/ppermute | solution.py:72
  379.1 16.9 %collective-permute-start.72 = (bf16[512,512]{1,0:T(8,128)(2,1)S(1)}, bf16[512,512]{1,0:T(8,128)(2,1)S(1)}, u32[]{:S(2)}, u32[]{:S(2)}) collective-permute-start(bf16[512,512]{1,0:T(8,128)(2,1)S(1)} %get-tuple-element.351), channel_id=1, source_target_pairs={{0,8},{8,0},{16,24},{24,16},{1,9},{9,1},{17,25},{25,17},{2,10},{10... | collective-permute-start | bytes 1572872 | tf_op jit(solution)/shard_map/ppermute | solution.py:77
  396.9 15.4 %collective-permute-start.74 = (bf16[512,512]{1,0:T(8,128)(2,1)}, bf16[512,512]{1,0:T(8,128)(2,1)}, u32[]{:S(2)}, u32[]{:S(2)}) collective-permute-start(bf16[512,512]{1,0:T(8,128)(2,1)} %add_convert_fusion.35), channel_id=1, source_target_pairs={{8,16},{16,8},{9,17},{17,9},{10,18},{18,10},{11,19},{19,11},{12,20... | collective-permute-start | bytes 1572872 | tf_op jit(solution)/shard_map/ppermute | solution.py:72
  398.4 19.6 %collective-permute-start.78 = (bf16[512,512]{1,0:T(8,128)(2,1)}, bf16[512,512]{1,0:T(8,128)(2,1)S(1)}, u32[]{:S(2)}, u32[]{:S(2)}) collective-permute-start(bf16[512,512]{1,0:T(8,128)(2,1)} %add_convert_fusion.36), channel_id=1, source_target_pairs={{8,16},{16,8},{9,17},{17,9},{10,18},{18,10},{11,19},{19,11},{12,20... | collective-permute-start | bytes 1572872 | tf_op jit(solution)/shard_map/ppermute | solution.py:72
  410.7 30.7 %collective-permute-start.81 = (bf16[512,512]{1,0:T(8,128)(2,1)}, bf16[512,512]{1,0:T(8,128)(2,1)}, u32[]{:S(2)}, u32[]{:S(2)}) collective-permute-start(bf16[512,512]{1,0:T(8,128)(2,1)} %add_convert_fusion.32), channel_id=1, source_target_pairs={{8,16},{16,8},{9,17},{17,9},{10,18},{18,10},{11,19},{19,11},{12,20... | collective-permute-start | bytes 1572872 | tf_op jit(solution)/shard_map/ppermute | solution.py:72
  414.9 26.5 %collective-permute-start.77 = (bf16[512,512]{1,0:T(8,128)(2,1)}, bf16[512,512]{1,0:T(8,128)(2,1)S(1)}, u32[]{:S(2)}, u32[]{:S(2)}) collective-permute-start(bf16[512,512]{1,0:T(8,128)(2,1)} %get-tuple-element.347), channel_id=1, source_target_pairs={{0,8},{8,0},{16,24},{24,16},{1,9},{9,1},{17,25},{25,17},{2,10},{10... | collective-permute-start | bytes 1572872 | tf_op jit(solution)/shard_map/ppermute | solution.py:77
  419.2 20.1 %collective-permute-start.79 = (bf16[512,512]{1,0:T(8,128)(2,1)}, bf16[512,512]{1,0:T(8,128)(2,1)}, u32[]{:S(2)}, u32[]{:S(2)}) collective-permute-start(bf16[512,512]{1,0:T(8,128)(2,1)} %get-tuple-element.345), channel_id=1, source_target_pairs={{0,8},{8,0},{16,24},{24,16},{1,9},{9,1},{17,25},{25,17},{2,10},{10... | collective-permute-start | bytes 1572872 | tf_op jit(solution)/shard_map/ppermute | solution.py:77
  443.6 16.7 %collective-permute-start.82 = (bf16[512,512]{1,0:T(8,128)(2,1)S(1)}, bf16[512,512]{1,0:T(8,128)(2,1)S(1)}, u32[]{:S(2)}, u32[]{:S(2)}) collective-permute-start(bf16[512,512]{1,0:T(8,128)(2,1)S(1)} %get-tuple-element.343), channel_id=1, source_target_pairs={{0,8},{8,0},{16,24},{24,16},{1,9},{9,1},{17,25},{25,17},{2,10},{10... | collective-permute-start | bytes 1572872 | tf_op jit(solution)/shard_map/ppermute | solution.py:77
  449.5 25.2 %collective-permute-start.85 = (bf16[512,512]{1,0:T(8,128)(2,1)}, bf16[512,512]{1,0:T(8,128)(2,1)}, u32[]{:S(2)}, u32[]{:S(2)}) collective-permute-start(bf16[512,512]{1,0:T(8,128)(2,1)} %get-tuple-element.339), channel_id=1, source_target_pairs={{0,8},{8,0},{16,24},{24,16},{1,9},{9,1},{17,25},{25,17},{2,10},{10... | collective-permute-start | bytes 1572872 | tf_op jit(solution)/shard_map/ppermute | solution.py:77
  462.6 19.5 %collective-permute-start.83 = (bf16[512,512]{1,0:T(8,128)(2,1)}, bf16[512,512]{1,0:T(8,128)(2,1)}, u32[]{:S(2)}, u32[]{:S(2)}) collective-permute-start(bf16[512,512]{1,0:T(8,128)(2,1)} %get-tuple-element.341), channel_id=1, source_target_pairs={{0,8},{8,0},{16,24},{24,16},{1,9},{9,1},{17,25},{25,17},{2,10},{10... | collective-permute-start | bytes 1572872 | tf_op jit(solution)/shard_map/ppermute | solution.py:77
  473.2 20.1 %collective-permute-start.87 = (bf16[512,512]{1,0:T(8,128)(2,1)}, bf16[512,512]{1,0:T(8,128)(2,1)}, u32[]{:S(2)}, u32[]{:S(2)}) collective-permute-start(bf16[512,512]{1,0:T(8,128)(2,1)} %add_convert_fusion.26), channel_id=1, source_target_pairs={{8,16},{16,8},{9,17},{17,9},{10,18},{18,10},{11,19},{19,11},{12,20... | collective-permute-start | bytes 1572872 | tf_op jit(solution)/shard_map/ppermute | solution.py:72
  476.8 34.1 %collective-permute-start.90 = (bf16[512,512]{1,0:T(8,128)(2,1)}, bf16[512,512]{1,0:T(8,128)(2,1)}, u32[]{:S(2)}, u32[]{:S(2)}) collective-permute-start(bf16[512,512]{1,0:T(8,128)(2,1)} %add_convert_fusion.24), channel_id=1, source_target_pairs={{8,16},{16,8},{9,17},{17,9},{10,18},{18,10},{11,19},{19,11},{12,20... | collective-permute-start | bytes 1572872 | tf_op jit(solution)/shard_map/ppermute | solution.py:72
  484.2 32.3 %collective-permute-start.95 = (bf16[512,512]{1,0:T(8,128)(2,1)}, bf16[512,512]{1,0:T(8,128)(2,1)}, u32[]{:S(2)}, u32[]{:S(2)}) collective-permute-start(bf16[512,512]{1,0:T(8,128)(2,1)} %add_convert_fusion.23), channel_id=1, source_target_pairs={{8,16},{16,8},{9,17},{17,9},{10,18},{18,10},{11,19},{19,11},{12,20... | collective-permute-start | bytes 1572872 | tf_op jit(solution)/shard_map/ppermute | solution.py:72
  499.3 17.2 %collective-permute-start.86 = (bf16[512,512]{1,0:T(8,128)(2,1)S(1)}, bf16[512,512]{1,0:T(8,128)(2,1)S(1)}, u32[]{:S(2)}, u32[]{:S(2)}) collective-permute-start(bf16[512,512]{1,0:T(8,128)(2,1)S(1)} %fusion.31), channel_id=1, source_target_pairs={{0,4},{4,0},{1,5},{5,1},{2,6},{6,2},{3,7},{7,3},{8,12},{12,8},{9,1... | collective-permute-start | bytes 1572872 | tf_op jit(solution)/shard_map/ppermute | solution.py:44
  509.9 19.6 %collective-permute-start.93 = (bf16[512,512]{1,0:T(8,128)(2,1)S(1)}, bf16[512,512]{1,0:T(8,128)(2,1)S(1)}, u32[]{:S(2)}, u32[]{:S(2)}) collective-permute-start(bf16[512,512]{1,0:T(8,128)(2,1)S(1)} %add_convert_fusion.21), channel_id=1, source_target_pairs={{8,16},{16,8},{9,17},{17,9},{10,18},{18,10},{11,19},{19,11},{12,20... | collective-permute-start | bytes 1572872 | tf_op jit(solution)/shard_map/ppermute | solution.py:72
  513.2 16.2 %collective-permute-start.91 = (bf16[512,512]{1,0:T(8,128)(2,1)S(1)}, bf16[512,512]{1,0:T(8,128)(2,1)S(1)}, u32[]{:S(2)}, u32[]{:S(2)}) collective-permute-start(bf16[512,512]{1,0:T(8,128)(2,1)S(1)} %get-tuple-element.335), channel_id=1, source_target_pairs={{0,8},{8,0},{16,24},{24,16},{1,9},{9,1},{17,25},{25,17},{2,10},{10... | collective-permute-start | bytes 1572872 | tf_op jit(solution)/shard_map/ppermute | solution.py:77
  518.8 21.8 %collective-permute-start.96 = (bf16[512,512]{1,0:T(8,128)(2,1)S(1)}, bf16[512,512]{1,0:T(8,128)(2,1)S(1)}, u32[]{:S(2)}, u32[]{:S(2)}) collective-permute-start(bf16[512,512]{1,0:T(8,128)(2,1)S(1)} %get-tuple-element.331), channel_id=1, source_target_pairs={{0,8},{8,0},{16,24},{24,16},{1,9},{9,1},{17,25},{25,17},{2,10},{10... | collective-permute-start | bytes 1572872 | tf_op jit(solution)/shard_map/ppermute | solution.py:77
  530.5 17.7 %collective-permute-start.94 = (bf16[512,512]{1,0:T(8,128)(2,1)S(1)}, bf16[512,512]{1,0:T(8,128)(2,1)S(1)}, u32[]{:S(2)}, u32[]{:S(2)}) collective-permute-start(bf16[512,512]{1,0:T(8,128)(2,1)S(1)} %get-tuple-element.333), channel_id=1, source_target_pairs={{0,8},{8,0},{16,24},{24,16},{1,9},{9,1},{17,25},{25,17},{2,10},{10... | collective-permute-start | bytes 1572872 | tf_op jit(solution)/shard_map/ppermute | solution.py:77
  541.4 16.5 %collective-permute-start.98 = (bf16[512,512]{1,0:T(8,128)(2,1)S(1)}, bf16[512,512]{1,0:T(8,128)(2,1)S(1)}, u32[]{:S(2)}, u32[]{:S(2)}) collective-permute-start(bf16[512,512]{1,0:T(8,128)(2,1)S(1)} %add_convert_fusion.18), channel_id=1, source_target_pairs={{8,16},{16,8},{9,17},{17,9},{10,18},{18,10},{11,19},{19,11},{12,20... | collective-permute-start | bytes 1572872 | tf_op jit(solution)/shard_map/ppermute | solution.py:72
  550.6 28.4 %collective-permute-start.104 = (bf16[512,512]{1,0:T(8,128)(2,1)}, bf16[512,512]{1,0:T(8,128)(2,1)}, u32[]{:S(2)}, u32[]{:S(2)}) collective-permute-start(bf16[512,512]{1,0:T(8,128)(2,1)} %get-tuple-element.325), channel_id=1, source_target_pairs={{0,8},{8,0},{16,24},{24,16},{1,9},{9,1},{17,25},{25,17},{2,10},{10... | collective-permute-start | bytes 1572872 | tf_op jit(solution)/shard_map/ppermute | solution.py:77
  559.2 19.8 %collective-permute-start.99 = (bf16[512,512]{1,0:T(8,128)(2,1)}, bf16[512,512]{1,0:T(8,128)(2,1)}, u32[]{:S(2)}, u32[]{:S(2)}) collective-permute-start(bf16[512,512]{1,0:T(8,128)(2,1)} %get-tuple-element.329), channel_id=1, source_target_pairs={{0,8},{8,0},{16,24},{24,16},{1,9},{9,1},{17,25},{25,17},{2,10},{10... | collective-permute-start | bytes 1572872 | tf_op jit(solution)/shard_map/ppermute | solution.py:77
  581.8 15.0 %collective-permute-start.100 = (bf16[512,512]{1,0:T(8,128)(2,1)S(1)}, bf16[512,512]{1,0:T(8,128)(2,1)S(1)}, u32[]{:S(2)}, u32[]{:S(2)}) collective-permute-start(bf16[512,512]{1,0:T(8,128)(2,1)S(1)} %get-tuple-element.327), channel_id=1, source_target_pairs={{0,8},{8,0},{16,24},{24,16},{1,9},{9,1},{17,25},{25,17},{2,10},{10... | collective-permute-start | bytes 1572872 | tf_op jit(solution)/shard_map/ppermute | solution.py:77
  586.5 18.3 %collective-permute-start.105 = (bf16[512,512]{1,0:T(8,128)(2,1)S(1)}, bf16[512,512]{1,0:T(8,128)(2,1)S(1)}, u32[]{:S(2)}, u32[]{:S(2)}) collective-permute-start(bf16[512,512]{1,0:T(8,128)(2,1)S(1)} %add_convert_fusion.11), channel_id=1, source_target_pairs={{8,16},{16,8},{9,17},{17,9},{10,18},{18,10},{11,19},{19,11},{12,20... | collective-permute-start | bytes 1572872 | tf_op jit(solution)/shard_map/ppermute | solution.py:72
  598.0 22.6 %collective-permute-start.108 = (bf16[512,512]{1,0:T(8,128)(2,1)S(1)}, bf16[512,512]{1,0:T(8,128)(2,1)S(1)}, u32[]{:S(2)}, u32[]{:S(2)}) collective-permute-start(bf16[512,512]{1,0:T(8,128)(2,1)S(1)} %add_convert_fusion.5.refs_10_), channel_id=1, source_target_pairs={{0,8},{8,0},{16,24},{24,16},{1,9},{9,1},{17,25},{25,17},{2,10},{10... | collective-permute-start | bytes 1572872 | tf_op jit(solution)/shard_map/ppermute | solution.py:77
  605.0 18.2 %collective-permute-start.106 = (bf16[512,512]{1,0:T(8,128)(2,1)S(1)}, bf16[512,512]{1,0:T(8,128)(2,1)S(1)}, u32[]{:S(2)}, u32[]{:S(2)}) collective-permute-start(bf16[512,512]{1,0:T(8,128)(2,1)S(1)} %add_convert_fusion.7.refs_8_), channel_id=1, source_target_pairs={{0,8},{8,0},{16,24},{24,16},{1,9},{9,1},{17,25},{25,17},{2,10},{10... | collective-permute-start | bytes 1572872 | tf_op jit(solution)/shard_map/ppermute | solution.py:77
  608.1 21.3 %collective-permute-start.102 = (bf16[512,512]{1,0:T(8,128)(2,1)S(1)}, bf16[512,512]{1,0:T(8,128)(2,1)S(1)}, u32[]{:S(2)}, u32[]{:S(2)}) collective-permute-start(bf16[512,512]{1,0:T(8,128)(2,1)S(1)} %add_convert_fusion.9), channel_id=1, source_target_pairs={{0,8},{8,0},{16,24},{24,16},{1,9},{9,1},{17,25},{25,17},{2,10},{10... | collective-permute-start | bytes 1572872 | tf_op jit(solution)/shard_map/ppermute | solution.py:77
  (195 other events, 1922.6 us)
Sparse Core Ops, SparseCore 0:
  32.1 38.5 all-gather.6
  72.2 37.5 all-gather.8
  111.4 35.9 all-gather.10
  341.9 86.5 all-gather.14
  430.0 46.3 all-gather.12
